TPU v7x, 32 devices: a whole 2x2x4 slice. The times are simulated.
32 devices in a mesh: tab: 8 (over z, y), col: 4 (over x, core).
Axes of the slice: x: 2, y: 2, z: 4, core: 2. Of those that a mesh axis runs over, the one named last changes fastest.
Arguments:
- bag_items: bfloat16 [128, 4, 48, 1024], P('tab', None, 'col'), may hold values from -3 to 3
- lengths: int32 [128, 1024], P('tab'), may hold values from 1 to 4
- field_slot: int32 [64], replicated, may hold values from 0 to 127, as said below
- filter_one: bfloat16 [32, 4096], replicated, may hold values from -0.09375 to 0.09375
- filter_two: bfloat16 [32, 2048], replicated, may hold values from -0.125 to 0.125
- cotangent: bfloat16 [64, 1024], P(None, ('tab', 'col')), may hold values from -12 to 12
Outputs:
- pooled: float32 [64, 1024], P(None, ('tab', 'col'))
- filter_grad_one: float32 [32, 4096], P(None, ('tab', 'col'))
- filter_grad_two: float32 [32, 2048], P(None, ('tab', 'col'))
- pooled_grad: bfloat16 [128, 48, 1024], P('tab', 'col')
Inputs may be any that keep to these rules, and one draw needn't show every extreme that they name: Distinct values; the table of field f is held by index field_slot[f] // 16 of tab; owners hold 0 to 16 fields and one owner holds 16.
All inputs are finite; a program needn't handle non-finite values.
Results may differ from a plain program's by a relative error of at most 0.017.
Values may be sent and summed in bfloat16 or wider, within the bound.
No kernel may reach another device: no remote copies, remote signals or barrier semaphores. Data moves between devices by JAX's collectives and lax.ppermute only.
A program may use at most 64 MiB of HBM per device.

v0:
```python
import math

import jax
import jax.numpy as jnp
from jax import lax
from jax.sharding import PartitionSpec as P

D = 48


def cross_block(first_cols, upstream, filter_one, filter_two):
    fields, columns = first_cols.shape
    map_count = filter_one.shape[0]
    first_pairs = (first_cols[:, None, :] * first_cols[None, :, :]).reshape(
        fields * fields, columns
    )
    first_maps = jnp.dot(filter_one, first_pairs, preferred_element_type=jnp.float32)
    hidden_cols = lax.optimization_barrier(first_maps.astype(jnp.bfloat16))
    second_pairs = (hidden_cols[:, None, :] * first_cols[None, :, :]).reshape(
        map_count * fields, columns
    )
    second_maps = jnp.dot(filter_two, second_pairs, preferred_element_type=jnp.float32)
    upper_grad = upstream[map_count:]
    grad_two = lax.dot_general(
        upper_grad, second_pairs, (((1,), (1,)), ((), ())), preferred_element_type=jnp.float32
    )
    pair_grad_two = lax.dot_general(
        filter_two, upper_grad, (((0,), (0,)), ((), ())), preferred_element_type=jnp.float32
    )
    pair_grad_two = lax.optimization_barrier(pair_grad_two.astype(jnp.bfloat16))
    pair_grad_two = pair_grad_two.reshape(map_count, fields, columns).astype(jnp.float32)
    first_float = first_cols.astype(jnp.float32)
    hidden_grad = jnp.sum(pair_grad_two * first_float[None], axis=1)
    field_grad = jnp.sum(pair_grad_two * hidden_cols.astype(jnp.float32)[:, None], axis=0)
    lower_grad = (upstream[:map_count].astype(jnp.float32) + hidden_grad).astype(jnp.bfloat16)
    grad_one = lax.dot_general(
        lower_grad, first_pairs, (((1,), (1,)), ((), ())), preferred_element_type=jnp.float32
    )
    pair_grad_one = lax.dot_general(
        filter_one, lower_grad, (((0,), (0,)), ((), ())), preferred_element_type=jnp.float32
    )
    pair_grad_one = lax.optimization_barrier(pair_grad_one.astype(jnp.bfloat16))
    pair_grad_one = pair_grad_one.reshape(fields, fields, columns).astype(jnp.float32)
    field_grad = (
        field_grad
        + jnp.sum(pair_grad_one * first_float[None], axis=1)
        + jnp.sum(pair_grad_one * first_float[:, None], axis=0)
    )
    return (first_maps, second_maps, field_grad.astype(jnp.bfloat16), grad_one, grad_two)


def cross_layers(embed_rows, upstream, filter_one, filter_two):
    fields, columns = embed_rows.shape
    map_count = filter_one.shape[0]
    block_cols = math.gcd(columns, 512)
    block_count = columns // block_cols
    embed_blocks = embed_rows.reshape(fields, block_count, block_cols).transpose(1, 0, 2)
    grad_blocks = upstream.reshape(2 * map_count, block_count, block_cols).transpose(1, 0, 2)

    def advance(totals, inputs):
        first_maps, second_maps, field_grad, grad_one, grad_two = cross_block(
            inputs[0], inputs[1], filter_one, filter_two
        )
        both_maps = jnp.concatenate([first_maps, second_maps], axis=0)
        return ((totals[0] + grad_one, totals[1] + grad_two), (both_maps, field_grad))

    zero_sums = (jnp.zeros(filter_one.shape, jnp.float32), jnp.zeros(filter_two.shape, jnp.float32))
    (grad_one, grad_two), (map_blocks, field_blocks) = lax.scan(
        advance, zero_sums, (embed_blocks, grad_blocks)
    )
    both_maps = map_blocks.transpose(1, 0, 2).reshape(2 * map_count, columns)
    field_grad = field_blocks.transpose(1, 0, 2).reshape(fields, columns)
    return (both_maps, field_grad, grad_one, grad_two)


def per_device(bag_items, lengths, field_slot, filter_one, filter_two, cotangent):
    slot_count, item_count, col_width, samples = bag_items.shape
    tab_count = lax.axis_size("tab")
    col_count = lax.axis_size("col")
    item_index = jnp.arange(item_count)[None, :, None, None]
    kept_items = jnp.where(
        item_index < lengths[:, None, None, :], bag_items, jnp.zeros_like(bag_items)
    )
    pooled_table = jnp.sum(kept_items, axis=1, dtype=jnp.float32).astype(jnp.bfloat16)
    per_owner = pooled_table.reshape(slot_count, col_width, tab_count, samples // tab_count)
    received = lax.all_to_all(per_owner, "tab", split_axis=2, concat_axis=0, tiled=True)
    grad_rows = lax.all_gather(cotangent, "col", axis=1, tiled=True)
    all_slots = received.shape[0]
    local_width = received.shape[1]
    local_samples = received.shape[3]
    slot_rows = received.reshape(all_slots, local_width * local_samples)
    embed_rows = jnp.take(slot_rows, field_slot, axis=0)
    grad_count = grad_rows.shape[0]
    upstream = jnp.broadcast_to(
        grad_rows[:, None, :], (grad_count, local_width, local_samples)
    ).astype(jnp.float32) * D ** (-0.5)
    upstream = upstream.astype(jnp.bfloat16).reshape(grad_count, local_width * local_samples)
    both_maps, field_grad, grad_one, grad_two = cross_layers(
        embed_rows, upstream, filter_one, filter_two
    )
    pooled_part = jnp.sum(
        both_maps.reshape(grad_count, local_width, local_samples), axis=1
    ) * D ** (-0.5)
    grad_table = jnp.zeros_like(slot_rows).at[field_slot].set(field_grad).reshape(received.shape)
    pooled = lax.psum_scatter(pooled_part, "col", scatter_dimension=1, tiled=True)
    returned = lax.all_to_all(grad_table, "tab", split_axis=0, concat_axis=2, tiled=True)
    pooled_grad = returned.reshape(slot_count, col_width, samples)
    grad_scale = samples ** (-0.5)
    map_count = grad_one.shape[0]
    first_shaped = (grad_one * grad_scale).reshape(map_count, tab_count, col_count, -1)
    second_shaped = (grad_two * grad_scale).reshape(map_count, tab_count, col_count, -1)
    first_shaped, second_shaped = (
        lax.psum_scatter(first_shaped, "col", scatter_dimension=2, tiled=True),
        lax.psum_scatter(second_shaped, "col", scatter_dimension=2, tiled=True),
    )
    first_shaped, second_shaped = (
        lax.psum_scatter(first_shaped, "tab", scatter_dimension=1, tiled=True),
        lax.psum_scatter(second_shaped, "tab", scatter_dimension=1, tiled=True),
    )
    grad_one = first_shaped.reshape(map_count, -1)
    grad_two = second_shaped.reshape(map_count, -1)
    return (pooled, grad_one, grad_two, pooled_grad)


def solution(mesh):
    in_specs = (P("tab", None, "col", None), P("tab", None), P(), P(), P(), P(None, ("tab", "col")))
    out_specs = (
        P(None, ("tab", "col")),
        P(None, ("tab", "col")),
        P(None, ("tab", "col")),
        P("tab", "col", None),
    )
    return jax.shard_map(
        per_device, mesh=mesh, in_specs=in_specs, out_specs=out_specs, check_vma=False
    )
```

profile of v0, /device:TPU:0, one launch (start us, length us, event | category | flops | bytes accessed | tf_op | source)
XLA Modules:
  0.0 345.1 jit_solution(914404592453202556)
XLA Ops:
  8.1 3.1 select_reduce_fusion
  12.4 7.3 %all-to-all-start = ((bf16[16,12,8,128]{3,0,1,2:T(8,128)(2,1)}), bf16[16,12,8,128]{3,0,1,2:T(8,128)(2,1)S(1)}, u32[]{:S(2)}, u32[]{:S(2)}) async-start(bf16[16,12,8,128]{3,0,1,2:T(8,128)(2,1)} %copy.57), calls=%async_computation | async-start | bytes 786432 | tf_op jit(solution)/shard_map/all_to_all | solution.py:86
  19.8 5.4 %all_gather.3 = bf16[64,128]{0,1:T(8,128)(2,1)S(1)} all-gather(bf16[64,32]{0,1:T(8,128)(2,1)S(1)} %copy-done.7), channel_id=1, replica_groups=mesh['tab'=8,'col'=4] {'col'}, dimensions={1}, use_global_device_ids=true | all-gather | bytes 20480 | tf_op jit(solution)/shard_map/all_gather | solution.py:87
  26.2 5.2 %all-to-all-done = bf16[16,12,8,128]{3,0,1,2:T(8,128)(2,1)S(1)} async-done(((bf16[16,12,8,128]{3,0,1,2:T(8,128)(2,1)}), bf16[16,12,8,128]{3,0,1,2:T(8,128)(2,1)S(1)}, u32[]{:S(2)}, u32[]{:S(2)}) %all-to-all-start) | async-done | bytes 393248 | tf_op jit(solution)/shard_map/all_to_all | solution.py:86
  33.4 107.2 %while.17 = (s32[]{:T(128)}, f32[32,4096]{1,0:T(8,128)S(1)}, f32[32,2048]{1,0:T(8,128)S(1)}, f32[3,64,512]{2,1,0:T(8,128)}, bf16[3,64,512]{2,1,0:T(8,128)(2,1)},...) while((s32[]{:T(128)}, f32[32,4096]{1,0:T(8,128)S(1)}, ...), condition=%wide.region_6.7_spmd.clone, body=%wide.region_1.6_spmd.clone.sunk | while | flops 623427584 | bytes 108364040 | solution.py:68
  34.3 2.2 broadcast_multiply_fusion.7
  38.0 3.0 copy.82
  41.0 3.0 multiply_reduce_fusion.7
  48.6 3.2 fusion.59
  51.9 7.1 %copy.83 = f32[4096,512]{1,0:T(8,128)} copy(bf16[4096,512]{0,1:T(8,128)(2,1)} %fusion.59) | data formatting | bytes 12582912 | tf_op jit(solution)/shard_map/while/body/eval_jaxpr/convert_element_type | solution.py:43
  59.0 8.8 %multiply_reduce_fusion.8 = (f32[64,512]{1,0:T(8,128)S(1)}, f32[64,512]{1,0:T(8,128)S(1)}) fusion(f32[64,512]{1,0:T(8,128)S(1)} %get-tuple-element.218, f32[4096,512]{1,0:T(8,128)} %copy.83, f32[64,64,512]{2,1,0:T(8,128)} %bitcast.128), kind=kLoop, calls=%fused_computation.3.clone.1 | loop fusion | flops 8323072 | bytes 17170432 | tf_op jit(solution)/shard_map/while/body/eval_jaxpr/reduce_sum | solution.py:46
  70.0 2.2 broadcast_multiply_fusion.7
  73.7 3.0 copy.82
  76.8 3.0 multiply_reduce_fusion.7
  84.4 3.2 fusion.59
  87.6 7.1 %copy.83 = f32[4096,512]{1,0:T(8,128)} copy(bf16[4096,512]{0,1:T(8,128)(2,1)} %fusion.59) | data formatting | bytes 12582912 | tf_op jit(solution)/shard_map/while/body/eval_jaxpr/convert_element_type | solution.py:43
  94.7 8.8 %multiply_reduce_fusion.8 = (f32[64,512]{1,0:T(8,128)S(1)}, f32[64,512]{1,0:T(8,128)S(1)}) fusion(f32[64,512]{1,0:T(8,128)S(1)} %get-tuple-element.218, f32[4096,512]{1,0:T(8,128)} %copy.83, f32[64,64,512]{2,1,0:T(8,128)} %bitcast.128), kind=kLoop, calls=%fused_computation.3.clone.1 | loop fusion | flops 8323072 | bytes 17170432 | tf_op jit(solution)/shard_map/while/body/eval_jaxpr/reduce_sum | solution.py:46
  105.8 2.2 broadcast_multiply_fusion.7
  108.0 1.5 fusion.56
  109.4 3.0 copy.82
  112.5 3.0 multiply_reduce_fusion.7
  120.1 3.2 fusion.59
  123.4 7.1 %copy.83 = f32[4096,512]{1,0:T(8,128)} copy(bf16[4096,512]{0,1:T(8,128)(2,1)} %fusion.59) | data formatting | bytes 12582912 | tf_op jit(solution)/shard_map/while/body/eval_jaxpr/convert_element_type | solution.py:43
  130.4 8.9 %multiply_reduce_fusion.8 = (f32[64,512]{1,0:T(8,128)S(1)}, f32[64,512]{1,0:T(8,128)S(1)}) fusion(f32[64,512]{1,0:T(8,128)S(1)} %get-tuple-element.218, f32[4096,512]{1,0:T(8,128)} %copy.83, f32[64,64,512]{2,1,0:T(8,128)} %bitcast.128), kind=kLoop, calls=%fused_computation.3.clone.1 | loop fusion | flops 8323072 | bytes 17170432 | tf_op jit(solution)/shard_map/while/body/eval_jaxpr/reduce_sum | solution.py:46
  145.7 3.6 %all-to-all-start.1 = ((bf16[128,12,1,128]{3,1,2,0:T(8,128)(2,1)}), bf16[128,12,1,128]{3,1,2,0:T(8,128)(2,1)S(1)}, u32[]{:S(2)}, u32[]{:S(2)}) async-start(bf16[128,12,1,128]{3,1,2,0:T(8,128)(2,1)} %copy.68), calls=%async_computation.5 | async-start | bytes 1048576 | tf_op jit(solution)/shard_map/all_to_all | solution.py:106
  150.8 12.0 %reduce-scatter.12.cloned.1.call-done = f32[32,8,1,64]{3,1,0,2:T(8,128)} async-done(((f32[32,8,4,64]{3,1,0,2:T(8,128)}), f32[32,8,1,64]{3,1,0,2:T(8,128)}) %reduce-scatter.12.cloned.1.call-update) | async-done | bytes 65552 | tf_op jit(solution)/shard_map/reduce_scatter | solution.py:114
  162.8 1.6 copy.65
  164.4 22.6 %reduce-scatter.8.cloned.1.call-done = f32[32,8,1,128]{3,1,0,2:T(8,128)} async-done(((f32[32,8,4,128]{3,1,0,2:T(8,128)}), f32[32,8,1,128]{3,1,0,2:T(8,128)}) %reduce-scatter.8.cloned.1.call-update) | async-done | bytes 131088 | tf_op jit(solution)/shard_map/reduce_scatter | solution.py:113
  187.1 1.6 copy.63
  189.8 19.7 %reduce-scatter.16.cloned.1.call-done = f32[32,64]{1,0:T(8,128)} async-done(((f32[128,64]{1,0:T(8,128)}), f32[32,64]{1,0:T(8,128)}) %reduce-scatter.16.cloned.1.call-update) | async-done | bytes 8208
  209.6 65.0 %reduce-scatter.14.cloned.1.call-done = f32[32,1,1,64]{3,0,2,1:T(8,128)} async-done(((f32[32,8,1,64]{3,0,2,1:T(8,128)}), f32[32,1,1,64]{3,0,2,1:T(8,128)}) %reduce-scatter.14.cloned.1.call-update) | async-done | bytes 8208 | tf_op jit(solution)/shard_map/reduce_scatter | solution.py:118
  274.5 64.0 %reduce-scatter.10.cloned.1.call-done = f32[32,1,1,128]{3,0,2,1:T(8,128)} async-done(((f32[32,8,1,128]{3,0,2,1:T(8,128)}), f32[32,1,1,128]{3,0,2,1:T(8,128)}) %reduce-scatter.10.cloned.1.call-update) | async-done | bytes 16400 | tf_op jit(solution)/shard_map/reduce_scatter | solution.py:117
  (112 shorter events, 36.0 us)
Async XLA Ops:
  7.2 12.6 %copy-start.7 = (bf16[64,32]{0,1:T(8,128)(2,1)S(1)}, bf16[64,32]{0,1:T(8,128)(2,1)}, u32[]{:S(2)}) copy-start(bf16[64,32]{0,1:T(8,128)(2,1)} %param.13) | copy-start | bytes 12292
  7.2 19.0 %copy-start.8 = (s32[64]{0:T(128)S(1)}, s32[64]{0:T(128)}, u32[]{:S(2)}) copy-start(s32[64]{0:T(128)} %param.10) | copy-start | bytes 772
  11.5 21.9 %copy-start.2 = (bf16[32,4096]{1,0:T(8,128)(2,1)S(1)}, bf16[32,4096]{1,0:T(8,128)(2,1)}, u32[]{:S(2)}) copy-start(bf16[32,4096]{1,0:T(8,128)(2,1)} %param.11) | copy-start | bytes 786436
  11.5 21.9 %copy-start.3 = (bf16[32,2048]{1,0:T(8,128)(2,1)S(1)}, bf16[32,2048]{1,0:T(8,128)(2,1)}, u32[]{:S(2)}) copy-start(bf16[32,2048]{1,0:T(8,128)(2,1)} %param.12) | copy-start | bytes 393220
  12.4 19.0 %all-to-all-start = ((bf16[16,12,8,128]{3,0,1,2:T(8,128)(2,1)}), bf16[16,12,8,128]{3,0,1,2:T(8,128)(2,1)S(1)}, u32[]{:S(2)}, u32[]{:S(2)}) async-start(bf16[16,12,8,128]{3,0,1,2:T(8,128)(2,1)} %copy.57), calls=%async_computation | async-start | bytes 786432 | tf_op jit(solution)/shard_map/all_to_all | solution.py:86
  19.7 143.1 %reduce-scatter.12.cloned.1.call-start = ((), (), s32[]{:S(2)}) async-start(), calls=%async_computation.9 | async-start | bytes 655360 | tf_op jit(solution)/shard_map/reduce_scatter | solution.py:114
  41.0 3.4 copy-start.1
  41.0 3.4 copy-start.4
  59.0 8.9 %copy-start = (f32[2048,512]{1,0:T(8,128)S(1)}, f32[2048,512]{1,0:T(8,128)}, u32[]{:S(2)}) copy-start(f32[2048,512]{1,0:T(8,128)} %copy.82) | copy-start | bytes 12582916 | tf_op jit(solution)/shard_map/while
  76.7 3.4 copy-start.1
  76.7 3.4 copy-start.4
  94.7 8.9 %copy-start = (f32[2048,512]{1,0:T(8,128)S(1)}, f32[2048,512]{1,0:T(8,128)}, u32[]{:S(2)}) copy-start(f32[2048,512]{1,0:T(8,128)} %copy.82) | copy-start | bytes 12582916 | tf_op jit(solution)/shard_map/while
  112.5 3.4 copy-start.1
  112.5 3.4 copy-start.4
  130.4 8.9 %copy-start = (f32[2048,512]{1,0:T(8,128)S(1)}, f32[2048,512]{1,0:T(8,128)}, u32[]{:S(2)}) copy-start(f32[2048,512]{1,0:T(8,128)} %copy.82) | copy-start | bytes 12582916 | tf_op jit(solution)/shard_map/while
  140.7 2.6 copy-start.6
  141.0 8.4 %copy-start.5 = (f32[3,64,512]{2,1,0:T(8,128)S(1)}, f32[3,64,512]{2,1,0:T(8,128)}, u32[]{:S(2)}) copy-start(f32[3,64,512]{2,1,0:T(8,128)} %get-tuple-element.54) | copy-start | bytes 1179652
  141.9 45.1 %reduce-scatter.8.cloned.1.call-start = ((), (), s32[]{:S(2)}) async-start(), calls=%async_computation.7 | async-start | bytes 655360 | tf_op jit(solution)/shard_map/reduce_scatter | solution.py:113
  145.7 42.9 %all-to-all-start.1 = ((bf16[128,12,1,128]{3,1,2,0:T(8,128)(2,1)}), bf16[128,12,1,128]{3,1,2,0:T(8,128)(2,1)S(1)}, u32[]{:S(2)}, u32[]{:S(2)}) async-start(bf16[128,12,1,128]{3,1,2,0:T(8,128)(2,1)} %copy.68), calls=%async_computation.5 | async-start | bytes 1048576 | tf_op jit(solution)/shard_map/all_to_all | solution.py:106
  149.4 60.2 %reduce-scatter.16.cloned.1.call-start = ((), (), s32[]{:S(2)}) async-start(), calls=%async_computation.11 | async-start | bytes 81920
  150.8 123.8 %reduce-scatter.14.cloned.1.call-start = ((), (), s32[]{:S(2)}) async-start(), calls=%async_computation.10 | async-start | bytes 147456 | tf_op jit(solution)/shard_map/reduce_scatter | solution.py:118
  164.4 174.2 %reduce-scatter.10.cloned.1.call-start = ((), (), s32[]{:S(2)}) async-start(), calls=%async_computation.8 | async-start | bytes 147456 | tf_op jit(solution)/shard_map/reduce_scatter | solution.py:117
Sparse Core Ops, SparseCore 0:
  142.0 20.6 reduce-scatter.11
  165.4 21.6 reduce-scatter.7
  190.1 19.4 reduce-scatter.15
  213.7 60.8 reduce-scatter.13
  278.6 59.8 reduce-scatter.9
where the time goes:
time: 346 us; the launch traced here: 345 us
  waiting for transfers between devices  189 us (55%)
  other arithmetic  55.6 us (16%)
  local copies, waits for them, and re-layouts  45.9 us (13%)
  matrix products  24.1 us (7%)
  between operations  14.1 us (4%)
  starting transfers between devices  11.1 us (3%)
  blocking collectives  5.37 us (2%)
    reduce_scatter x1, waiting for transfers between devices, per_device(): lax.psum_scatter(second_shaped, 'tab', scatter_dimension=1, tiled=True)  65 us
    reduce_scatter x1, waiting for transfers between devices, per_device(): lax.psum_scatter(first_shaped, 'tab', scatter_dimension=1, tiled=True)  64 us
    reduce_sum x3, other arithmetic, cross_block(): jnp.sum(pair_grad_one * first_float[None], axis=1)  26.5 us
    reduce_scatter x1, waiting for transfers between devices, per_device(): lax.psum_scatter(first_shaped, 'col', scatter_dimension=2, tiled=True)  22.6 us
    convert_element_type x3, local copies, waits for them, and re-layouts, cross_block(): pair_grad_one.reshape(fields, fields, columns).astype(jnp.float32)  21.2 us
    unnamed x6, waiting for transfers between devices  19.8 us
    reduce_scatter x1, waiting for transfers between devices, per_device(): lax.psum_scatter(second_shaped, 'col', scatter_dimension=2, tiled=True)  12 us
    dot_general x3, matrix products, cross_block(): lax.dot_general(filter_one, lower_grad, (((0,), (0,)), ((), ())), preferr...  9.73 us
  transfers between devices with their start and end apart: 7, of which 6 were waited for; matrix products, arithmetic and copies ran while one was open for 3% of the time, Pallas kernels for 0%

commit v1 on v0

v1 whole, which is shorter than its diff:
```python
import functools

import jax
import jax.numpy as jnp
from jax import lax
from jax.experimental import pallas as pl
from jax.experimental.pallas import tpu as pltpu
from jax.sharding import PartitionSpec as P

BF16 = jnp.bfloat16
F32 = jnp.float32
VMEM_BYTES = 48 * 1024 * 1024
MATMUL_ROWS = 512


def params():
    return pltpu.CompilerParams(vmem_limit_bytes=VMEM_BYTES)


def cost(flops, moved):
    return pl.CostEstimate(flops=flops, bytes_accessed=moved, transcendentals=0)


def whole():
    return pl.BlockSpec(memory_space=pltpu.VMEM)


def dot(left, right):
    return jnp.dot(left, right, preferred_element_type=F32)


def dot_lanes(left, right):
    return lax.dot_general(left, right, (((1,), (1,)), ((), ())), preferred_element_type=F32)


def pool_kernel(bag_ref, lengths_ref, out_ref, rows_ref):
    slots, items, width, _ = bag_ref.shape
    chunks, _, lanes = out_ref.shape
    for chunk in range(chunks):
        here = pl.ds(chunk * lanes, lanes)
        for slot in range(slots):
            count = lengths_ref[slot : slot + 1, here]
            total = jnp.zeros((width, lanes), F32)
            for item in range(items):
                value = bag_ref[slot, item, :, here].astype(F32)
                total = total + jnp.where(count > item, value, 0.0)
            rows_ref[pl.ds(slot, width, stride=slots), :] = total
        out_ref[chunk] = rows_ref[...].astype(BF16)


def pool(bag_items, lengths, tab_count):
    slots, items, width, samples = bag_items.shape
    lanes = samples // tab_count
    steps = min(4, tab_count)
    per_step = tab_count // steps
    return pl.pallas_call(
        pool_kernel,
        grid=(steps,),
        in_specs=[
            pl.BlockSpec((slots, items, width, per_step * lanes), lambda i: (0, 0, 0, i)),
            pl.BlockSpec((slots, per_step * lanes), lambda i: (0, i)),
        ],
        out_specs=pl.BlockSpec((per_step, width * slots, lanes), lambda i: (i, 0, 0)),
        out_shape=jax.ShapeDtypeStruct((tab_count, width * slots, lanes), BF16),
        scratch_shapes=[pltpu.VMEM((width * slots, lanes), F32)],
        compiler_params=params(),
        name="pool_bags",
    )(bag_items, lengths)


def field_rows(received_ref, onehot, column, slots):
    parts = [
        received_ref[t, pl.ds(pl.multiple_of(column * slots, slots), slots), :]
        for t in range(received_ref.shape[0])
    ]
    rows = parts[0] if len(parts) == 1 else jnp.concatenate(parts, axis=0)
    return dot(onehot, rows)


def filter_kernel(
    packed, scales,
    col_ref, received_ref, slot_ref, cot_ref, sym_ref, second_ref,
    *refs,
):
    out_count = packed[0] if packed else 2
    outs = refs[:out_count]
    embed_ref, hidden_ref, lower_ref = refs[out_count : out_count + 3]
    up_ref, z_ref, x_ref, h_ref, pooled_ref, grad_ref, pack_ref = refs[out_count + 3 :]
    fields = slot_ref.shape[0]
    maps, positions = hidden_ref.shape
    lanes = cot_ref.shape[1]
    width = positions // lanes
    slots = received_ref.shape[1] // width
    pair = 2 * lanes
    all_slots = received_ref.shape[0] * slots
    scale = scales[0]
    onehot = (lax.broadcasted_iota(jnp.int32, (fields, all_slots), 1) == slot_ref[...]).astype(BF16)
    up = (cot_ref[...].astype(F32) * scale).astype(BF16).astype(F32)
    up_ref[:, :lanes] = up
    up_ref[:, lanes:] = up
    pooled_ref[...] = jnp.zeros_like(pooled_ref)
    grad_ref[...] = jnp.zeros_like(grad_ref)

    def step(index, carry):
        here = pl.ds(pl.multiple_of(index * pair, pair), pair)
        x_float = jnp.concatenate(
            [field_rows(received_ref, onehot, 2 * index + k, slots) for k in range(2)], axis=1
        )
        x_ref[...] = x_float
        x = x_float.astype(BF16)
        embed_ref[:, here] = x
        hidden_grad = jnp.zeros((maps, pair), F32)
        rows = min(MATMUL_ROWS, maps * maps)
        for start in range(0, maps * maps, rows):
            z = dot(second_ref[start : start + rows, :], x)
            z_ref[start : start + rows, :] = z
            for k in range(rows // maps):
                o = start // maps + k
                hidden_grad = hidden_grad + up_ref[maps + o : maps + o + 1, :] * z[k * maps : (k + 1) * maps]
        lower = (up_ref[:maps, :] + hidden_grad).astype(BF16)
        lower_ref[:, here] = lower
        lower = lower.astype(F32)
        rows = min(MATMUL_ROWS, maps * fields)
        for start in range(0, maps * fields, rows):
            y = dot(sym_ref[start : start + rows, :], x).reshape(rows // fields, fields, pair)
            o = start // fields
            h_ref[o : o + rows // fields, :] = 0.5 * jnp.sum(y * x_float[None], axis=1)
        first_maps = h_ref[...]
        pooled_ref[:maps, :] += first_maps
        hidden = first_maps.astype(BF16)
        hidden_ref[:, here] = hidden
        hidden = hidden.astype(F32)
        h_ref[...] = hidden
        for o in range(maps):
            total = jnp.sum(z_ref[o * maps : (o + 1) * maps, :] * hidden, axis=0, keepdims=True)
            pooled_ref[maps + o : maps + o + 1, :] += total
        group = MATMUL_ROWS // maps
        for first in range(0, fields, group):
            pairs = jnp.concatenate(
                [(x_ref[first + k : first + k + 1, :] * lower).astype(BF16) for k in range(group)], axis=0
            )
            grad_ref[first * maps : (first + group) * maps, :] += dot_lanes(pairs, x)
        upper = up_ref[maps:, :]
        base = fields * maps
        for first in range(0, maps, group):
            pairs = jnp.concatenate(
                [(h_ref[first + k : first + k + 1, :] * upper).astype(BF16) for k in range(group)], axis=0
            )
            grad_ref[base + first * maps : base + (first + group) * maps, :] += dot_lanes(pairs, x)
        return carry

    lax.fori_loop(0, width // 2, step, 0)
    pooled = (pooled_ref[:, :lanes] + pooled_ref[:, lanes:]) * scale
    if not packed:
        outs[0][...] = grad_ref[...] * scales[1]
        outs[1][...] = pooled
        return
    cols, tabs = packed
    share = lanes // cols
    tall = 2 * maps * share // lanes
    for c in range(cols):
        pack_ref[c] = jnp.concatenate(
            [
                pooled[g * tall : (g + 1) * tall, c * share : (c + 1) * share]
                for g in range(lanes // share)
            ],
            axis=1,
        )
    own = col_ref[0]
    block = maps + maps // 2
    for r in range(cols):
        c = jnp.bitwise_xor(own, r)
        for t in range(tabs):
            k = t * cols + c
            at = pl.multiple_of(k * 2 * maps, 2 * maps)
            first = grad_ref[pl.ds(at, 2 * maps), :]
            first = jnp.concatenate([first[:maps], first[maps:]], axis=1)
            at = pl.multiple_of(base_rows(fields, maps) + k * maps, maps)
            second = grad_ref[pl.ds(at, maps), :]
            second = jnp.concatenate([second[: maps // 2], second[maps // 2 :]], axis=1)
            outs[r][t * block : (t + 1) * block, :] = (
                jnp.concatenate([first, second], axis=0) * scales[1]
            ).astype(BF16)
        outs[r][tabs * block :, :] = pack_ref[c].astype(BF16)


def base_rows(fields, maps):
    return fields * maps


def filter_part(packed, scales, col, received, slot, cot, sym, second, width):
    fields = slot.shape[0]
    maps = cot.shape[0] // 2
    lanes = cot.shape[1]
    positions = width * lanes
    pair = 2 * lanes
    kept = [
        jax.ShapeDtypeStruct((fields, positions), BF16),
        jax.ShapeDtypeStruct((maps, positions), BF16),
        jax.ShapeDtypeStruct((maps, positions), BF16),
    ]
    grads = (fields + maps) * maps
    if packed:
        cols, tabs = packed
        tall = 2 * maps // cols
        piece = (tabs * (maps + maps // 2) + tall, lanes)
        outs = [jax.ShapeDtypeStruct(piece, BF16)] * cols
        pack = pltpu.VMEM((cols, tall, lanes), F32)
    else:
        outs = [
            jax.ShapeDtypeStruct((grads, fields), F32),
            jax.ShapeDtypeStruct((2 * maps, lanes), F32),
        ]
        pack = pltpu.VMEM((1, 8, lanes), F32)
    return pl.pallas_call(
        functools.partial(filter_kernel, packed, scales),
        in_specs=[pl.BlockSpec(memory_space=pltpu.SMEM)] + [whole()] * 5,
        out_specs=[whole()] * (len(outs) + 3),
        out_shape=outs + kept,
        scratch_shapes=[
            pltpu.VMEM((2 * maps, pair), F32),
            pltpu.VMEM((maps * maps, pair), F32),
            pltpu.VMEM((fields, pair), F32),
            pltpu.VMEM((maps, pair), F32),
            pltpu.VMEM((2 * maps, pair), F32),
            pltpu.VMEM((grads, fields), F32),
            pack,
        ],
        compiler_params=params(),
        cost_estimate=cost(8 * maps * fields * fields * positions, 4 * received.size),
        name="filter_part",
    )(col, received, slot, cot, sym, second)


def embed_kernel(
    scale, slots, slot_ref, cot_ref, sym_ref, turned_ref, embed_ref, hidden_ref, lower_ref,
    out_ref, up_ref, low_ref, hid_ref, pair_ref,
):
    fields = slot_ref.shape[1]
    maps, positions = hidden_ref.shape
    lanes = cot_ref.shape[1]
    width = positions // lanes
    tabs = out_ref.shape[0]
    all_slots = tabs * slots
    pair = 2 * lanes
    spread = (lax.broadcasted_iota(jnp.int32, (all_slots, fields), 0) == slot_ref[...]).astype(BF16)
    up = (cot_ref[maps:, :].astype(F32) * scale).astype(BF16).astype(F32)
    up_ref[:, :lanes] = up
    up_ref[:, lanes:] = up

    def step(index, carry):
        here = pl.ds(pl.multiple_of(index * pair, pair), pair)
        x = embed_ref[:, here]
        low_ref[...] = lower_ref[:, here].astype(F32)
        hid_ref[...] = hidden_ref[:, here].astype(F32)
        upper = up_ref[...]
        for h in range(maps):
            pair_ref[h * maps : (h + 1) * maps, :] = (hid_ref[h : h + 1, :] * upper).astype(BF16)
        total = dot(turned_ref[...], pair_ref[...])
        rows = min(MATMUL_ROWS, maps * fields)
        for start in range(0, maps * fields, rows):
            y = dot(sym_ref[start : start + rows, :], x)
            for k in range(rows // fields):
                o = start // fields + k
                total = total + low_ref[o : o + 1, :] * y[k * fields : (k + 1) * fields]
        table = dot(spread, total.astype(BF16)).astype(BF16)
        for k in range(2):
            at = pl.ds(pl.multiple_of((2 * index + k) * slots, slots), slots)
            for t in range(tabs):
                out_ref[t, at, :] = table[t * slots : (t + 1) * slots, k * lanes : (k + 1) * lanes]
        return carry

    lax.fori_loop(0, width // 2, step, 0)


def embed_part(scale, slots, slot_row, cot, sym, turned, embed, hidden, lower, tabs, rows, width):
    fields = slot_row.shape[1]
    maps = hidden.shape[0]
    lanes = cot.shape[1]
    pair = 2 * lanes
    return pl.pallas_call(
        functools.partial(embed_kernel, scale, slots),
        in_specs=[whole()] * 7,
        out_specs=whole(),
        out_shape=jax.ShapeDtypeStruct((tabs, rows, lanes), BF16),
        scratch_shapes=[
            pltpu.VMEM((maps, pair), F32),
            pltpu.VMEM((maps, pair), F32),
            pltpu.VMEM((maps, pair), F32),
            pltpu.VMEM((maps * maps, pair), BF16),
        ],
        compiler_params=params(),
        cost_estimate=cost(4 * maps * fields * fields * width * lanes, 4 * tabs * rows * lanes),
        name="embed_part",
    )(slot_row, cot, sym, turned, embed, hidden, lower)


def owner_kernel(table_ref, out_ref, rows_ref):
    slots, width, _ = out_ref.shape
    tabs, _, lanes = table_ref.shape
    for t in range(tabs):
        rows_ref[...] = table_ref[t, : width * slots, :].astype(F32)
        for slot in range(slots):
            value = rows_ref[pl.ds(slot, width, stride=slots), :]
            out_ref[slot, :, pl.ds(t * lanes, lanes)] = value.astype(BF16)


def owner_part(table, slots, width):
    tabs, _, lanes = table.shape
    return pl.pallas_call(
        owner_kernel,
        in_specs=[whole()],
        out_specs=whole(),
        out_shape=jax.ShapeDtypeStruct((slots, width, tabs * lanes), BF16),
        scratch_shapes=[pltpu.VMEM((width * slots, lanes), F32)],
        compiler_params=params(),
        name="owner_part",
    )(table)


def per_device(bag_items, lengths, field_slot, filter_one, filter_two, cotangent):
    slots, _, width, samples = bag_items.shape
    tabs = lax.axis_size("tab")
    cols = lax.axis_size("col")
    devices = tabs * cols
    lanes = samples // tabs
    maps = filter_one.shape[0]
    fields = field_slot.shape[0]
    scale = (width * cols) ** -0.5
    scales = (scale, samples**-0.5)
    sent = pool(bag_items, lengths, tabs)
    received = lax.all_to_all(sent, "tab", split_axis=0, concat_axis=0, tiled=True)
    cot = lax.all_gather(cotangent, "col", axis=1, tiled=True)
    square = filter_one.reshape(maps, fields, fields).astype(F32)
    sym = (square + square.transpose(0, 2, 1)).astype(BF16).reshape(maps * fields, fields)
    second = filter_two.reshape(maps * maps, fields)
    turned = filter_two.reshape(maps, maps, fields).transpose(2, 1, 0).reshape(fields, maps * maps)
    small = slots % 16 != 0
    if small:
        received = received.reshape(tabs, width, slots, lanes).transpose(1, 0, 2, 3)
        received = received.reshape(1, width * tabs * slots, lanes)
    packable = (
        fields * fields == devices * lanes
        and fields * 2 == lanes
        and maps == devices
        and cols & (cols - 1) == 0
        and not small
    )
    col = lax.axis_index("col").astype(jnp.int32).reshape(1)
    results = filter_part(
        (cols, tabs) if packable else None,
        scales, col, received, field_slot.reshape(fields, 1), cot, sym, second, width,
    )
    embed, hidden, lower = results[-3:]
    table_rows = received.shape[1]
    block = maps + maps // 2
    if packable:
        parts = [results[0]]
        for r in range(1, cols):
            parts.append(lax.ppermute(results[r], "col", [(c, c ^ r) for c in range(cols)]))
        table = embed_part(
            scale, slots, field_slot.reshape(1, fields), cot, sym, turned, embed, hidden, lower,
            tabs, table_rows + block, width,
        )
        total = functools.reduce(lambda a, b: a + b, [part.astype(F32) for part in parts])
        grads = total[: tabs * block].astype(BF16).reshape(tabs, block, lanes)
        table = lax.dynamic_update_slice(table, grads, (0, table_rows, 0))
        returned = lax.all_to_all(table, "tab", split_axis=0, concat_axis=0, tiled=True)
        pooled_grad = owner_part(returned, slots, width)
        grads = jnp.sum(returned[:, table_rows:, :].astype(F32), axis=0)
        grad_one = grads[:maps]
        grad_two = jnp.concatenate([grads[maps:, :fields], grads[maps:, fields:]], axis=0)
        share = lanes // cols
        packs = total[tabs * block :]
        pooled = jnp.concatenate(
            [packs[:, g * share : (g + 1) * share] for g in range(lanes // share)], axis=0
        )
        return (pooled, grad_one, grad_two, pooled_grad)
    table = embed_part(
        scale, table_rows // width, field_slot.reshape(1, fields), cot, sym, turned, embed, hidden, lower,
        received.shape[0], table_rows, width,
    )
    if small:
        table = table.reshape(width, tabs, slots, lanes).transpose(1, 0, 2, 3)
        table = table.reshape(tabs, width * slots, lanes)
    returned = lax.all_to_all(table, "tab", split_axis=0, concat_axis=0, tiled=True)
    pooled_grad = owner_part(returned, slots, width)
    pooled = lax.psum_scatter(results[1], "col", scatter_dimension=1, tiled=True)
    shaped = results[0].reshape(fields + maps, maps, fields).transpose(1, 0, 2)
    grad_one = shaped[:, :fields].reshape(maps, tabs, cols, -1)
    grad_two = shaped[:, fields:].reshape(maps, tabs, cols, -1)
    grad_one = lax.psum_scatter(grad_one, "col", scatter_dimension=2, tiled=True)
    grad_two = lax.psum_scatter(grad_two, "col", scatter_dimension=2, tiled=True)
    grad_one = lax.psum_scatter(grad_one, "tab", scatter_dimension=1, tiled=True)
    grad_two = lax.psum_scatter(grad_two, "tab", scatter_dimension=1, tiled=True)
    return (pooled, grad_one.reshape(maps, -1), grad_two.reshape(maps, -1), pooled_grad)


def solution(mesh):
    in_specs = (P("tab", None, "col", None), P("tab", None), P(), P(), P(), P(None, ("tab", "col")))
    out_specs = (
        P(None, ("tab", "col")),
        P(None, ("tab", "col")),
        P(None, ("tab", "col")),
        P("tab", "col", None),
    )
    return jax.shard_map(
        per_device, mesh=mesh, in_specs=in_specs, out_specs=out_specs, check_vma=False
    )
```

time: 346 us -> 61.3 us (0.18)
  waiting for transfers between devices: 189 us -> 18.7 us
  other arithmetic: 55.6 us -> 0.86 us
  local copies, waits for them, and re-layouts: 45.9 us -> 6.87 us
  matrix products: 24.1 us -> 0 us
  Pallas kernels: 0 us -> 15.5 us
  between operations: 14.1 us -> 0.81 us
    reduce_scatter x4 -> x0, waiting for transfers between devices: 164 us -> none  [the longest x1 65 us: per_device(): lax.psum_scatter(second_shaped, 'tab', scatter_dimension=1, tiled=True)]
    reduce_sum x11 -> x1, other arithmetic: 40.8 us -> 0.02 us  [per_device(): grads = jnp.sum(returned[:, table_rows:, :].astype(F32), axis=0)]
    convert_element_type x7 -> x2, local copies, waits for them, and re-layouts: 30.4 us -> 0.74 us  [per_device(): square = filter_one.reshape(maps, fields, fields).astype(F32)]
    dot_general x18 -> x0, matrix products: 24.1 us -> none  [the longest x3 9.73 us: cross_block(): lax.dot_general(filter_one, lower_grad, (((0,), (0,)), ((), ())), preferr...]
    unnamed x6 -> x0, waiting for transfers between devices: 19.8 us -> none
    pallas_call x0 -> x4, Pallas kernels: none -> 15.5 us  [the longest x1 8.28 us: filter_part(): pl.pallas_call(functools.partial(filter_kernel, packed, scales), in_specs...]
    all_to_all x2, waiting for transfers between devices: 5.21 us -> 18.7 us  [the longest x1 13.6 us: per_device(): lax.all_to_all(table, 'tab', split_axis=0, concat_axis=0, tiled=True)]
    mul x12 -> x0, other arithmetic: 9.67 us -> none  [the longest x3 6.6 us: cross_block(): first_cols[:, None, :] * first_cols[None, :, :]]
  transfers between devices with their start and end apart: 7 -> 5, of which waited for: 6 -> 2; matrix products, arithmetic and copies ran while one was open for 3% -> 4% of each run, Pallas kernels for 0% -> 8%
where the time goes in v1:
time: 61.3 us; the launch traced here: 60.9 us
  waiting for transfers between devices  18.7 us (31%)
  Pallas kernels  15.5 us (25%)
  starting transfers between devices  13 us (21%)
  local copies, waits for them, and re-layouts  6.87 us (11%)
  blocking collectives  5.19 us (8%)
  other arithmetic  0.86 us (1%)
  between operations  0.81 us (1%)
    all_to_all x1, waiting for transfers between devices, per_device(): lax.all_to_all(table, 'tab', split_axis=0, concat_axis=0, tiled=True)  13.6 us
    pallas_call x1, Pallas kernels, filter_part(): pl.pallas_call(functools.partial(filter_kernel, packed, scales), in_specs...  8.28 us
    all_to_all x1, starting transfers between devices, per_device(): lax.all_to_all(sent, 'tab', split_axis=0, concat_axis=0, tiled=True)  7.41 us
    all_gather x1, blocking collectives, per_device(): cot = lax.all_gather(cotangent, 'col', axis=1, tiled=True)  5.19 us
    all_to_all x1, waiting for transfers between devices, per_device(): lax.all_to_all(sent, 'tab', split_axis=0, concat_axis=0, tiled=True)  5.07 us
    pallas_call x1, Pallas kernels, embed_part(): pl.pallas_call(functools.partial(embed_kernel, scale, slots), in_specs=[w...  4.98 us
    unnamed x15, local copies, waits for them, and re-layouts  3.79 us
    all_to_all x1, starting transfers between devices, per_device(): lax.all_to_all(table, 'tab', split_axis=0, concat_axis=0, tiled=True)  3.62 us
  transfers between devices with their start and end apart: 5, of which 2 were waited for; matrix products, arithmetic and copies ran while one was open for 4% of the time, Pallas kernels for 8%

profile of v1, /device:TPU:0, one launch (start us, length us, event | category | flops | bytes accessed | tf_op | source)
XLA Modules:
  0.0 60.9 jit_solution(9415631352108829999)
XLA Ops:
  0.6 2.1 %copy.25.bag_ref = bf16[16,4,12,1024]{3,2,1,0:T(8,128)(2,1)S(1)} copy(bf16[16,4,12,1024]{3,1,2,0:T(4,128)(2,1)} %param.6) | data formatting | bytes 3145728 | tf_op args[0]
  2.8 0.0 copy-start.4
  2.8 2.0 %pool_bags.1 = bf16[8,192,128]{2,1,0:T(8,128)(2,1)} custom-call(bf16[16,4,12,1024]{3,2,1,0:T(8,128)(2,1)S(1)} %copy.25.bag_ref, s32[16,1024]{1,0:T(8,128)S(1)} %copy-done), custom_call_target="tpu_custom_call" | custom-call | tf_op jit(solution)/shard_map/pool_bags/pallas_call | solution.py:56
  4.8 7.4 %all-to-all-start = ((bf16[8,192,128]{2,1,0:T(8,128)(2,1)}), bf16[8,192,128]{2,1,0:T(8,128)(2,1)S(1)}, u32[]{:S(2)}, u32[]{:S(2)}) async-start(bf16[8,192,128]{2,1,0:T(8,128)(2,1)} %pool_bags.1), calls=%async_computation | async-start | bytes 786432 | tf_op jit(solution)/shard_map/all_to_all | solution.py:332
  12.2 0.4 reshape.43
  12.6 0.3 copy.26
  13.0 5.2 %all_gather.3 = bf16[64,128]{0,1:T(8,128)(2,1)S(1)} all-gather(bf16[64,32]{0,1:T(8,128)(2,1)S(1)} %copy-done.5), channel_id=1, replica_groups=mesh['tab'=8,'col'=4] {'col'}, dimensions={1}, use_global_device_ids=true | all-gather | bytes 20480 | tf_op jit(solution)/shard_map/all_gather | solution.py:333
  18.1 0.1 copy.28.cot_ref
  18.2 0.2 reshape.38.second_ref
  18.5 0.1 copy.27.slot_ref
  18.6 0.2 fusion
  18.8 5.1 %all-to-all-done.received_ref = bf16[8,192,128]{2,1,0:T(8,128)(2,1)S(1)} async-done(((bf16[8,192,128]{2,1,0:T(8,128)(2,1)}), bf16[8,192,128]{2,1,0:T(8,128)(2,1)S(1)}, u32[]{:S(2)}, u32[]{:S(2)}) %all-to-all-start) | async-done | bytes 393248 | tf_op jit(solution)/shard_map/all_to_all | solution.py:332
  23.9 8.3 %filter_part.1 = (bf16[400,128]{1,0:T(8,128)(2,1)S(1)}, bf16[400,128]{1,0:T(8,128)(2,1)S(1)}, bf16[400,128]{1,0:T(8,128)(2,1)S(1)}, bf16[400,128]{1,0:T(8,128)(2...) custom-call(s32[1]{0:T(128)} %bitcast.col_ref, ...), custom_call_target="tpu_custom_call" | custom-call | flops 1610612736 | bytes 786432 | tf_op jit(solution)/shard_map/filter_part/pallas_call | solution.py:215
  32.1 0.1 collective-permute-start
  32.2 1.6 %collective-permute-start.1 = (bf16[400,128]{1,0:T(8,128)(2,1)S(1)}, bf16[400,128]{1,0:T(8,128)(2,1)S(1)}, u32[]{:S(2)}, u32[]{:S(2)}) collective-permute-start(bf16[400,128]{1,0:T(8,128)(2,1)S(1)} %get-tuple-element.13), channel_id=1, source_target_pairs={{0,2},{1,3},{2,0},{3,1},{4,6},{5,7},{6,4},{7,5},{8,10},{9,11},{10,... | collective-permute-start | bytes 307208 | tf_op jit(solution)/shard_map/ppermute | solution.py:360
  33.8 0.3 collective-permute-start.2
  34.1 0.2 reshape.40
  34.3 0.1 copy.29
  34.5 0.1 copy.31.turned_ref
  34.6 5.0 %embed_part.1 = bf16[8,240,128]{2,1,0:T(8,128)(2,1)} custom-call(s32[1,64]{1,0:T(1,128)S(1)} %bitcast.15, bf16[64,128]{1,0:T(8,128)(2,1)S(1)} %copy.28.cot_ref, bf16[2048,64]{1,0:T(8,128)(2,1)S(1)} %bitcast.13, bf16[64,1024]{1,0:T(8,128)(2,1)S(1)} %copy.31.turned_ref, bf16[64,1536]{1,0:T(8,128)(2,1)S(1)} %get-tuple-element.15.embed_ref, ...), custom_call_target="tpu_custom_call" | custom-call | flops 805306368 | bytes 983040 | tf_op jit(solution)/shard_map/embed_part/pallas_call | solution.py:281
  39.6 0.0 collective-permute-done
  39.6 0.1 convert_add_fusion
  39.7 0.7 %constant_dynamic-update-slice_fusion = bf16[8,240,128]{2,1,0:T(8,128)(2,1)} fusion(bf16[8,240,128]{2,1,0:T(8,128)(2,1)} %embed_part.1, bf16[8,48,128]{2,1,0:T(8,128)(2,1)S(1)} %bitcast.17), kind=kLoop, calls=%fused_computation.7 | loop fusion | bytes 196608 | tf_op jit(solution)/shard_map/dynamic_update_slice | solution.py:367
  40.3 3.6 %all-to-all-start.1 = ((bf16[8,240,128]{2,1,0:T(8,128)(2,1)}), bf16[8,240,128]{2,1,0:T(8,128)(2,1)S(1)}, u32[]{:S(2)}, u32[]{:S(2)}) async-start(bf16[8,240,128]{2,1,0:T(8,128)(2,1)} %constant_dynamic-update-slice_fusion), calls=%async_computation.1 | async-start | bytes 983040 | tf_op jit(solution)/shard_map/all_to_all | solution.py:368
  44.0 0.1 fusion.1
  44.0 0.7 %copy.32 = f32[64,32]{0,1:T(8,128)} copy(f32[64,32]{1,0:T(8,128)S(1)} %pad_maximum_fusion) | data formatting | bytes 16384
  44.7 13.6 %all-to-all-done.1.table_ref = bf16[8,240,128]{2,1,0:T(8,128)(2,1)S(1)} async-done(((bf16[8,240,128]{2,1,0:T(8,128)(2,1)}), bf16[8,240,128]{2,1,0:T(8,128)(2,1)S(1)}, u32[]{:S(2)}, u32[]{:S(2)}) %all-to-all-start.1) | async-done | bytes 491552 | tf_op jit(solution)/shard_map/all_to_all | solution.py:368
  58.4 0.1 fusion.2
  58.4 0.6 slice.48
  59.0 0.3 owner_part.1
  59.3 1.0 %copy.33 = bf16[16,12,1024]{2,0,1:T(8,128)(2,1)} copy(bf16[16,12,1024]{2,1,0:T(8,128)(2,1)S(1)} %owner_part.1) | data formatting | bytes 786432
  60.3 0.6 pad_maximum_fusion.1
  (16 shorter events, 0.1 us)
Async XLA Ops:
  0.6 2.1 %copy-start = (s32[16,1024]{1,0:T(8,128)S(1)}, s32[16,1024]{1,0:T(8,128)}, u32[]{:S(2)}) copy-start(s32[16,1024]{1,0:T(8,128)} %lengths_ref.1) | copy-start | bytes 196612
  2.8 9.4 %copy-start.4 = (bf16[32,4096]{1,0:T(8,128)(2,1)S(1)}, bf16[32,4096]{1,0:T(8,128)(2,1)}, u32[]{:S(2)}) copy-start(bf16[32,4096]{1,0:T(8,128)(2,1)} %param.9) | copy-start | bytes 786436
  4.7 8.2 %copy-start.5 = (bf16[64,32]{0,1:T(8,128)(2,1)S(1)}, bf16[64,32]{0,1:T(8,128)(2,1)}, u32[]{:S(2)}) copy-start(bf16[64,32]{0,1:T(8,128)(2,1)} %param.11) | copy-start | bytes 12292
  4.8 13.5 %copy-start.2 = (bf16[32,2048]{1,0:T(8,128)(2,1)S(1)}, bf16[32,2048]{1,0:T(8,128)(2,1)}, u32[]{:S(2)}) copy-start(bf16[32,2048]{1,0:T(8,128)(2,1)} %param.10) | copy-start | bytes 393220
  4.8 19.1 %all-to-all-start = ((bf16[8,192,128]{2,1,0:T(8,128)(2,1)}), bf16[8,192,128]{2,1,0:T(8,128)(2,1)S(1)}, u32[]{:S(2)}, u32[]{:S(2)}) async-start(bf16[8,192,128]{2,1,0:T(8,128)(2,1)} %pool_bags.1), calls=%async_computation | async-start | bytes 786432 | tf_op jit(solution)/shard_map/all_to_all | solution.py:332
  12.2 6.3 %copy-start.1 = (s32[64]{0:T(128)S(1)}, s32[64]{0:T(128)}, u32[]{:S(2)}) copy-start(s32[64]{0:T(128)} %param.8) | copy-start | bytes 772
  23.9 10.2 %copy-start.3 = (bf16[32,2048]{1,0:T(8,128)(2,1)S(1)}, bf16[32,2048]{1,0:T(8,128)(2,1)}, u32[]{:S(2)}) copy-start(bf16[32,2048]{1,0:T(8,128)(2,1)} %param.10) | copy-start | bytes 393220
  32.1 7.4 %collective-permute-start = (bf16[400,128]{1,0:T(8,128)(2,1)S(1)}, bf16[400,128]{1,0:T(8,128)(2,1)S(1)}, u32[]{:S(2)}, u32[]{:S(2)}) collective-permute-start(bf16[400,128]{1,0:T(8,128)(2,1)S(1)} %get-tuple-element.12), channel_id=1, source_target_pairs={{0,1},{1,0},{2,3},{3,2},{4,5},{5,4},{6,7},{7,6},{8,9},{9,8},{10,11... | collective-permute-start | bytes 307208 | tf_op jit(solution)/shard_map/ppermute | solution.py:360
  32.2 7.3 %collective-permute-start.1 = (bf16[400,128]{1,0:T(8,128)(2,1)S(1)}, bf16[400,128]{1,0:T(8,128)(2,1)S(1)}, u32[]{:S(2)}, u32[]{:S(2)}) collective-permute-start(bf16[400,128]{1,0:T(8,128)(2,1)S(1)} %get-tuple-element.13), channel_id=1, source_target_pairs={{0,2},{1,3},{2,0},{3,1},{4,6},{5,7},{6,4},{7,5},{8,10},{9,11},{10,... | collective-permute-start | bytes 307208 | tf_op jit(solution)/shard_map/ppermute | solution.py:360
  33.8 5.8 %collective-permute-start.2 = (bf16[400,128]{1,0:T(8,128)(2,1)S(1)}, bf16[400,128]{1,0:T(8,128)(2,1)S(1)}, u32[]{:S(2)}, u32[]{:S(2)}) collective-permute-start(bf16[400,128]{1,0:T(8,128)(2,1)S(1)} %get-tuple-element.14), channel_id=1, source_target_pairs={{0,3},{1,2},{2,1},{3,0},{4,7},{5,6},{6,5},{7,4},{8,11},{9,10},{10,... | collective-permute-start | bytes 307208 | tf_op jit(solution)/shard_map/ppermute | solution.py:360
  40.3 18.0 %all-to-all-start.1 = ((bf16[8,240,128]{2,1,0:T(8,128)(2,1)}), bf16[8,240,128]{2,1,0:T(8,128)(2,1)S(1)}, u32[]{:S(2)}, u32[]{:S(2)}) async-start(bf16[8,240,128]{2,1,0:T(8,128)(2,1)} %constant_dynamic-update-slice_fusion), calls=%async_computation.1 | async-start | bytes 983040 | tf_op jit(solution)/shard_map/all_to_all | solution.py:368

commit v2 on v1

v2 whole, which is shorter than its diff:
```python
import functools

import jax
import jax.numpy as jnp
from jax import lax
from jax.experimental import pallas as pl
from jax.experimental.pallas import tpu as pltpu
from jax.sharding import PartitionSpec as P

BF16 = jnp.bfloat16
F32 = jnp.float32
VMEM_BYTES = 48 * 1024 * 1024
MATMUL_ROWS = 512


def params():
    return pltpu.CompilerParams(vmem_limit_bytes=VMEM_BYTES)


def cost(flops, moved):
    return pl.CostEstimate(flops=flops, bytes_accessed=moved, transcendentals=0)


def whole():
    return pl.BlockSpec(memory_space=pltpu.VMEM)


def dot(left, right):
    return jnp.dot(left, right, preferred_element_type=F32)


def dot_lanes(left, right):
    return lax.dot_general(left, right, (((1,), (1,)), ((), ())), preferred_element_type=F32)


def pool_kernel(steps, bag_hbm, lengths_hbm, out_ref, bag_ref, lengths_ref, rows_ref, sems):
    slots, width, items, _ = bag_hbm.shape
    chunks, _, lanes = out_ref.shape
    per_step = chunks // steps
    counts = pltpu.make_async_copy(lengths_hbm, lengths_ref, sems.at[steps])
    counts.start()
    copies = []
    for k in range(steps):
        part = pl.ds(k * per_step * lanes, per_step * lanes)
        copy = pltpu.make_async_copy(
            bag_hbm.at[:, :, :, part], bag_ref.at[:, :, :, part], sems.at[k]
        )
        copy.start()
        copies.append(copy)
    counts.wait()
    for chunk in range(chunks):
        if chunk % per_step == 0:
            copies[chunk // per_step].wait()
        here = pl.ds(chunk * lanes, lanes)
        buffer = chunk % 2
        for slot in range(slots):
            at = slot * width * items
            rows_ref[buffer, at : at + width * items, :] = (
                bag_ref[slot, :, :, here].astype(F32).reshape(width * items, lanes)
            )
        count = lengths_ref[:, here]
        for d in range(width):
            total = jnp.zeros((slots, lanes), F32)
            for item in range(items):
                value = rows_ref[buffer, pl.ds(d * items + item, slots, stride=width * items), :]
                total = total + jnp.where(count > item, value, 0.0)
            out_ref[chunk, d * slots : (d + 1) * slots, :] = total.astype(BF16)


def pool(bag_items, lengths, tab_count):
    bag = bag_items.transpose(0, 2, 1, 3)
    slots, width, items, samples = bag.shape
    lanes = samples // tab_count
    steps = min(4, tab_count)
    return pl.pallas_call(
        functools.partial(pool_kernel, steps),
        in_specs=[pl.BlockSpec(memory_space=pltpu.HBM)] * 2,
        out_specs=whole(),
        out_shape=jax.ShapeDtypeStruct((tab_count, width * slots, lanes), BF16),
        scratch_shapes=[
            pltpu.VMEM(bag.shape, BF16),
            pltpu.VMEM(lengths.shape, jnp.int32),
            pltpu.VMEM((2, width * slots * items, lanes), F32),
            pltpu.SemaphoreType.DMA((steps + 1,)),
        ],
        compiler_params=pltpu.CompilerParams(vmem_limit_bytes=62 * 1024 * 1024),
        name="pool_bags",
    )(bag, lengths)


def embed_kernel(
    scale,
    received_ref, slot_ref, slot_row_ref, cot_ref, sym_ref, second_ref, inner_ref,
    table_ref, embed_ref, hidden_ref, lower_ref, one_ref,
    up_ref, x_ref, low_ref, maps_ref, sum_ref, buf_ref,
):
    fields = slot_ref.shape[0]
    maps, positions = hidden_ref.shape
    lanes = cot_ref.shape[1]
    width = positions // lanes
    tabs = received_ref.shape[0]
    slots = received_ref.shape[1] // width
    pair = 2 * lanes
    all_slots = tabs * slots
    onehot = (lax.broadcasted_iota(jnp.int32, (fields, all_slots), 1) == slot_ref[...]).astype(BF16)
    spread = (
        lax.broadcasted_iota(jnp.int32, (all_slots, fields), 0) == slot_row_ref[...]
    ).astype(BF16)
    up = (cot_ref[...].astype(F32) * scale).astype(BF16).astype(F32)
    up_ref[:, :lanes] = up
    up_ref[:, lanes:] = up
    for d in range(width):
        parts = [received_ref[t, d * slots : (d + 1) * slots, :] for t in range(tabs)]
        x = dot(onehot, parts[0] if len(parts) == 1 else jnp.concatenate(parts, axis=0))
        x_ref[:, d * lanes : (d + 1) * lanes] = x
        embed_ref[:, d * lanes : (d + 1) * lanes] = x.astype(BF16)
    sum_ref[...] = jnp.zeros_like(sum_ref)

    rows = 1024
    jobs = []
    for p in range(width // 2):
        jobs += [("z", p, start) for start in range(0, maps * maps, rows)]
        jobs += [("y", p, start) for start in range(0, maps * fields, rows)]

    def issue(number):
        kind, p, start = jobs[number]
        source = second_ref if kind == "z" else sym_ref
        x = embed_ref[:, p * pair : (p + 1) * pair]
        buf_ref[number % 2] = dot(source[start : start + rows, :], x)

    state = {}
    def consume(number):
        kind, p, start = jobs[number]
        here = pl.ds(p * pair, pair)
        b = p % 2
        y_ref = buf_ref.at[number % 2]
        if kind == "z":
            lower = up_ref[:maps, :] if start == 0 else state["lower"]
            for k in range(rows // maps):
                o = start // maps + k
                lower = lower + up_ref[maps + o : maps + o + 1, :] * y_ref[k * maps : (k + 1) * maps, :]
            state["lower"] = lower
            if start + rows == maps * maps:
                lower = lower.astype(BF16)
                lower_ref[:, here] = lower
                low_ref[b] = lower.astype(F32)
            return
        gradient = jnp.zeros((fields, pair), F32) if start == 0 else state["gradient"]
        x_float = x_ref[:, here]
        for k in range(rows // fields):
            o = start // fields + k
            mine = y_ref[k * fields : (k + 1) * fields, :]
            gradient = gradient + low_ref[b, o : o + 1, :] * mine
            maps_ref[b, o : o + 1, :] = 0.5 * jnp.sum(mine * x_float, axis=0, keepdims=True)
        state["gradient"] = gradient
        if start + rows < maps * fields:
            return
        first_maps = maps_ref[b]
        sum_ref[...] += first_maps
        hidden = first_maps.astype(BF16)
        hidden_ref[:, here] = hidden
        maps_ref[b] = hidden.astype(F32)
        sides = [gradient[:, :lanes], gradient[:, lanes:]]
        for h in range(maps):
            inner = inner_ref[h * fields : (h + 1) * fields, :]
            for k in range(2):
                sides[k] = sides[k] + maps_ref[b, h : h + 1, k * lanes : (k + 1) * lanes] * inner
        for k in range(2):
            table = dot(spread, sides[k].astype(BF16)).astype(BF16)
            at = (2 * p + k) * slots
            for t in range(tabs):
                table_ref[t, at : at + slots, :] = table[t * slots : (t + 1) * slots, :]

    ahead = 1
    for number in range(ahead):
        issue(number)
    for number in range(len(jobs)):
        if number + ahead < len(jobs):
            issue(number + ahead)
        consume(number)
    one_ref[...] = sum_ref[:, :lanes] + sum_ref[:, lanes:]


def embed_part(scale, received, slot, cot, sym, second, inner, width):
    fields = slot.shape[0]
    maps = cot.shape[0] // 2
    lanes = cot.shape[1]
    positions = width * lanes
    pair = 2 * lanes
    return pl.pallas_call(
        functools.partial(embed_kernel, scale),
        in_specs=[whole()] * 7,
        out_specs=[whole()] * 5,
        out_shape=[
            jax.ShapeDtypeStruct(received.shape, BF16),
            jax.ShapeDtypeStruct((fields, positions), BF16),
            jax.ShapeDtypeStruct((maps, positions), BF16),
            jax.ShapeDtypeStruct((maps, positions), BF16),
            jax.ShapeDtypeStruct((maps, lanes), F32),
        ],
        scratch_shapes=[
            pltpu.VMEM((2 * maps, pair), F32),
            pltpu.VMEM((fields, positions), F32),
            pltpu.VMEM((2, maps, pair), F32),
            pltpu.VMEM((2, maps, pair), F32),
            pltpu.VMEM((maps, pair), F32),
            pltpu.VMEM((2, 1024, pair), F32),
        ],
        compiler_params=params(),
        cost_estimate=cost(8 * maps * fields * fields * positions, 4 * received.size),
        name="embed_part",
    )(received, slot.reshape(fields, 1), slot.reshape(1, fields), cot, sym, second, inner)


def filter_kernel(
    packed, scales, place_ref, cot_ref, second_ref, embed_ref, hidden_ref, lower_ref, one_ref, *refs
):
    outs = refs[:2]
    x_ref, hid_ref, inner_ref, grad_ref, pair_ref, pack_ref = refs[2:]
    fields = embed_ref.shape[0]
    maps, positions = hidden_ref.shape
    lanes = cot_ref.shape[1]
    width = positions // lanes
    pair = 2 * lanes
    scale = scales[0]
    up = (cot_ref[maps:, :].astype(F32) * scale).astype(BF16)
    x_ref[...] = embed_ref[...].astype(F32)
    hid_ref[...] = hidden_ref[...].astype(F32)
    rows = 512
    steps = [
        (p, start) for p in range(width // 2) for start in range(0, fields * maps, rows)
    ]

    def products(number):
        p, start = steps[number]
        here = pl.ds(p * pair, pair)
        lower = lower_ref[:, here].astype(F32)
        for k in range(rows // maps):
            f = start // maps + k
            pair_ref[number % 2, k * maps : (k + 1) * maps, :] = (
                x_ref[f : f + 1, here] * lower
            ).astype(BF16)

    def sums(number):
        p, start = steps[number]
        part = dot_lanes(pair_ref[number % 2], embed_ref[:, p * pair : (p + 1) * pair])
        if p == 0:
            grad_ref[start : start + rows, :] = part
        else:
            grad_ref[start : start + rows, :] += part

    def inner(first, count):
        totals = [jnp.zeros((fields, lanes), F32)] * count
        for d in range(width):
            here = pl.ds(d * lanes, lanes)
            x = x_ref[:, here]
            for k in range(count):
                totals[k] = totals[k] + hid_ref[first + k : first + k + 1, here] * x
        for k in range(count):
            at = (first + k) * fields
            inner_ref[at : at + fields, :] = totals[k].astype(BF16)

    group, first = 4, 0
    products(0)
    for number in range(len(steps)):
        if number + 1 < len(steps):
            products(number + 1)
        if number % 3 == 0 and first < maps:
            inner(first, group)
            first += group
        sums(number)
    for first in range(first, maps, group):
        inner(first, group)
    base = fields * maps
    second = dot_lanes(up, inner_ref[...])
    for h in range(maps):
        grad_ref[base + h * maps : base + (h + 1) * maps, :] = second[:, h * fields : (h + 1) * fields]
    two = dot(second_ref[...], inner_ref[...])
    pooled = jnp.concatenate([one_ref[...], two], axis=0) * scale
    if not packed:
        outs[0][...] = grad_ref[...] * scales[1]
        outs[1][...] = pooled
        return
    cols, tabs = packed
    share = lanes // cols
    tall = 2 * maps * share // lanes
    for c in range(cols):
        pack_ref[c] = jnp.concatenate(
            [
                pooled[g * tall : (g + 1) * tall, c * share : (c + 1) * share]
                for g in range(lanes // share)
            ],
            axis=1,
        )
    own_col = place_ref[0]
    block = maps + maps // 2
    rows = tabs * block + tall
    for r in range(cols):
        c = jnp.bitwise_xor(own_col, r)
        out, base = outs[r % 2], r // 2 * rows
        for q in range(tabs):
            k = q * cols + c
            first = grad_ref[pl.ds(pl.multiple_of(k * 2 * maps, 2 * maps), 2 * maps), :]
            first = jnp.concatenate([first[:maps], first[maps:]], axis=1)
            second = grad_ref[pl.ds(pl.multiple_of((2 * tabs * cols + k) * maps, maps), maps), :]
            second = jnp.concatenate([second[: maps // 2], second[maps // 2 :]], axis=1)
            out[base + q * block : base + (q + 1) * block, :] = (
                jnp.concatenate([first, second], axis=0) * scales[1]
            ).astype(BF16)
        out[base + tabs * block : base + rows, :] = pack_ref[c].astype(BF16)


def filter_part(packed, scales, place, cot, second, embed, hidden, lower, one):
    fields, positions = embed.shape
    maps = hidden.shape[0]
    lanes = cot.shape[1]
    pair = 2 * lanes
    grads = (fields + maps) * maps
    if packed:
        cols, tabs = packed
        tall = 2 * maps // cols
        piece = (cols // 2 * (tabs * (maps + maps // 2) + tall), lanes)
        outs = [jax.ShapeDtypeStruct(piece, BF16)] * 2
        pack = pltpu.VMEM((cols, tall, lanes), F32)
    else:
        outs = [
            jax.ShapeDtypeStruct((grads, fields), F32),
            jax.ShapeDtypeStruct((2 * maps, lanes), F32),
        ]
        pack = pltpu.VMEM((1, 8, lanes), F32)
    return pl.pallas_call(
        functools.partial(filter_kernel, packed, scales),
        in_specs=[pl.BlockSpec(memory_space=pltpu.SMEM)] + [whole()] * 6,
        out_specs=[whole()] * len(outs),
        out_shape=outs,
        scratch_shapes=[
            pltpu.VMEM((fields, positions), F32),
            pltpu.VMEM((maps, positions), F32),
            pltpu.VMEM((maps * fields, lanes), BF16),
            pltpu.VMEM((grads, fields), F32),
            pltpu.VMEM((2, 512, pair), BF16),
            pack,
        ],
        compiler_params=params(),
        cost_estimate=cost(6 * maps * fields * fields * positions, 8 * embed.size),
        name="filter_part",
    )(place, cot, second, embed, hidden, lower, one)


def owner_kernel(table_ref, out_ref):
    width, slots, _ = out_ref.shape
    tabs, _, lanes = table_ref.shape
    for t in range(tabs):
        for d in range(width):
            out_ref[d, :, t * lanes : (t + 1) * lanes] = table_ref[t, d * slots : (d + 1) * slots, :]


def owner_part(table, slots, width):
    tabs, _, lanes = table.shape
    return pl.pallas_call(
        owner_kernel,
        in_specs=[whole()],
        out_specs=whole(),
        out_shape=jax.ShapeDtypeStruct((width, slots, tabs * lanes), BF16),
        compiler_params=params(),
        name="owner_part",
    )(table).transpose(1, 0, 2)


def grad_kernel(count, *refs):
    parts, (one_ref, two_ref) = refs[:count], refs[count:]
    maps, lanes = one_ref.shape
    blocks = [part[...] for part in parts] if count > 1 else [parts[0][t] for t in range(parts[0].shape[0])]
    total = functools.reduce(lambda a, b: a + b, [block.astype(F32) for block in blocks])
    one_ref[...] = total[:maps]
    two_ref[: maps // 2, :] = total[maps:, : lanes // 2]
    two_ref[maps // 2 :, :] = total[maps:, lanes // 2 :]


def grad_part(parts, maps):
    parts = parts if isinstance(parts, list) else [parts]
    lanes = parts[0].shape[-1]
    return pl.pallas_call(
        functools.partial(grad_kernel, len(parts)),
        in_specs=[whole()] * len(parts),
        out_specs=[whole()] * 2,
        out_shape=[
            jax.ShapeDtypeStruct((maps, lanes), F32),
            jax.ShapeDtypeStruct((maps, lanes // 2), F32),
        ],
        compiler_params=params(),
        name="grad_part",
    )(*parts)


def per_device(bag_items, lengths, field_slot, filter_one, filter_two, cotangent):
    slots, _, width, samples = bag_items.shape
    tabs = lax.axis_size("tab")
    cols = lax.axis_size("col")
    devices = tabs * cols
    lanes = samples // tabs
    maps = filter_one.shape[0]
    fields = field_slot.shape[0]
    scale = (width * cols) ** -0.5
    scales = (scale, samples**-0.5)
    sent = pool(bag_items, lengths, tabs)
    received = lax.all_to_all(sent, "tab", split_axis=0, concat_axis=0, tiled=True)
    cot = lax.all_gather(cotangent, "col", axis=1, tiled=True)
    square = filter_one.reshape(maps, fields, fields).astype(F32)
    sym = (square + square.transpose(0, 2, 1)).astype(BF16).reshape(maps * fields, fields)
    second = filter_two.reshape(maps * maps, fields)
    upper = (cot[maps:].astype(F32) * scale).astype(BF16)
    inner = lax.dot_general(
        filter_two, upper, (((0,), (0,)), ((), ())), preferred_element_type=F32
    ).astype(BF16).astype(F32)
    small = slots % 16 != 0
    if small:
        received = received.reshape(tabs, width, slots, lanes).transpose(1, 0, 2, 3)
        received = received.reshape(1, width * tabs * slots, lanes)
    packable = (
        fields * fields == devices * lanes
        and fields * 2 == lanes
        and maps == devices
        and cols & (cols - 1) == 0
        and cols > 1
        and tabs & (tabs - 1) == 0
        and not small
    )
    place = lax.axis_index("col").astype(jnp.int32).reshape(1)
    table, embed, hidden, lower, one = embed_part(
        scale, received, field_slot, cot, sym, second, inner, width
    )
    results = filter_part(
        (cols, tabs) if packable else None, scales, place, cot, filter_two, embed, hidden, lower, one
    )
    if small:
        table = table.reshape(width, tabs, slots, lanes).transpose(1, 0, 2, 3)
        table = table.reshape(tabs, width * slots, lanes)
    returned = lax.all_to_all(table, "tab", split_axis=0, concat_axis=0, tiled=True)
    if packable:
        block = maps + maps // 2
        def swap(value, bit, pieces):
            step = value.shape[0] // pieces
            moved = [
                lax.ppermute(
                    value[i * step : (i + 1) * step], "col", [(c, c ^ bit) for c in range(cols)]
                )
                for i in range(pieces)
            ]
            return jnp.concatenate(moved, axis=0) if pieces > 1 else moved[0]

        total = results[0].astype(F32) + swap(results[1], 1, 2).astype(F32)
        half = total.shape[0] // 2
        total = total[:half] + swap(total[half:].astype(BF16), 2, 1).astype(F32)
        grads = total[: tabs * block].astype(BF16).reshape(tabs, block, lanes)
        returned, grads = lax.optimization_barrier((returned, grads))
        grads = lax.all_to_all(grads, "tab", split_axis=0, concat_axis=0, tiled=True)
        pooled_grad = owner_part(returned, slots, width)
        grad_one, grad_two = grad_part(grads, maps)
        share = lanes // cols
        packs = total[tabs * block :]
        pooled = jnp.concatenate(
            [packs[:, g * share : (g + 1) * share] for g in range(lanes // share)], axis=0
        )
        return (pooled, grad_one, grad_two, pooled_grad)
    pooled_grad = owner_part(returned, slots, width)
    pooled = lax.psum_scatter(results[1], "col", scatter_dimension=1, tiled=True)
    shaped = results[0].reshape(fields + maps, maps, fields).transpose(1, 0, 2)
    grad_one = shaped[:, :fields].reshape(maps, tabs, cols, -1)
    grad_two = shaped[:, fields:].reshape(maps, tabs, cols, -1)
    grad_one = lax.psum_scatter(grad_one, "col", scatter_dimension=2, tiled=True)
    grad_two = lax.psum_scatter(grad_two, "col", scatter_dimension=2, tiled=True)
    grad_one = lax.psum_scatter(grad_one, "tab", scatter_dimension=1, tiled=True)
    grad_two = lax.psum_scatter(grad_two, "tab", scatter_dimension=1, tiled=True)
    return (pooled, grad_one.reshape(maps, -1), grad_two.reshape(maps, -1), pooled_grad)


def solution(mesh):
    in_specs = (P("tab", None, "col", None), P("tab", None), P(), P(), P(), P(None, ("tab", "col")))
    out_specs = (
        P(None, ("tab", "col")),
        P(None, ("tab", "col")),
        P(None, ("tab", "col")),
        P("tab", "col", None),
    )
    return jax.shard_map(
        per_device, mesh=mesh, in_specs=in_specs, out_specs=out_specs, check_vma=False
    )
```

time: 61.3 us -> 57.4 us (0.936)
  starting transfers between devices: 13 us -> 18.1 us
  waiting for transfers between devices: 18.7 us -> 13.9 us
  local copies, waits for them, and re-layouts: 6.87 us -> 4.44 us
  Pallas kernels: 15.5 us -> 13.9 us
    all_to_all x1, waiting for transfers between devices: 13.6 us -> 0.91 us  [per_device(): lax.all_to_all(table, 'tab', split_axis=0, concat_axis=0, tiled=True)]
    all_to_all x0 -> x1, waiting for transfers between devices: none -> 5.5 us  [per_device(): lax.all_to_all(grads, 'tab', split_axis=0, concat_axis=0, tiled=True)]
    all_to_all x0 -> x1, starting transfers between devices: none -> 5.08 us  [per_device(): lax.all_to_all(grads, 'tab', split_axis=0, concat_axis=0, tiled=True)]
    pallas_call x1, Pallas kernels: 8.28 us -> 3.26 us  [filter_part(): pl.pallas_call(functools.partial(filter_kernel, packed, scales), in_specs...]
    ppermute x3, waiting for transfers between devices: 0.01 us -> 4.59 us  [swap(): lax.ppermute(value[i * step:(i + 1) * step], 'col', [(c, c ^ bit) for c i...]
    pallas_call x2 -> x3, Pallas kernels: 6.95 us -> 9.82 us  [the longest x1 5.9 us: embed_part(): pl.pallas_call(functools.partial(embed_kernel, scale), in_specs=[whole()]...]
    unnamed x15 -> x11, local copies, waits for them, and re-layouts: 3.79 us -> 1.54 us
    all_to_all x1, waiting for transfers between devices: 5.07 us -> 2.87 us  [per_device(): lax.all_to_all(sent, 'tab', split_axis=0, concat_axis=0, tiled=True)]
  transfers between devices with their start and end apart: 5 -> 6, of which waited for: 2 -> 6; matrix products, arithmetic and copies ran while one was open for 4% -> 7% of each run, Pallas kernels for 8% -> 7%
where the time goes in v2:
time: 57.4 us; the launch traced here: 57 us
  starting transfers between devices  18.1 us (32%)
  Pallas kernels  13.9 us (24%)
  waiting for transfers between devices  13.9 us (24%)
  blocking collectives  5.18 us (9%)
  local copies, waits for them, and re-layouts  4.44 us (8%)
  between operations  0.77 us (1%)
    all_to_all x1, starting transfers between devices, per_device(): lax.all_to_all(sent, 'tab', split_axis=0, concat_axis=0, tiled=True)  7.29 us
    pallas_call x1, Pallas kernels, embed_part(): pl.pallas_call(functools.partial(embed_kernel, scale), in_specs=[whole()]...  5.9 us
    all_to_all x1, waiting for transfers between devices, per_device(): lax.all_to_all(grads, 'tab', split_axis=0, concat_axis=0, tiled=True)  5.5 us
    all_gather x1, blocking collectives, per_device(): cot = lax.all_gather(cotangent, 'col', axis=1, tiled=True)  5.18 us
    all_to_all x1, starting transfers between devices, per_device(): lax.all_to_all(grads, 'tab', split_axis=0, concat_axis=0, tiled=True)  5.08 us
    ppermute x3, waiting for transfers between devices, swap(): lax.ppermute(value[i * step:(i + 1) * step], 'col', [(c, c ^ bit) for c i...  4.59 us
    all_to_all x1, starting transfers between devices, per_device(): lax.all_to_all(table, 'tab', split_axis=0, concat_axis=0, tiled=True)  3.62 us
    pallas_call x1, Pallas kernels, filter_part(): pl.pallas_call(functools.partial(filter_kernel, packed, scales), in_specs...  3.26 us
  transfers between devices with their start and end apart: 6, of which 6 were waited for; matrix products, arithmetic and copies ran while one was open for 7% of the time, Pallas kernels for 7%

profile of v2, /device:TPU:0, one launch (start us, length us, event | category | flops | bytes accessed | tf_op | source)
XLA Modules:
  0.0 57.0 jit_solution(13404190490300508967)
XLA Ops:
  0.6 3.2 %pool_bags.1 = bf16[8,192,128]{2,1,0:T(8,128)(2,1)} custom-call(bf16[16,12,4,1024]{3,2,1,0:T(4,128)(2,1)} %bitcast.17, s32[16,1024]{1,0:T(8,128)} %lengths_hbm.1), custom_call_target="tpu_custom_call" | custom-call | tf_op jit(solution)/shard_map/pool_bags/pallas_call | solution.py:75
  3.9 7.3 %all-to-all-start = ((bf16[8,192,128]{2,1,0:T(8,128)(2,1)}), bf16[8,192,128]{2,1,0:T(8,128)(2,1)S(1)}, u32[]{:S(2)}, u32[]{:S(2)}) async-start(bf16[8,192,128]{2,1,0:T(8,128)(2,1)} %pool_bags.1), calls=%async_computation | async-start | bytes 786432 | tf_op jit(solution)/shard_map/all_to_all | solution.py:407
  11.2 0.0 copy-start.4
  11.2 0.0 copy-start
  11.2 0.4 reshape.35
  11.6 0.0 copy-start.1
  11.6 1.3 %copy.20 = f32[32,64,64]{1,2,0:T(8,128)} copy(f32[32,64,64]{2,1,0:T(8,128)S(1)} %reshape.35) | data formatting | bytes 1048576 | tf_op jit(solution)/shard_map/convert_element_type | solution.py:409
  13.0 5.2 %all_gather.3 = bf16[64,128]{0,1:T(8,128)(2,1)S(1)} all-gather(bf16[64,32]{0,1:T(8,128)(2,1)S(1)} %copy-done.4), channel_id=1, replica_groups=mesh['tab'=8,'col'=4] {'col'}, dimensions={1}, use_global_device_ids=true | all-gather | bytes 20480 | tf_op jit(solution)/shard_map/all_gather | solution.py:408
  18.1 0.1 copy.24.cot_ref
  18.2 0.2 reshape.33.second_ref
  18.5 0.1 copy.22.slot_ref
  18.6 0.4 fusion.1.inner_ref
  19.0 0.8 %copy-done.2 = f32[32,64,64]{1,2,0:T(8,128)S(1)} copy-done((f32[32,64,64]{1,2,0:T(8,128)S(1)}, f32[32,64,64]{1,2,0:T(8,128)}, u32[]{:S(2)}) %copy-start.2) | copy-done | bytes 524312
  19.8 0.2 fusion.2
  20.0 2.9 %all-to-all-done.received_ref = bf16[8,192,128]{2,1,0:T(8,128)(2,1)S(1)} async-done(((bf16[8,192,128]{2,1,0:T(8,128)(2,1)}), bf16[8,192,128]{2,1,0:T(8,128)(2,1)S(1)}, u32[]{:S(2)}, u32[]{:S(2)}) %all-to-all-start) | async-done | bytes 393248 | tf_op jit(solution)/shard_map/all_to_all | solution.py:407
  22.9 5.9 %embed_part.1 = (bf16[8,192,128]{2,1,0:T(8,128)(2,1)}, bf16[64,1536]{1,0:T(8,128)(2,1)S(1)}, bf16[32,1536]{1,0:T(8,128)(2,1)S(1)}, bf16[32,1536]{1,0:T(8,128)(2,1)S(1)}, f32[32,128]{1,0:T(8,128)S(1)}) custom-call(bf16[8,192,128]{2,1,0:T(8,128)(2,1)S(1)} %all-to-all-done.received_ref, s32[64,1]{1,0:T(8,128)S(1)} %copy.22.slot_ref, s32[1,64]{1,0:T(1,128)S(1)} %bitcast.16, ...), custom_call_target="tpu_custom_call" | custom-call | flops 1610612736 | bytes 786432 | tf_op jit(solution)/shard_map/embed_part/pallas_call | solution.py:190
  28.8 3.6 %all-to-all-start.1 = ((bf16[8,192,128]{2,1,0:T(8,128)(2,1)}), bf16[8,192,128]{2,1,0:T(8,128)(2,1)S(1)}, u32[]{:S(2)}, u32[]{:S(2)}) async-start(bf16[8,192,128]{2,1,0:T(8,128)(2,1)} %get-tuple-element.21), calls=%async_computation.1 | async-start | bytes 786432 | tf_op jit(solution)/shard_map/all_to_all | solution.py:439
  32.4 3.3 %filter_part.1 = (bf16[800,128]{1,0:T(8,128)(2,1)S(1)}, bf16[800,128]{1,0:T(8,128)(2,1)S(1)}) custom-call(s32[1]{0:T(128)} %bitcast.place_ref, bf16[64,128]{1,0:T(8,128)(2,1)S(1)} %copy.24.cot_ref, bf16[32,2048]{1,0:T(8,128)(2,1)S(1)} %copy-done, bf16[64,1536]{1,0:T(8,128)(2,1)S(1)} %get-tuple-element.15.embed_ref, ...), custom_call_target="tpu_custom_call" | custom-call | flops 1207959552 | bytes 786432 | tf_op jit(solution)/shard_map/filter_part/pallas_call | solution.py:331
  35.7 0.1 collective-permute-start
  35.8 0.5 collective-permute-start.1
  36.3 0.8 %collective-permute-done = bf16[400,128]{1,0:T(8,128)(2,1)S(1)} collective-permute-done((bf16[400,128]{1,0:T(8,128)(2,1)S(1)}, bf16[400,128]{1,0:T(8,128)(2,1)S(1)}, u32[]{:S(2)}, u32[]{:S(2)}) %collective-permute-start) | collective-permute-done | bytes 102432 | tf_op jit(solution)/shard_map/ppermute | solution.py:445
  37.1 0.2 collective-permute-done.1
  37.3 1.6 %collective-permute-start.2 = (bf16[400,128]{1,0:T(8,128)(2,1)S(1)}, bf16[400,128]{1,0:T(8,128)(2,1)S(1)}, u32[]{:S(2)}, u32[]{:S(2)}) collective-permute-start(bf16[400,128]{1,0:T(8,128)(2,1)S(1)} %slice.62), channel_id=1, source_target_pairs={{0,2},{1,3},{2,0},{3,1},{4,6},{5,7},{6,4},{7,5},{8,10},{9,11},{10,... | collective-permute-start | bytes 307208 | tf_op jit(solution)/shard_map/ppermute | solution.py:445
  38.8 3.6 %collective-permute-done.2 = bf16[400,128]{1,0:T(8,128)(2,1)S(1)} collective-permute-done((bf16[400,128]{1,0:T(8,128)(2,1)S(1)}, bf16[400,128]{1,0:T(8,128)(2,1)S(1)}, u32[]{:S(2)}, u32[]{:S(2)}) %collective-permute-start.2) | collective-permute-done | bytes 102432 | tf_op jit(solution)/shard_map/ppermute | solution.py:445
  42.5 0.7 %slice.63 = bf16[384,128]{1,0:T(8,128)(2,1)} slice(f32[400,128]{1,0:T(8,128)S(1)} %slice_add_fusion), slice={[0:384], [0:128]} | slice | bytes 196608 | tf_op jit(solution)/shard_map/slice | solution.py:455
  43.2 0.9 %all-to-all-done.1.table_ref = bf16[8,192,128]{2,1,0:T(8,128)(2,1)S(1)} async-done(((bf16[8,192,128]{2,1,0:T(8,128)(2,1)}), bf16[8,192,128]{2,1,0:T(8,128)(2,1)S(1)}, u32[]{:S(2)}, u32[]{:S(2)}) %all-to-all-start.1) | async-done | bytes 393248 | tf_op jit(solution)/shard_map/all_to_all | solution.py:439
  44.1 5.1 %all-to-all-start.2 = ((bf16[8,48,128]{2,1,0:T(8,128)(2,1)}), bf16[8,48,128]{2,1,0:T(8,128)(2,1)S(1)}, u32[]{:S(2)}, u32[]{:S(2)}) async-start(bf16[8,48,128]{2,1,0:T(8,128)(2,1)} %bitcast.7), calls=%async_computation.2 | async-start | bytes 196608 | tf_op jit(solution)/shard_map/all_to_all | solution.py:457
  49.2 0.1 fusion.6
  49.2 0.7 %copy.25 = f32[64,32]{0,1:T(8,128)} copy(f32[64,32]{1,0:T(8,128)S(1)} %pad_maximum_fusion) | data formatting | bytes 16384
  49.9 0.9 %owner_part.1 = bf16[12,16,1024]{2,1,0:T(8,128)(2,1)} custom-call(bf16[8,192,128]{2,1,0:T(8,128)(2,1)S(1)} %all-to-all-done.1.table_ref), custom_call_target="tpu_custom_call" | custom-call | tf_op jit(solution)/shard_map/owner_part/pallas_call | solution.py:360
  50.8 5.5 %all-to-all-done.2.refs_0_ = bf16[8,48,128]{2,1,0:T(8,128)(2,1)S(1)} async-done(((bf16[8,48,128]{2,1,0:T(8,128)(2,1)}), bf16[8,48,128]{2,1,0:T(8,128)(2,1)S(1)}, u32[]{:S(2)}, u32[]{:S(2)}) %all-to-all-start.2) | async-done | bytes 98336 | tf_op jit(solution)/shard_map/all_to_all | solution.py:457
  56.3 0.7 %grad_part.1 = (f32[32,128]{1,0:T(8,128)}, f32[32,64]{1,0:T(8,128)}) custom-call(bf16[8,48,128]{2,1,0:T(8,128)(2,1)S(1)} %all-to-all-done.2.refs_0_), custom_call_target="tpu_custom_call" | custom-call | tf_op jit(solution)/shard_map/grad_part/pallas_call | solution.py:383
  (11 shorter events, 0.1 us)
Async XLA Ops:
  0.6 10.5 %copy-start.3 = (bf16[32,4096]{1,0:T(8,128)(2,1)S(1)}, bf16[32,4096]{1,0:T(8,128)(2,1)}, u32[]{:S(2)}) copy-start(bf16[32,4096]{1,0:T(8,128)(2,1)} %param.9) | copy-start | bytes 786436
  3.9 19.0 %all-to-all-start = ((bf16[8,192,128]{2,1,0:T(8,128)(2,1)}), bf16[8,192,128]{2,1,0:T(8,128)(2,1)S(1)}, u32[]{:S(2)}, u32[]{:S(2)}) async-start(bf16[8,192,128]{2,1,0:T(8,128)(2,1)} %pool_bags.1), calls=%async_computation | async-start | bytes 786432 | tf_op jit(solution)/shard_map/all_to_all | solution.py:407
  11.2 1.8 %copy-start.4 = (bf16[64,32]{0,1:T(8,128)(2,1)S(1)}, bf16[64,32]{0,1:T(8,128)(2,1)}, u32[]{:S(2)}) copy-start(bf16[64,32]{0,1:T(8,128)(2,1)} %param.11) | copy-start | bytes 12292
  11.2 7.0 %copy-start = (bf16[32,2048]{1,0:T(8,128)(2,1)S(1)}, bf16[32,2048]{1,0:T(8,128)(2,1)}, u32[]{:S(2)}) copy-start(bf16[32,2048]{1,0:T(8,128)(2,1)} %second_ref.1) | copy-start | bytes 393220
  11.6 6.9 %copy-start.1 = (s32[64]{0:T(128)S(1)}, s32[64]{0:T(128)}, u32[]{:S(2)}) copy-start(s32[64]{0:T(128)} %param.8) | copy-start | bytes 772
  18.6 1.2 %copy-start.2 = (f32[32,64,64]{1,2,0:T(8,128)S(1)}, f32[32,64,64]{1,2,0:T(8,128)}, u32[]{:S(2)}) copy-start(f32[32,64,64]{1,2,0:T(8,128)} %copy.20) | copy-start | bytes 1572868
  28.8 15.3 %all-to-all-start.1 = ((bf16[8,192,128]{2,1,0:T(8,128)(2,1)}), bf16[8,192,128]{2,1,0:T(8,128)(2,1)S(1)}, u32[]{:S(2)}, u32[]{:S(2)}) async-start(bf16[8,192,128]{2,1,0:T(8,128)(2,1)} %get-tuple-element.21), calls=%async_computation.1 | async-start | bytes 786432 | tf_op jit(solution)/shard_map/all_to_all | solution.py:439
  35.7 1.4 %collective-permute-start = (bf16[400,128]{1,0:T(8,128)(2,1)S(1)}, bf16[400,128]{1,0:T(8,128)(2,1)S(1)}, u32[]{:S(2)}, u32[]{:S(2)}) collective-permute-start(bf16[400,128]{1,0:T(8,128)(2,1)S(1)} %get-tuple-element.42), channel_id=1, source_target_pairs={{0,1},{1,0},{2,3},{3,2},{4,5},{5,4},{6,7},{7,6},{8,9},{9,8},{10,11... | collective-permute-start | bytes 307208 | tf_op jit(solution)/shard_map/ppermute | solution.py:445
  35.8 1.4 %collective-permute-start.1 = (bf16[400,128]{1,0:T(8,128)(2,1)S(1)}, bf16[400,128]{1,0:T(8,128)(2,1)S(1)}, u32[]{:S(2)}, u32[]{:S(2)}) collective-permute-start(bf16[400,128]{1,0:T(8,128)(2,1)S(1)} %get-tuple-element.43), channel_id=1, source_target_pairs={{0,1},{1,0},{2,3},{3,2},{4,5},{5,4},{6,7},{7,6},{8,9},{9,8},{10,11... | collective-permute-start | bytes 307208 | tf_op jit(solution)/shard_map/ppermute | solution.py:445
  37.3 5.2 %collective-permute-start.2 = (bf16[400,128]{1,0:T(8,128)(2,1)S(1)}, bf16[400,128]{1,0:T(8,128)(2,1)S(1)}, u32[]{:S(2)}, u32[]{:S(2)}) collective-permute-start(bf16[400,128]{1,0:T(8,128)(2,1)S(1)} %slice.62), channel_id=1, source_target_pairs={{0,2},{1,3},{2,0},{3,1},{4,6},{5,7},{6,4},{7,5},{8,10},{9,11},{10,... | collective-permute-start | bytes 307208 | tf_op jit(solution)/shard_map/ppermute | solution.py:445
  44.1 12.2 %all-to-all-start.2 = ((bf16[8,48,128]{2,1,0:T(8,128)(2,1)}), bf16[8,48,128]{2,1,0:T(8,128)(2,1)S(1)}, u32[]{:S(2)}, u32[]{:S(2)}) async-start(bf16[8,48,128]{2,1,0:T(8,128)(2,1)} %bitcast.7), calls=%async_computation.2 | async-start | bytes 196608 | tf_op jit(solution)/shard_map/all_to_all | solution.py:457

commit v3 on v2

v3 whole, which is shorter than its diff:
```python
import functools

import jax
import jax.numpy as jnp
from jax import lax
from jax.experimental import pallas as pl
from jax.experimental.pallas import tpu as pltpu
from jax.sharding import PartitionSpec as P

BF16 = jnp.bfloat16
F32 = jnp.float32
VMEM_BYTES = 48 * 1024 * 1024
MATMUL_ROWS = 1024
FILTER_ROWS = 512


def params():
    return pltpu.CompilerParams(vmem_limit_bytes=VMEM_BYTES)


def cost(flops, moved):
    return pl.CostEstimate(flops=flops, bytes_accessed=moved, transcendentals=0)


def whole():
    return pl.BlockSpec(memory_space=pltpu.VMEM)


def dot(left, right):
    return jnp.dot(left, right, preferred_element_type=F32)


def dot_lanes(left, right):
    return lax.dot_general(left, right, (((1,), (1,)), ((), ())), preferred_element_type=F32)


def tab_orders(tabs):
    first = [t // 2 if t % 2 == 0 else tabs - 1 - t // 2 for t in range(tabs)]
    return first, first[tabs // 2 :] + first[: tabs // 2]


def position(orders, place_ref, t):
    near, far = orders[0].index(t), orders[1].index(t)
    if near == far:
        return near
    return jnp.where(lax.rem(place_ref[0], 2) == 0, near, far)


def exchange(value, orders, cols):
    if orders[0] == orders[1]:
        return lax.all_to_all(value, "tab", split_axis=0, concat_axis=0, tiled=True)
    groups = [[t * cols + c for t in orders[c % 2]] for c in range(cols)]
    return lax.all_to_all(
        value, ("tab", "col"), split_axis=0, concat_axis=0, tiled=True, axis_index_groups=groups
    )


def pool_kernel(steps, orders, place_ref, bag_hbm, lengths_hbm, out_ref, bag_ref, lengths_ref, rows_ref, sems):
    slots, width, items, _ = bag_hbm.shape
    chunks, _, lanes = out_ref.shape
    per_step = chunks // steps
    counts = pltpu.make_async_copy(lengths_hbm, lengths_ref, sems.at[steps])
    counts.start()
    copies = []
    for k in range(steps):
        part = pl.ds(k * per_step * lanes, per_step * lanes)
        copy = pltpu.make_async_copy(
            bag_hbm.at[:, :, :, part], bag_ref.at[:, :, :, part], sems.at[k]
        )
        copy.start()
        copies.append(copy)
    counts.wait()
    for chunk in range(chunks):
        if chunk % per_step == 0:
            copies[chunk // per_step].wait()
        here = pl.ds(chunk * lanes, lanes)
        buffer = chunk % 2
        block = position(orders, place_ref, chunk)
        for slot in range(slots):
            at = slot * width * items
            rows_ref[buffer, at : at + width * items, :] = (
                bag_ref[slot, :, :, here].astype(F32).reshape(width * items, lanes)
            )
        count = lengths_ref[:, here]
        for d in range(width):
            total = jnp.zeros((slots, lanes), F32)
            for item in range(items):
                value = rows_ref[buffer, pl.ds(d * items + item, slots, stride=width * items), :]
                total = total + jnp.where(count > item, value, 0.0)
            out_ref[block, d * slots : (d + 1) * slots, :] = total.astype(BF16)


def pool(orders, place, bag_items, lengths):
    tab_count = len(orders[0])
    bag = bag_items.transpose(0, 2, 1, 3)
    slots, width, items, samples = bag.shape
    lanes = samples // tab_count
    steps = min(4, tab_count)
    return pl.pallas_call(
        functools.partial(pool_kernel, steps, orders),
        in_specs=[pl.BlockSpec(memory_space=pltpu.SMEM)] + [pl.BlockSpec(memory_space=pltpu.HBM)] * 2,
        out_specs=whole(),
        out_shape=jax.ShapeDtypeStruct((tab_count, width * slots, lanes), BF16),
        scratch_shapes=[
            pltpu.VMEM(bag.shape, BF16),
            pltpu.VMEM(lengths.shape, jnp.int32),
            pltpu.VMEM((2, width * slots * items, lanes), F32),
            pltpu.SemaphoreType.DMA((steps + 1,)),
        ],
        compiler_params=pltpu.CompilerParams(vmem_limit_bytes=62 * 1024 * 1024),
        name="pool_bags",
    )(place, bag, lengths)


def forward_kernel(
    packed, orders, scales, count,
    place_ref, received_ref, slot_ref, sym_ref, second_ref, filter_ref,
    *refs,
):
    cot_refs, refs = refs[:count], refs[count:]
    outs = refs[:2]
    (
        embed_ref, hidden_ref, lower_ref, upper_ref,
        cot_ref, up_ref, x_ref, hid_ref, maps_ref, sum_ref, inner_ref, grad_ref, buf_ref, pair_ref,
        pack_ref,
    ) = refs[2:]
    fields = slot_ref.shape[0]
    maps, positions = hidden_ref.shape
    lanes = upper_ref.shape[1]
    width = positions // lanes
    tabs = received_ref.shape[0]
    slots = received_ref.shape[1] // width
    pair = 2 * lanes
    scale = scales[0]
    for r in range(count):
        cot_ref[r] = cot_refs[r][...].astype(F32)
    share = lanes // count
    for c in range(count):
        block = cot_ref[jnp.bitwise_xor(place_ref[0], c)] if count > 1 else cot_ref[0]
        up_ref[:, c * share : (c + 1) * share] = (block * scale).astype(BF16).astype(F32)
    up_ref[:, lanes:] = up_ref[:, :lanes]
    upper = up_ref[maps:, :lanes].astype(BF16)
    upper_ref[...] = upper
    onehot = (
        lax.broadcasted_iota(jnp.int32, (fields, tabs * slots), 1) == slot_ref[...]
    ).astype(BF16)
    order = [position(orders, place_ref, t) if tabs > 1 else 0 for t in range(tabs)]
    for d in range(width):
        parts = [received_ref[order[t], d * slots : (d + 1) * slots, :] for t in range(tabs)]
        x = dot(onehot, parts[0] if len(parts) == 1 else jnp.concatenate(parts, axis=0))
        x_ref[:, d * lanes : (d + 1) * lanes] = x
        embed_ref[:, d * lanes : (d + 1) * lanes] = x.astype(BF16)
    sum_ref[...] = jnp.zeros_like(sum_ref)
    rows = MATMUL_ROWS
    jobs = []
    for p in range(width // 2):
        jobs += [("z", p, start) for start in range(0, maps * maps, rows)]
        jobs += [("y", p, start) for start in range(0, maps * fields, rows)]

    def issue(number):
        kind, p, start = jobs[number]
        source = second_ref if kind == "z" else sym_ref
        x = embed_ref[:, p * pair : (p + 1) * pair]
        buf_ref[number % 2] = dot(source[start : start + rows, :], x)

    state = {}

    def consume(number):
        kind, p, start = jobs[number]
        here = pl.ds(p * pair, pair)
        b = p % 2
        y_ref = buf_ref.at[number % 2]
        if kind == "z":
            lower = up_ref[:maps, :] if start == 0 else state["lower"]
            for k in range(rows // maps):
                o = start // maps + k
                lower = lower + up_ref[maps + o : maps + o + 1, :] * y_ref[k * maps : (k + 1) * maps, :]
            state["lower"] = lower
            if start + rows == maps * maps:
                lower_ref[:, here] = lower.astype(BF16)
            return
        x_float = x_ref[:, here]
        for k in range(rows // fields):
            o = start // fields + k
            mine = y_ref[k * fields : (k + 1) * fields, :]
            maps_ref[b, o : o + 1, :] = 0.5 * jnp.sum(mine * x_float, axis=0, keepdims=True)
        if start + rows < maps * fields:
            return
        first_maps = maps_ref[b]
        sum_ref[...] += first_maps
        hidden = first_maps.astype(BF16)
        hidden_ref[:, here] = hidden
        hid_ref[:, here] = hidden.astype(F32)

    issue(0)
    for number in range(len(jobs)):
        if number + 1 < len(jobs):
            issue(number + 1)
        consume(number)

    rows = FILTER_ROWS
    steps = [
        (p, start) for p in range(width // 2) for start in range(0, fields * maps, rows)
    ]

    def products(number):
        p, start = steps[number]
        here = pl.ds(p * pair, pair)
        lower = lower_ref[:, here].astype(F32)
        for k in range(rows // maps):
            f = start // maps + k
            pair_ref[number % 2, k * maps : (k + 1) * maps, :] = (
                x_ref[f : f + 1, here] * lower
            ).astype(BF16)

    def sums(number):
        p, start = steps[number]
        part = dot_lanes(pair_ref[number % 2], embed_ref[:, p * pair : (p + 1) * pair])
        if p == 0:
            grad_ref[start : start + rows, :] = part
        else:
            grad_ref[start : start + rows, :] += part

    def inner(first, size):
        totals = [jnp.zeros((fields, lanes), F32)] * size
        for d in range(width):
            here = pl.ds(d * lanes, lanes)
            x = x_ref[:, here]
            for k in range(size):
                totals[k] = totals[k] + hid_ref[first + k : first + k + 1, here] * x
        for k in range(size):
            at = (first + k) * fields
            inner_ref[at : at + fields, :] = totals[k].astype(BF16)

    group, first = 4, 0
    products(0)
    for number in range(len(steps)):
        if number + 1 < len(steps):
            products(number + 1)
        if number % 3 == 0 and first < maps:
            inner(first, group)
            first += group
        sums(number)
    for first in range(first, maps, group):
        inner(first, group)
    base = fields * maps
    second = dot_lanes(upper, inner_ref[...])
    for h in range(maps):
        grad_ref[base + h * maps : base + (h + 1) * maps, :] = second[:, h * fields : (h + 1) * fields]
    two = dot(filter_ref[...], inner_ref[...])
    pooled = jnp.concatenate([sum_ref[:, :lanes] + sum_ref[:, lanes:], two], axis=0) * scale
    if not packed:
        outs[0][...] = grad_ref[...] * scales[1]
        outs[1][...] = pooled
        return
    cols, tabs = packed
    tall = 2 * maps * share // lanes
    for c in range(cols):
        pack_ref[c] = jnp.concatenate(
            [
                pooled[g * tall : (g + 1) * tall, c * share : (c + 1) * share]
                for g in range(lanes // share)
            ],
            axis=1,
        )
    own_col = place_ref[0]
    block = maps + maps // 2
    rows = tabs * block + tall
    for r in range(cols):
        c = jnp.bitwise_xor(own_col, r)
        out, base = outs[r % 2], r // 2 * rows
        for q in range(tabs):
            near, far = orders[0][q], orders[1][q]
            k = jnp.where(lax.rem(c, 2) == 0, near, far) * cols + c
            first = grad_ref[pl.ds(pl.multiple_of(k * 2 * maps, 2 * maps), 2 * maps), :]
            first = jnp.concatenate([first[:maps], first[maps:]], axis=1)
            second = grad_ref[pl.ds(pl.multiple_of((2 * tabs * cols + k) * maps, maps), maps), :]
            second = jnp.concatenate([second[: maps // 2], second[maps // 2 :]], axis=1)
            out[base + q * block : base + (q + 1) * block, :] = (
                jnp.concatenate([first, second], axis=0) * scales[1]
            ).astype(BF16)
        out[base + tabs * block : base + rows, :] = pack_ref[c].astype(BF16)


def forward_part(packed, orders, scales, place, received, slot, cots, sym, second, filter_two, width):
    fields = slot.shape[0]
    maps = cots[0].shape[0] // 2
    lanes = cots[0].shape[1] * len(cots)
    positions = width * lanes
    pair = 2 * lanes
    grads = (fields + maps) * maps
    if packed:
        cols, tabs = packed
        tall = 2 * maps // cols
        piece = (cols // 2 * (tabs * (maps + maps // 2) + tall), lanes)
        outs = [jax.ShapeDtypeStruct(piece, BF16)] * 2
        pack = pltpu.VMEM((cols, tall, lanes), F32)
    else:
        outs = [
            jax.ShapeDtypeStruct((grads, fields), F32),
            jax.ShapeDtypeStruct((2 * maps, lanes), F32),
        ]
        pack = pltpu.VMEM((1, 8, lanes), F32)
    return pl.pallas_call(
        functools.partial(forward_kernel, packed, orders, scales, len(cots)),
        in_specs=[pl.BlockSpec(memory_space=pltpu.SMEM)] + [whole()] * (5 + len(cots)),
        out_specs=[whole()] * 6,
        out_shape=outs
        + [
            jax.ShapeDtypeStruct((fields, positions), BF16),
            jax.ShapeDtypeStruct((maps, positions), BF16),
            jax.ShapeDtypeStruct((maps, positions), BF16),
            jax.ShapeDtypeStruct((maps, lanes), BF16),
        ],
        scratch_shapes=[
            pltpu.VMEM((len(cots),) + cots[0].shape, F32),
            pltpu.VMEM((2 * maps, pair), F32),
            pltpu.VMEM((fields, positions), F32),
            pltpu.VMEM((maps, positions), F32),
            pltpu.VMEM((2, maps, pair), F32),
            pltpu.VMEM((maps, pair), F32),
            pltpu.VMEM((maps * fields, lanes), BF16),
            pltpu.VMEM((grads, fields), F32),
            pltpu.VMEM((2, MATMUL_ROWS, pair), F32),
            pltpu.VMEM((2, FILTER_ROWS, pair), BF16),
            pack,
        ],
        compiler_params=params(),
        cost_estimate=cost(8 * maps * fields * fields * positions, 4 * received.size),
        name="forward_part",
    )(place, received, slot.reshape(fields, 1), sym, second, filter_two, *cots)


def embed_kernel(
    orders, slots,
    place_ref, slot_ref, sym_ref, turned_ref, upper_ref, embed_ref, hidden_ref, lower_ref,
    table_ref, inner_ref, low_ref, hid_ref, buf_ref,
):
    fields, positions = embed_ref.shape
    maps, lanes = upper_ref.shape
    width = positions // lanes
    tabs = table_ref.shape[0]
    pair = 2 * lanes
    spread = (
        lax.broadcasted_iota(jnp.int32, (tabs * slots, fields), 0) == slot_ref[...]
    ).astype(BF16)
    order = [position(orders, place_ref, t) if tabs > 1 else 0 for t in range(tabs)]
    inner_ref[...] = dot(turned_ref[...], upper_ref[...])
    low_ref[...] = lower_ref[...].astype(F32)
    hid_ref[...] = hidden_ref[...].astype(F32)
    rows = MATMUL_ROWS
    jobs = [(p, start) for p in range(width // 2) for start in range(0, maps * fields, rows)]

    def issue(number):
        p, start = jobs[number]
        x = embed_ref[:, p * pair : (p + 1) * pair]
        buf_ref[number % 2] = dot(sym_ref[start : start + rows, :], x)

    state = {}

    def consume(number):
        p, start = jobs[number]
        here = pl.ds(p * pair, pair)
        y_ref = buf_ref.at[number % 2]
        gradient = jnp.zeros((fields, pair), F32) if start == 0 else state["gradient"]
        for k in range(rows // fields):
            o = start // fields + k
            gradient = gradient + low_ref[o : o + 1, here] * y_ref[k * fields : (k + 1) * fields, :]
        state["gradient"] = gradient
        if start + rows < maps * fields:
            return
        sides = [gradient[:, :lanes], gradient[:, lanes:]]
        for h in range(maps):
            inner = inner_ref[h * fields : (h + 1) * fields, :]
            for k in range(2):
                at = pl.ds(p * pair + k * lanes, lanes)
                sides[k] = sides[k] + hid_ref[h : h + 1, at] * inner
        for k in range(2):
            table = dot(spread, sides[k].astype(BF16)).astype(BF16)
            at = (2 * p + k) * slots
            for t in range(tabs):
                table_ref[order[t], at : at + slots, :] = table[t * slots : (t + 1) * slots, :]

    issue(0)
    for number in range(len(jobs)):
        if number + 1 < len(jobs):
            issue(number + 1)
        consume(number)


def embed_part(orders, slots, place, slot, sym, turned, upper, embed, hidden, lower, shape):
    fields, positions = embed.shape
    maps, lanes = upper.shape
    pair = 2 * lanes
    return pl.pallas_call(
        functools.partial(embed_kernel, orders, slots),
        in_specs=[pl.BlockSpec(memory_space=pltpu.SMEM)] + [whole()] * 7,
        out_specs=whole(),
        out_shape=jax.ShapeDtypeStruct(shape, BF16),
        scratch_shapes=[
            pltpu.VMEM((maps * fields, lanes), F32),
            pltpu.VMEM((maps, positions), F32),
            pltpu.VMEM((maps, positions), F32),
            pltpu.VMEM((2, MATMUL_ROWS, pair), F32),
        ],
        compiler_params=params(),
        cost_estimate=cost(4 * maps * fields * fields * positions, 8 * embed.size),
        name="embed_part",
    )(place, slot.reshape(1, fields), sym, turned, upper, embed, hidden, lower)


def owner_kernel(orders, place_ref, table_ref, out_ref, *grads):
    width, slots, _ = out_ref.shape
    tabs, _, lanes = table_ref.shape
    for t in range(tabs):
        block = position(orders, place_ref, t)
        for d in range(width):
            out_ref[d, :, t * lanes : (t + 1) * lanes] = table_ref[
                block, d * slots : (d + 1) * slots, :
            ]
    if not grads:
        return
    one_ref, two_ref = grads
    maps = one_ref.shape[0]
    total = table_ref[0, width * slots :, :].astype(F32)
    for t in range(1, tabs):
        total = total + table_ref[t, width * slots :, :].astype(F32)
    one_ref[...] = total[:maps]
    two_ref[: maps // 2, :] = total[maps:, : lanes // 2]
    two_ref[maps // 2 :, :] = total[maps:, lanes // 2 :]


def owner_part(orders, place, table, slots, width, maps):
    tabs, rows, lanes = table.shape
    shapes = [jax.ShapeDtypeStruct((width, slots, tabs * lanes), BF16)]
    if rows > width * slots:
        shapes += [
            jax.ShapeDtypeStruct((maps, lanes), F32),
            jax.ShapeDtypeStruct((maps, lanes // 2), F32),
        ]
    results = pl.pallas_call(
        functools.partial(owner_kernel, orders),
        in_specs=[pl.BlockSpec(memory_space=pltpu.SMEM), whole()],
        out_specs=[whole()] * len(shapes),
        out_shape=shapes,
        compiler_params=params(),
        name="owner_part",
    )(place, table)
    return results[0].transpose(1, 0, 2), *results[1:]


def per_device(bag_items, lengths, field_slot, filter_one, filter_two, cotangent):
    slots, _, width, samples = bag_items.shape
    tabs = lax.axis_size("tab")
    cols = lax.axis_size("col")
    devices = tabs * cols
    lanes = samples // tabs
    maps = filter_one.shape[0]
    fields = field_slot.shape[0]
    scales = ((width * cols) ** -0.5, samples**-0.5)
    place = lax.axis_index("col").astype(jnp.int32).reshape(1)
    small = slots % 16 != 0
    packable = (
        fields * fields == devices * lanes
        and fields * 2 == lanes
        and maps == devices
        and cols & (cols - 1) == 0
        and cols > 1
        and tabs % 2 == 0
        and not small
    )
    orders = tab_orders(tabs) if packable else (list(range(tabs)),) * 2
    sent = pool(orders, place, bag_items, lengths)
    sent, cotangent = lax.optimization_barrier((sent, cotangent))
    received = exchange(sent, orders, cols)
    if cols & (cols - 1):
        cots = [lax.all_gather(cotangent, "col", axis=1, tiled=True)]
    else:
        cots = [cotangent] + [
            lax.ppermute(cotangent, "col", [(c, c ^ r) for c in range(cols)])
            for r in range(1, cols)
        ]
    square = filter_one.reshape(maps, fields, fields).astype(F32)
    sym = (square + square.transpose(0, 2, 1)).astype(BF16).reshape(maps * fields, fields)
    second = filter_two.reshape(maps * maps, fields)
    if small:
        received = received.reshape(tabs, width, slots, lanes).transpose(1, 0, 2, 3)
        received = received.reshape(1, width * tabs * slots, lanes)
    keep, away, embed, hidden, lower, upper = forward_part(
        (cols, tabs) if packable else None,
        orders, scales, place, received, field_slot, cots, sym, second, filter_two, width,
    )
    chunks, rows, _ = received.shape
    block = maps + maps // 2 if packable else 0
    table = embed_part(
        orders, rows // width, place, field_slot, sym, filter_two.T, upper, embed, hidden, lower,
        (chunks, rows + block, lanes),
    )
    if packable:
        total = keep.astype(F32)
        bit = 1
        while True:
            total = total + lax.ppermute(
                away, "col", [(c, c ^ bit) for c in range(cols)]
            ).astype(F32)
            bit *= 2
            if bit == cols:
                break
            half = total.shape[0] // 2
            total, away = total[:half], total[half:].astype(BF16)
        grads = total[: tabs * block].astype(BF16).reshape(tabs, block, lanes)
        table = lax.dynamic_update_slice(table, grads, (0, rows, 0))
        returned = exchange(table, orders, cols)
        pooled_grad, grad_one, grad_two = owner_part(orders, place, returned, slots, width, maps)
        share = lanes // cols
        packs = total[tabs * block :]
        pooled = jnp.concatenate(
            [packs[:, g * share : (g + 1) * share] for g in range(lanes // share)], axis=0
        )
        return (pooled, grad_one, grad_two, pooled_grad)
    if small:
        table = table.reshape(width, tabs, slots, lanes).transpose(1, 0, 2, 3)
        table = table.reshape(tabs, width * slots, lanes)
    returned = exchange(table, orders, cols)
    (pooled_grad,) = owner_part(orders, place, returned, slots, width, maps)
    pooled = lax.psum_scatter(away, "col", scatter_dimension=1, tiled=True)
    shaped = keep.reshape(fields + maps, maps, fields).transpose(1, 0, 2)
    grad_one = shaped[:, :fields].reshape(maps, tabs, cols, -1)
    grad_two = shaped[:, fields:].reshape(maps, tabs, cols, -1)
    grad_one = lax.psum_scatter(grad_one, "col", scatter_dimension=2, tiled=True)
    grad_two = lax.psum_scatter(grad_two, "col", scatter_dimension=2, tiled=True)
    grad_one = lax.psum_scatter(grad_one, "tab", scatter_dimension=1, tiled=True)
    grad_two = lax.psum_scatter(grad_two, "tab", scatter_dimension=1, tiled=True)
    return (pooled, grad_one.reshape(maps, -1), grad_two.reshape(maps, -1), pooled_grad)


def solution(mesh):
    in_specs = (P("tab", None, "col", None), P("tab", None), P(), P(), P(), P(None, ("tab", "col")))
    out_specs = (
        P(None, ("tab", "col")),
        P(None, ("tab", "col")),
        P(None, ("tab", "col")),
        P("tab", "col", None),
    )
    return jax.shard_map(
        per_device, mesh=mesh, in_specs=in_specs, out_specs=out_specs, check_vma=False
    )
```

time: 57.4 us -> 53.9 us (0.939)
  waiting for transfers between devices: 13.9 us -> 20.3 us
  blocking collectives: 5.18 us -> 0 us
  starting transfers between devices: 18.1 us -> 14.3 us
  local copies, waits for them, and re-layouts: 4.44 us -> 3.54 us
    all_to_all x3 -> x2, waiting for transfers between devices: 9.28 us -> 18 us  [exchange(): lax.all_to_all(value, ('tab', 'col'), split_axis=0, concat_axis=0, tiled=...]
    all_to_all x3 -> x2, starting transfers between devices: 16 us -> 10.8 us  [exchange(): lax.all_to_all(value, ('tab', 'col'), split_axis=0, concat_axis=0, tiled=...]
    all_gather x1 -> x0, blocking collectives: 5.18 us -> none  [per_device(): cot = lax.all_gather(cotangent, 'col', axis=1, tiled=True)]
    ppermute x3 -> x5, waiting for transfers between devices: 4.59 us -> 2.36 us  [the longest x2 1.44 us: per_device(): lax.ppermute(away, 'col', [(c, c ^ bit) for c in range(cols)]).astype(F32)]
    ppermute x3 -> x5, starting transfers between devices: 2.14 us -> 3.55 us  [the longest x3 1.93 us: per_device(): lax.ppermute(cotangent, 'col', [(c, c ^ r) for c in range(cols)])]
    convert_element_type x2, local copies, waits for them, and re-layouts: 1.73 us -> 0.74 us  [per_device(): square = filter_one.reshape(maps, fields, fields).astype(F32)]
    dynamic_update_slice x0 -> x1, local copies, waits for them, and re-layouts: none -> 0.68 us  [per_device(): table = lax.dynamic_update_slice(table, grads, (0, rows, 0))]
    slice x1, local copies, waits for them, and re-layouts: 0.66 us -> 0.01 us  [per_device(): grads = total[:tabs * block].astype(BF16).reshape(tabs, block, lanes)]
  transfers between devices with their start and end apart: 6 -> 7, of which waited for: 6 -> 4; matrix products, arithmetic and copies ran while one was open for 7% -> 4% of each run, Pallas kernels for 7% -> 9%
where the time goes in v3:
time: 53.9 us; the launch traced here: 53.6 us
  waiting for transfers between devices  20.3 us (38%)
  Pallas kernels  14.3 us (27%)
  starting transfers between devices  14.3 us (27%)
  local copies, waits for them, and re-layouts  3.54 us (7%)
  between operations  0.79 us (1%)
    all_to_all x2, waiting for transfers between devices, exchange(): lax.all_to_all(value, ('tab', 'col'), split_axis=0, concat_axis=0, tiled=...  18 us
    all_to_all x2, starting transfers between devices, exchange(): lax.all_to_all(value, ('tab', 'col'), split_axis=0, concat_axis=0, tiled=...  10.8 us
    pallas_call x1, Pallas kernels, forward_part(): pl.pallas_call(functools.partial(forward_kernel, packed, orders, scales,...  5.63 us
    pallas_call x1, Pallas kernels, embed_part(): pl.pallas_call(functools.partial(embed_kernel, orders, slots), in_specs=[...  4.63 us
    pallas_call x1, Pallas kernels, pool(): pl.pallas_call(functools.partial(pool_kernel, steps, orders), in_specs=[p...  3.22 us
    ppermute x3, starting transfers between devices, per_device(): lax.ppermute(cotangent, 'col', [(c, c ^ r) for c in range(cols)])  1.93 us
    ppermute x2, starting transfers between devices, per_device(): lax.ppermute(away, 'col', [(c, c ^ bit) for c in range(cols)]).astype(F32)  1.63 us
    unnamed x10, local copies, waits for them, and re-layouts  1.6 us
  transfers between devices with their start and end apart: 7, of which 4 were waited for; matrix products, arithmetic and copies ran while one was open for 4% of the time, Pallas kernels for 9%

profile of v3, /device:TPU:0, one launch (start us, length us, event | category | flops | bytes accessed | tf_op | source)
XLA Modules:
  0.0 53.6 jit_solution(8760000075795009057)
XLA Ops:
  0.7 3.2 %pool_bags.1 = bf16[8,192,128]{2,1,0:T(8,128)(2,1)} custom-call(s32[1]{0:T(128)} %bitcast.place_ref, bf16[16,12,4,1024]{3,2,1,0:T(4,128)(2,1)} %bitcast.17, s32[16,1024]{1,0:T(8,128)} %lengths_hbm.1), custom_call_target="tpu_custom_call" | custom-call | tf_op jit(solution)/shard_map/pool_bags/pallas_call | solution.py:99
  3.9 7.3 %all-to-all-start = ((bf16[8,192,128]{2,1,0:T(8,128)(2,1)}), bf16[8,192,128]{2,1,0:T(8,128)(2,1)S(1)}, u32[]{:S(2)}, u32[]{:S(2)}) async-start(bf16[8,192,128]{2,1,0:T(8,128)(2,1)} %pool_bags.1), calls=%async_computation | async-start | bytes 786432 | tf_op jit(solution)/shard_map/all_to_all | solution.py:53
  11.2 0.1 copy.23.refs_0_
  11.3 0.1 collective-permute-start
  11.4 1.6 %collective-permute-start.1 = (bf16[64,32]{1,0:T(8,128)(2,1)S(1)}, bf16[64,32]{1,0:T(8,128)(2,1)S(1)}, u32[]{:S(2)}, u32[]{:S(2)}) collective-permute-start(bf16[64,32]{1,0:T(8,128)(2,1)S(1)} %copy.23.refs_0_), channel_id=1, source_target_pairs={{0,2},{1,3},{2,0},{3,1},{4,6},{5,7},{6,4},{7,5},{8,10},{9,11},{10,... | collective-permute-start | bytes 12296 | tf_op jit(solution)/shard_map/ppermute | solution.py:480
  12.9 0.3 collective-permute-start.2
  13.2 0.4 reshape.35
  13.6 0.3 copy.18
  14.0 0.0 copy-start.1
  14.0 0.0 copy-start
  14.0 0.2 fusion
  14.2 0.5 copy-done.1
  14.6 0.1 copy.22.slot_ref
  14.7 0.2 copy-done
  14.9 0.2 reshape.32.second_ref
  15.1 0.0 collective-permute-done.refs_1_
  15.2 0.0 collective-permute-done.1.refs_2_
  15.2 0.9 %collective-permute-done.2.refs_3_ = bf16[64,32]{1,0:T(8,128)(2,1)S(1)} collective-permute-done((bf16[64,32]{1,0:T(8,128)(2,1)S(1)}, bf16[64,32]{1,0:T(8,128)(2,1)S(1)}, u32[]{:S(2)}, u32[]{:S(2)}) %collective-permute-start.2) | collective-permute-done | bytes 4128 | tf_op jit(solution)/shard_map/ppermute | solution.py:480
  16.1 5.9 %all-to-all-done.received_ref = bf16[8,192,128]{2,1,0:T(8,128)(2,1)S(1)} async-done(((bf16[8,192,128]{2,1,0:T(8,128)(2,1)}), bf16[8,192,128]{2,1,0:T(8,128)(2,1)S(1)}, u32[]{:S(2)}, u32[]{:S(2)}) %all-to-all-start) | async-done | bytes 393248 | tf_op jit(solution)/shard_map/all_to_all | solution.py:53
  22.0 5.6 %forward_part.1 = (bf16[800,128]{1,0:T(8,128)(2,1)S(1)}, bf16[800,128]{1,0:T(8,128)(2,1)S(1)}, bf16[64,1536]{1,0:T(8,128)(2,1)S(1)}, bf16[32,1536]{1,0:T(8,128)(...) custom-call(s32[1]{0:T(128)} %bitcast.place_ref, ...), custom_call_target="tpu_custom_call" | custom-call | flops 1610612736 | bytes 786432 | tf_op jit(solution)/shard_map/forward_part/pallas_call | solution.py:304
  27.6 0.1 collective-permute-start.3
  27.7 1.4 %collective-permute-done.3 = bf16[800,128]{1,0:T(8,128)(2,1)S(1)} collective-permute-done((bf16[800,128]{1,0:T(8,128)(2,1)S(1)}, bf16[800,128]{1,0:T(8,128)(2,1)S(1)}, u32[]{:S(2)}, u32[]{:S(2)}) %collective-permute-start.3) | collective-permute-done | bytes 204832 | tf_op jit(solution)/shard_map/ppermute | solution.py:503
  29.2 1.6 %collective-permute-start.4 = (bf16[400,128]{1,0:T(8,128)(2,1)S(1)}, bf16[400,128]{1,0:T(8,128)(2,1)S(1)}, u32[]{:S(2)}, u32[]{:S(2)}) collective-permute-start(bf16[400,128]{1,0:T(8,128)(2,1)S(1)} %slice.45), channel_id=1, source_target_pairs={{0,2},{1,3},{2,0},{3,1},{4,6},{5,7},{6,4},{7,5},{8,10},{9,11},{10,... | collective-permute-start | bytes 307208 | tf_op jit(solution)/shard_map/ppermute | solution.py:503
  30.7 0.3 copy.24
  31.0 4.6 %embed_part.1 = bf16[8,240,128]{2,1,0:T(8,128)(2,1)} custom-call(s32[1]{0:T(128)} %bitcast.place_ref, s32[1,64]{1,0:T(1,128)S(1)} %bitcast.16, bf16[2048,64]{1,0:T(8,128)(2,1)S(1)} %bitcast.13, bf16[2048,32]{1,0:T(8,128)(2,1)S(1)} %bitcast.14, bf16[32,128]{1,0:T(8,128)(2,1)S(1)} %get-tuple-element.19.upper_ref, ...), custom_call_target="tpu_custom_call" | custom-call | flops 805306368 | bytes 786432 | tf_op jit(solution)/shard_map/embed_part/pallas_call | solution.py:395
  35.6 0.0 collective-permute-done.4
  35.7 0.7 %constant_dynamic-update-slice_fusion = bf16[8,240,128]{2,1,0:T(8,128)(2,1)} fusion(bf16[8,240,128]{2,1,0:T(8,128)(2,1)} %embed_part.1, bf16[8,48,128]{2,1,0:T(8,128)(2,1)S(1)} %bitcast.18), kind=kLoop, calls=%fused_computation.7 | loop fusion | bytes 196608 | tf_op jit(solution)/shard_map/dynamic_update_slice | solution.py:512
  36.4 3.5 %all-to-all-start.1 = ((bf16[8,240,128]{2,1,0:T(8,128)(2,1)}), bf16[8,240,128]{2,1,0:T(8,128)(2,1)S(1)}, u32[]{:S(2)}, u32[]{:S(2)}) async-start(bf16[8,240,128]{2,1,0:T(8,128)(2,1)} %constant_dynamic-update-slice_fusion), calls=%async_computation.1 | async-start | bytes 983040 | tf_op jit(solution)/shard_map/all_to_all | solution.py:53
  39.9 0.1 fusion.1
  39.9 0.7 %copy.25 = f32[64,32]{0,1:T(8,128)} copy(f32[64,32]{1,0:T(8,128)S(1)} %pad_maximum_fusion) | data formatting | bytes 16384
  40.6 12.1 %all-to-all-done.1.table_ref = bf16[8,240,128]{2,1,0:T(8,128)(2,1)S(1)} async-done(((bf16[8,240,128]{2,1,0:T(8,128)(2,1)}), bf16[8,240,128]{2,1,0:T(8,128)(2,1)S(1)}, u32[]{:S(2)}, u32[]{:S(2)}) %all-to-all-start.1) | async-done | bytes 491552 | tf_op jit(solution)/shard_map/all_to_all | solution.py:53
  52.7 0.9 %owner_part.1 = (bf16[12,16,1024]{2,1,0:T(8,128)(2,1)}, f32[32,128]{1,0:T(8,128)}, f32[32,64]{1,0:T(8,128)}) custom-call(s32[1]{0:T(128)} %bitcast.place_ref, bf16[8,240,128]{2,1,0:T(8,128)(2,1)S(1)} %all-to-all-done.1.table_ref), custom_call_target="tpu_custom_call" | custom-call | tf_op jit(solution)/shard_map/owner_part/pallas_call | solution.py:441
  (9 shorter events, 0.1 us)
Async XLA Ops:
  0.6 10.6 %copy-start.3 = (bf16[64,32]{0,1:T(8,128)(2,1)S(1)}, bf16[64,32]{0,1:T(8,128)(2,1)}, u32[]{:S(2)}) copy-start(bf16[64,32]{0,1:T(8,128)(2,1)} %param.11) | copy-start | bytes 12292
  0.6 12.6 %copy-start.2 = (bf16[32,4096]{1,0:T(8,128)(2,1)S(1)}, bf16[32,4096]{1,0:T(8,128)(2,1)}, u32[]{:S(2)}) copy-start(bf16[32,4096]{1,0:T(8,128)(2,1)} %param.9) | copy-start | bytes 786436
  3.9 18.1 %all-to-all-start = ((bf16[8,192,128]{2,1,0:T(8,128)(2,1)}), bf16[8,192,128]{2,1,0:T(8,128)(2,1)S(1)}, u32[]{:S(2)}, u32[]{:S(2)}) async-start(bf16[8,192,128]{2,1,0:T(8,128)(2,1)} %pool_bags.1), calls=%async_computation | async-start | bytes 786432 | tf_op jit(solution)/shard_map/all_to_all | solution.py:53
  11.3 3.9 %collective-permute-start = (bf16[64,32]{1,0:T(8,128)(2,1)S(1)}, bf16[64,32]{1,0:T(8,128)(2,1)S(1)}, u32[]{:S(2)}, u32[]{:S(2)}) collective-permute-start(bf16[64,32]{1,0:T(8,128)(2,1)S(1)} %copy.23.refs_0_), channel_id=1, source_target_pairs={{0,1},{1,0},{2,3},{3,2},{4,5},{5,4},{6,7},{7,6},{8,9},{9,8},{10,11... | collective-permute-start | bytes 12296 | tf_op jit(solution)/shard_map/ppermute | solution.py:480
  11.4 3.8 %collective-permute-start.1 = (bf16[64,32]{1,0:T(8,128)(2,1)S(1)}, bf16[64,32]{1,0:T(8,128)(2,1)S(1)}, u32[]{:S(2)}, u32[]{:S(2)}) collective-permute-start(bf16[64,32]{1,0:T(8,128)(2,1)S(1)} %copy.23.refs_0_), channel_id=1, source_target_pairs={{0,2},{1,3},{2,0},{3,1},{4,6},{5,7},{6,4},{7,5},{8,10},{9,11},{10,... | collective-permute-start | bytes 12296 | tf_op jit(solution)/shard_map/ppermute | solution.py:480
  12.9 3.2 %collective-permute-start.2 = (bf16[64,32]{1,0:T(8,128)(2,1)S(1)}, bf16[64,32]{1,0:T(8,128)(2,1)S(1)}, u32[]{:S(2)}, u32[]{:S(2)}) collective-permute-start(bf16[64,32]{1,0:T(8,128)(2,1)S(1)} %copy.23.refs_0_), channel_id=1, source_target_pairs={{0,3},{1,2},{2,1},{3,0},{4,7},{5,6},{6,5},{7,4},{8,11},{9,10},{10,... | collective-permute-start | bytes 12296 | tf_op jit(solution)/shard_map/ppermute | solution.py:480
  14.0 0.7 %copy-start.1 = (s32[64]{0:T(128)S(1)}, s32[64]{0:T(128)}, u32[]{:S(2)}) copy-start(s32[64]{0:T(128)} %param.8) | copy-start | bytes 772
  14.0 0.9 %copy-start = (bf16[32,2048]{1,0:T(8,128)(2,1)S(1)}, bf16[32,2048]{1,0:T(8,128)(2,1)}, u32[]{:S(2)}) copy-start(bf16[32,2048]{1,0:T(8,128)(2,1)} %filter_ref.1) | copy-start | bytes 393220
  27.6 1.5 %collective-permute-start.3 = (bf16[800,128]{1,0:T(8,128)(2,1)S(1)}, bf16[800,128]{1,0:T(8,128)(2,1)S(1)}, u32[]{:S(2)}, u32[]{:S(2)}) collective-permute-start(bf16[800,128]{1,0:T(8,128)(2,1)S(1)} %get-tuple-element.18), channel_id=1, source_target_pairs={{0,1},{1,0},{2,3},{3,2},{4,5},{5,4},{6,7},{7,6},{8,9},{9,8},{10,11... | collective-permute-start | bytes 614408 | tf_op jit(solution)/shard_map/ppermute | solution.py:503
  29.2 6.5 %collective-permute-start.4 = (bf16[400,128]{1,0:T(8,128)(2,1)S(1)}, bf16[400,128]{1,0:T(8,128)(2,1)S(1)}, u32[]{:S(2)}, u32[]{:S(2)}) collective-permute-start(bf16[400,128]{1,0:T(8,128)(2,1)S(1)} %slice.45), channel_id=1, source_target_pairs={{0,2},{1,3},{2,0},{3,1},{4,6},{5,7},{6,4},{7,5},{8,10},{9,11},{10,... | collective-permute-start | bytes 307208 | tf_op jit(solution)/shard_map/ppermute | solution.py:503
  36.4 16.3 %all-to-all-start.1 = ((bf16[8,240,128]{2,1,0:T(8,128)(2,1)}), bf16[8,240,128]{2,1,0:T(8,128)(2,1)S(1)}, u32[]{:S(2)}, u32[]{:S(2)}) async-start(bf16[8,240,128]{2,1,0:T(8,128)(2,1)} %constant_dynamic-update-slice_fusion), calls=%async_computation.1 | async-start | bytes 983040 | tf_op jit(solution)/shard_map/all_to_all | solution.py:53

commit v4 on v3

--- a/solution.py
+++ b/solution.py
@@ -12,6 +12,7 @@
 VMEM_BYTES = 48 * 1024 * 1024
 MATMUL_ROWS = 1024
 FILTER_ROWS = 512
+INNER_GROUPS = 2
 
 
 def params():
@@ -35,7 +36,7 @@
 
 
 def tab_orders(tabs):
-    first = [t // 2 if t % 2 == 0 else tabs - 1 - t // 2 for t in range(tabs)]
+    first = [tabs - 1 - i // 2 if i % 2 == 0 else i // 2 for i in range(tabs)]
     return first, first[tabs // 2 :] + first[: tabs // 2]
 
 
@@ -198,28 +199,32 @@
             issue(number + 1)
         consume(number)
 
-    rows = FILTER_ROWS
-    steps = [
-        (p, start) for p in range(width // 2) for start in range(0, fields * maps, rows)
-    ]
-
-    def products(number):
-        p, start = steps[number]
-        here = pl.ds(p * pair, pair)
-        lower = lower_ref[:, here].astype(F32)
-        for k in range(rows // maps):
-            f = start // maps + k
-            pair_ref[number % 2, k * maps : (k + 1) * maps, :] = (
-                x_ref[f : f + 1, here] * lower
+    some = FILTER_ROWS // maps
+    own_col = place_ref[0]
+
+    def products(first):
+        lower = lower_ref[...].astype(F32)
+        for k in range(some):
+            f = first + k
+            pair_ref[first // some % 2, k * maps : (k + 1) * maps, :] = (
+                x_ref[f : f + 1, :] * lower
             ).astype(BF16)
 
-    def sums(number):
-        p, start = steps[number]
-        part = dot_lanes(pair_ref[number % 2], embed_ref[:, p * pair : (p + 1) * pair])
-        if p == 0:
-            grad_ref[start : start + rows, :] = part
-        else:
-            grad_ref[start : start + rows, :] += part
+    def keep_rows(k, rows, at):
+        cols, tabs = packed
+        c = k % cols
+        at += orders[c % 2].index(k // cols) * (maps + maps // 2)
+        half = rows.shape[0] // 2
+        both = jnp.concatenate([rows[:half], rows[half:]], axis=1) * scales[1]
+        pack_ref[jnp.bitwise_xor(own_col, c), at : at + half, :] = both.astype(BF16)
+
+    def sums(first):
+        part = dot_lanes(pair_ref[first // some % 2], embed_ref[...])
+        if not packed:
+            grad_ref[first * maps : (first + some) * maps, :] = part
+            return
+        for k in range(some // 2):
+            keep_rows(first // 2 + k, part[2 * k * maps : 2 * (k + 1) * maps], 0)
 
     def inner(first, size):
         totals = [jnp.zeros((fields, lanes), F32)] * size
@@ -232,54 +237,45 @@
             at = (first + k) * fields
             inner_ref[at : at + fields, :] = totals[k].astype(BF16)
 
-    group, first = 4, 0
+    group, done = 4, 0
     products(0)
-    for number in range(len(steps)):
-        if number + 1 < len(steps):
-            products(number + 1)
-        if number % 3 == 0 and first < maps:
-            inner(first, group)
-            first += group
-        sums(number)
-    for first in range(first, maps, group):
-        inner(first, group)
-    base = fields * maps
+    for first in range(0, fields, some):
+        if first + some < fields:
+            products(first + some)
+        for _ in range(INNER_GROUPS):
+            if done < maps:
+                inner(done, group)
+                done += group
+        sums(first)
+    for done in range(done, maps, group):
+        inner(done, group)
     second = dot_lanes(upper, inner_ref[...])
-    for h in range(maps):
-        grad_ref[base + h * maps : base + (h + 1) * maps, :] = second[:, h * fields : (h + 1) * fields]
     two = dot(filter_ref[...], inner_ref[...])
     pooled = jnp.concatenate([sum_ref[:, :lanes] + sum_ref[:, lanes:], two], axis=0) * scale
     if not packed:
+        base = fields * maps
+        for h in range(maps):
+            grad_ref[base + h * maps : base + (h + 1) * maps, :] = second[
+                :, h * fields : (h + 1) * fields
+            ]
         outs[0][...] = grad_ref[...] * scales[1]
         outs[1][...] = pooled
         return
     cols, tabs = packed
+    for h in range(maps):
+        keep_rows(h, second[:, h * fields : (h + 1) * fields], maps)
     tall = 2 * maps * share // lanes
+    last = tabs * (maps + maps // 2)
     for c in range(cols):
-        pack_ref[c] = jnp.concatenate(
+        pack_ref[jnp.bitwise_xor(own_col, c), last : last + tall, :] = jnp.concatenate(
             [
                 pooled[g * tall : (g + 1) * tall, c * share : (c + 1) * share]
                 for g in range(lanes // share)
             ],
             axis=1,
-        )
-    own_col = place_ref[0]
-    block = maps + maps // 2
-    rows = tabs * block + tall
+        ).astype(BF16)
     for r in range(cols):
-        c = jnp.bitwise_xor(own_col, r)
-        out, base = outs[r % 2], r // 2 * rows
-        for q in range(tabs):
-            near, far = orders[0][q], orders[1][q]
-            k = jnp.where(lax.rem(c, 2) == 0, near, far) * cols + c
-            first = grad_ref[pl.ds(pl.multiple_of(k * 2 * maps, 2 * maps), 2 * maps), :]
-            first = jnp.concatenate([first[:maps], first[maps:]], axis=1)
-            second = grad_ref[pl.ds(pl.multiple_of((2 * tabs * cols + k) * maps, maps), maps), :]
-            second = jnp.concatenate([second[: maps // 2], second[maps // 2 :]], axis=1)
-            out[base + q * block : base + (q + 1) * block, :] = (
-                jnp.concatenate([first, second], axis=0) * scales[1]
-            ).astype(BF16)
-        out[base + tabs * block : base + rows, :] = pack_ref[c].astype(BF16)
+        outs[r % 2][r // 2 * (last + tall) : (r // 2 + 1) * (last + tall), :] = pack_ref[r]
 
 
 def forward_part(packed, orders, scales, place, received, slot, cots, sym, second, filter_two, width):
@@ -294,13 +290,13 @@
         tall = 2 * maps // cols
         piece = (cols // 2 * (tabs * (maps + maps // 2) + tall), lanes)
         outs = [jax.ShapeDtypeStruct(piece, BF16)] * 2
-        pack = pltpu.VMEM((cols, tall, lanes), F32)
+        pack = pltpu.VMEM((cols, tabs * (maps + maps // 2) + tall, lanes), BF16)
     else:
         outs = [
             jax.ShapeDtypeStruct((grads, fields), F32),
             jax.ShapeDtypeStruct((2 * maps, lanes), F32),
         ]
-        pack = pltpu.VMEM((1, 8, lanes), F32)
+        pack = pltpu.VMEM((1, 16, lanes), BF16)
     return pl.pallas_call(
         functools.partial(forward_kernel, packed, orders, scales, len(cots)),
         in_specs=[pl.BlockSpec(memory_space=pltpu.SMEM)] + [whole()] * (5 + len(cots)),
@@ -320,9 +316,9 @@
             pltpu.VMEM((2, maps, pair), F32),
             pltpu.VMEM((maps, pair), F32),
             pltpu.VMEM((maps * fields, lanes), BF16),
-            pltpu.VMEM((grads, fields), F32),
+            pltpu.VMEM((8 if packed else grads, fields), F32),
             pltpu.VMEM((2, MATMUL_ROWS, pair), F32),
-            pltpu.VMEM((2, FILTER_ROWS, pair), BF16),
+            pltpu.VMEM((2, FILTER_ROWS, positions), BF16),
             pack,
         ],
         compiler_params=params(),
@@ -331,23 +327,56 @@
     )(place, received, slot.reshape(fields, 1), sym, second, filter_two, *cots)
 
 
+def second_kernel(turned_ref, upper_ref, hidden_ref, out_ref, inner_ref, hid_ref):
+    fields, positions = out_ref.shape
+    maps, lanes = upper_ref.shape
+    inner_ref[...] = dot(turned_ref[...], upper_ref[...])
+    hid_ref[...] = hidden_ref[...].astype(F32)
+    size = 4
+    for first in range(0, positions, size * lanes):
+        totals = [jnp.zeros((fields, lanes), F32)] * size
+        for h in range(maps):
+            inner = inner_ref[h * fields : (h + 1) * fields, :]
+            for k in range(size):
+                at = first + k * lanes
+                totals[k] = totals[k] + hid_ref[h : h + 1, at : at + lanes] * inner
+        for k in range(size):
+            out_ref[:, first + k * lanes : first + (k + 1) * lanes] = totals[k]
+
+
+def second_part(turned, upper, hidden):
+    maps, positions = hidden.shape
+    fields = turned.shape[0] // maps
+    return pl.pallas_call(
+        second_kernel,
+        in_specs=[whole()] * 3,
+        out_specs=whole(),
+        out_shape=jax.ShapeDtypeStruct((fields, positions), F32),
+        scratch_shapes=[
+            pltpu.VMEM((maps * fields, upper.shape[1]), F32),
+            pltpu.VMEM((maps, positions), F32),
+        ],
+        compiler_params=params(),
+        cost_estimate=cost(2 * maps * fields * positions, 8 * fields * positions),
+        name="second_part",
+    )(turned, upper, hidden)
+
+
 def embed_kernel(
     orders, slots,
-    place_ref, slot_ref, sym_ref, turned_ref, upper_ref, embed_ref, hidden_ref, lower_ref,
-    table_ref, inner_ref, low_ref, hid_ref, buf_ref,
+    place_ref, slot_ref, sym_ref, embed_ref, lower_ref, second_ref,
+    table_ref, low_ref, buf_ref,
 ):
     fields, positions = embed_ref.shape
-    maps, lanes = upper_ref.shape
+    maps = lower_ref.shape[0]
+    tabs, _, lanes = table_ref.shape
     width = positions // lanes
-    tabs = table_ref.shape[0]
     pair = 2 * lanes
     spread = (
         lax.broadcasted_iota(jnp.int32, (tabs * slots, fields), 0) == slot_ref[...]
     ).astype(BF16)
     order = [position(orders, place_ref, t) if tabs > 1 else 0 for t in range(tabs)]
-    inner_ref[...] = dot(turned_ref[...], upper_ref[...])
     low_ref[...] = lower_ref[...].astype(F32)
-    hid_ref[...] = hidden_ref[...].astype(F32)
     rows = MATMUL_ROWS
     jobs = [(p, start) for p in range(width // 2) for start in range(0, maps * fields, rows)]
 
@@ -362,21 +391,16 @@
         p, start = jobs[number]
         here = pl.ds(p * pair, pair)
         y_ref = buf_ref.at[number % 2]
-        gradient = jnp.zeros((fields, pair), F32) if start == 0 else state["gradient"]
+        gradient = second_ref[:, here] if start == 0 else state["gradient"]
         for k in range(rows // fields):
             o = start // fields + k
             gradient = gradient + low_ref[o : o + 1, here] * y_ref[k * fields : (k + 1) * fields, :]
         state["gradient"] = gradient
         if start + rows < maps * fields:
             return
-        sides = [gradient[:, :lanes], gradient[:, lanes:]]
-        for h in range(maps):
-            inner = inner_ref[h * fields : (h + 1) * fields, :]
-            for k in range(2):
-                at = pl.ds(p * pair + k * lanes, lanes)
-                sides[k] = sides[k] + hid_ref[h : h + 1, at] * inner
+        gradient = gradient.astype(BF16)
         for k in range(2):
-            table = dot(spread, sides[k].astype(BF16)).astype(BF16)
+            table = dot(spread, gradient[:, k * lanes : (k + 1) * lanes]).astype(BF16)
             at = (2 * p + k) * slots
             for t in range(tabs):
                 table_ref[order[t], at : at + slots, :] = table[t * slots : (t + 1) * slots, :]
@@ -388,25 +412,23 @@
         consume(number)
 
 
-def embed_part(orders, slots, place, slot, sym, turned, upper, embed, hidden, lower, shape):
+def embed_part(orders, slots, place, slot, sym, embed, lower, second, shape):
     fields, positions = embed.shape
-    maps, lanes = upper.shape
-    pair = 2 * lanes
+    maps = lower.shape[0]
+    pair = 2 * shape[2]
     return pl.pallas_call(
         functools.partial(embed_kernel, orders, slots),
-        in_specs=[pl.BlockSpec(memory_space=pltpu.SMEM)] + [whole()] * 7,
+        in_specs=[pl.BlockSpec(memory_space=pltpu.SMEM)] + [whole()] * 5,
         out_specs=whole(),
         out_shape=jax.ShapeDtypeStruct(shape, BF16),
         scratch_shapes=[
-            pltpu.VMEM((maps * fields, lanes), F32),
-            pltpu.VMEM((maps, positions), F32),
             pltpu.VMEM((maps, positions), F32),
             pltpu.VMEM((2, MATMUL_ROWS, pair), F32),
         ],
         compiler_params=params(),
-        cost_estimate=cost(4 * maps * fields * fields * positions, 8 * embed.size),
+        cost_estimate=cost(200 * maps * fields * fields * positions, 8 * embed.size),
         name="embed_part",
-    )(place, slot.reshape(1, fields), sym, turned, upper, embed, hidden, lower)
+    )(place, slot.reshape(1, fields), sym, embed, lower, second)
 
 
 def owner_kernel(orders, place_ref, table_ref, out_ref, *grads):
@@ -493,8 +515,8 @@
     chunks, rows, _ = received.shape
     block = maps + maps // 2 if packable else 0
     table = embed_part(
-        orders, rows // width, place, field_slot, sym, filter_two.T, upper, embed, hidden, lower,
-        (chunks, rows + block, lanes),
+        orders, rows // width, place, field_slot, sym, embed, lower,
+        second_part(filter_two.T, upper, hidden), (chunks, rows, lanes),
     )
     if packable:
         total = keep.astype(F32)
@@ -509,7 +531,7 @@
             half = total.shape[0] // 2
             total, away = total[:half], total[half:].astype(BF16)
         grads = total[: tabs * block].astype(BF16).reshape(tabs, block, lanes)
-        table = lax.dynamic_update_slice(table, grads, (0, rows, 0))
+        table = jnp.concatenate([table, grads], axis=1)
         returned = exchange(table, orders, cols)
         pooled_grad, grad_one, grad_two = owner_part(orders, place, returned, slots, width, maps)
         share = lanes // cols

time: 53.9 us -> 51.3 us (0.952)
  waiting for transfers between devices: 20.3 us -> 13.3 us
  starting transfers between devices: 14.3 us -> 19.4 us
  other arithmetic: 0.24 us -> 1.06 us
  Pallas kernels: 14.3 us -> 13.5 us
  local copies, waits for them, and re-layouts: 3.54 us -> 2.86 us
    all_to_all x2, waiting for transfers between devices: 18 us -> 11.4 us  [exchange(): lax.all_to_all(value, ('tab', 'col'), split_axis=0, concat_axis=0, tiled=...]
    all_to_all x2, starting transfers between devices: 10.8 us -> 15.9 us  [exchange(): lax.all_to_all(value, ('tab', 'col'), split_axis=0, concat_axis=0, tiled=...]
    pallas_call x1, Pallas kernels: 4.63 us -> 2.82 us  [embed_part(): pl.pallas_call(functools.partial(embed_kernel, orders, slots), in_specs=[...]
    pallas_call x0 -> x1, Pallas kernels: none -> 1.35 us  [second_part(): pl.pallas_call(second_kernel, in_specs=[whole()] * 3, out_specs=whole(),...]
    concatenate x0 -> x1, other arithmetic: none -> 0.81 us  [per_device(): table = jnp.concatenate([table, grads], axis=1)]
    dynamic_update_slice x1 -> x0, local copies, waits for them, and re-layouts: 0.68 us -> none  [per_device(): table = lax.dynamic_update_slice(table, grads, (0, rows, 0))]
  transfers between devices with their start and end apart: 7 -> 7, of which waited for: 4 -> 4; matrix products, arithmetic and copies ran while one was open for 4% -> 5% of each run, Pallas kernels for 9% -> 8%
where the time goes in v4:
time: 51.3 us; the launch traced here: 51 us
  starting transfers between devices  19.4 us (38%)
  Pallas kernels  13.5 us (26%)
  waiting for transfers between devices  13.3 us (26%)
  local copies, waits for them, and re-layouts  2.86 us (6%)
  other arithmetic  1.06 us (2%)
  between operations  0.81 us (2%)
    all_to_all x2, starting transfers between devices, exchange(): lax.all_to_all(value, ('tab', 'col'), split_axis=0, concat_axis=0, tiled=...  15.9 us
    all_to_all x2, waiting for transfers between devices, exchange(): lax.all_to_all(value, ('tab', 'col'), split_axis=0, concat_axis=0, tiled=...  11.4 us
    pallas_call x1, Pallas kernels, forward_part(): pl.pallas_call(functools.partial(forward_kernel, packed, orders, scales,...  5.24 us
    pallas_call x1, Pallas kernels, pool(): pl.pallas_call(functools.partial(pool_kernel, steps, orders), in_specs=[p...  3.22 us
    pallas_call x1, Pallas kernels, embed_part(): pl.pallas_call(functools.partial(embed_kernel, orders, slots), in_specs=[...  2.82 us
    ppermute x3, starting transfers between devices, per_device(): lax.ppermute(cotangent, 'col', [(c, c ^ r) for c in range(cols)])  1.93 us
    ppermute x2, starting transfers between devices, per_device(): lax.ppermute(away, 'col', [(c, c ^ bit) for c in range(cols)]).astype(F32)  1.62 us
    unnamed x10, local copies, waits for them, and re-layouts  1.6 us
  transfers between devices with their start and end apart: 7, of which 4 were waited for; matrix products, arithmetic and copies ran while one was open for 5% of the time, Pallas kernels for 8%

profile of v4, /device:TPU:0, one launch (start us, length us, event | category | flops | bytes accessed | tf_op | source)
XLA Modules:
  0.0 51.0 jit_solution(15329124357244010037)
XLA Ops:
  0.7 3.2 %pool_bags.1 = bf16[8,192,128]{2,1,0:T(8,128)(2,1)} custom-call(s32[1]{0:T(128)} %bitcast.place_ref, bf16[16,12,4,1024]{3,2,1,0:T(4,128)(2,1)} %bitcast.17, s32[16,1024]{1,0:T(8,128)} %lengths_hbm.1), custom_call_target="tpu_custom_call" | custom-call | tf_op jit(solution)/shard_map/pool_bags/pallas_call | solution.py:100
  3.9 9.4 %all-to-all-start = ((bf16[8,192,128]{2,1,0:T(8,128)(2,1)}), bf16[8,192,128]{2,1,0:T(8,128)(2,1)S(1)}, u32[]{:S(2)}, u32[]{:S(2)}) async-start(bf16[8,192,128]{2,1,0:T(8,128)(2,1)} %pool_bags.1), calls=%async_computation | async-start | bytes 786432 | tf_op jit(solution)/shard_map/all_to_all | solution.py:54
  13.3 0.1 copy.23.refs_0_
  13.4 0.1 collective-permute-start
  13.4 1.6 %collective-permute-start.1 = (bf16[64,32]{1,0:T(8,128)(2,1)S(1)}, bf16[64,32]{1,0:T(8,128)(2,1)S(1)}, u32[]{:S(2)}, u32[]{:S(2)}) collective-permute-start(bf16[64,32]{1,0:T(8,128)(2,1)S(1)} %copy.23.refs_0_), channel_id=1, source_target_pairs={{0,2},{1,3},{2,0},{3,1},{4,6},{5,7},{6,4},{7,5},{8,10},{9,11},{10,... | collective-permute-start | bytes 12296 | tf_op jit(solution)/shard_map/ppermute | solution.py:502
  15.0 0.3 collective-permute-start.2
  15.3 0.4 reshape.35
  15.7 0.3 copy.18
  16.1 0.0 copy-start.1
  16.1 0.0 copy-start
  16.1 0.2 fusion
  16.3 0.5 copy-done.1
  16.7 0.1 copy.22.slot_ref
  16.8 0.2 copy-done
  17.0 0.2 reshape.32.second_ref
  17.2 0.0 collective-permute-done.refs_1_
  17.2 0.0 collective-permute-done.1.refs_2_
  17.2 0.9 %collective-permute-done.2.refs_3_ = bf16[64,32]{1,0:T(8,128)(2,1)S(1)} collective-permute-done((bf16[64,32]{1,0:T(8,128)(2,1)S(1)}, bf16[64,32]{1,0:T(8,128)(2,1)S(1)}, u32[]{:S(2)}, u32[]{:S(2)}) %collective-permute-start.2) | collective-permute-done | bytes 4128 | tf_op jit(solution)/shard_map/ppermute | solution.py:502
  18.2 2.9 %all-to-all-done.received_ref = bf16[8,192,128]{2,1,0:T(8,128)(2,1)S(1)} async-done(((bf16[8,192,128]{2,1,0:T(8,128)(2,1)}), bf16[8,192,128]{2,1,0:T(8,128)(2,1)S(1)}, u32[]{:S(2)}, u32[]{:S(2)}) %all-to-all-start) | async-done | bytes 393248 | tf_op jit(solution)/shard_map/all_to_all | solution.py:54
  21.1 5.2 %forward_part.1 = (bf16[800,128]{1,0:T(8,128)(2,1)S(1)}, bf16[800,128]{1,0:T(8,128)(2,1)S(1)}, bf16[64,1536]{1,0:T(8,128)(2,1)S(1)}, bf16[32,1536]{1,0:T(8,128)(...) custom-call(s32[1]{0:T(128)} %bitcast.place_ref, ...), custom_call_target="tpu_custom_call" | custom-call | flops 1610612736 | bytes 786432 | tf_op jit(solution)/shard_map/forward_part/pallas_call | solution.py:300
  26.3 0.1 collective-permute-start.3
  26.4 0.3 copy.24
  26.7 1.3 %second_part.1.second_ref = f32[64,1536]{1,0:T(8,128)S(1)} custom-call(bf16[2048,32]{1,0:T(8,128)(2,1)S(1)} %bitcast.12, bf16[32,128]{1,0:T(8,128)(2,1)S(1)} %get-tuple-element.21.upper_ref, bf16[32,1536]{1,0:T(8,128)(2,1)S(1)} %get-tuple-element.22.hidden_ref), custom_call_target="tpu_custom_call" | custom-call | flops 6291456 | bytes 786432 | tf_op jit(solution)/shard_map/second_part/pallas_call | solution.py:350
  28.1 1.6 %collective-permute-start.4 = (bf16[400,128]{1,0:T(8,128)(2,1)S(1)}, bf16[400,128]{1,0:T(8,128)(2,1)S(1)}, u32[]{:S(2)}, u32[]{:S(2)}) collective-permute-start(bf16[400,128]{1,0:T(8,128)(2,1)S(1)} %slice.45), channel_id=1, source_target_pairs={{0,2},{1,3},{2,0},{3,1},{4,6},{5,7},{6,4},{7,5},{8,10},{9,11},{10,... | collective-permute-start | bytes 307208 | tf_op jit(solution)/shard_map/ppermute | solution.py:525
  29.7 2.8 %embed_part.1 = bf16[8,192,128]{2,1,0:T(8,128)(2,1)S(1)} custom-call(s32[1]{0:T(128)} %bitcast.place_ref, s32[1,64]{1,0:T(1,128)S(1)} %bitcast.16, bf16[2048,64]{1,0:T(8,128)(2,1)S(1)} %bitcast.14, bf16[64,1536]{1,0:T(8,128)(2,1)S(1)} %get-tuple-element.19.embed_ref, bf16[32,1536]{1,0:T(8,128)(2,1)S(1)} %get-tuple-element.20.lower_ref, ...), custom_call_target="tpu_custom_call" | custom-call | flops 40265318400 | bytes 786432 | tf_op jit(solution)/shard_map/embed_part/pallas_call | solution.py:419
  32.5 1.0 %collective-permute-done.4 = bf16[400,128]{1,0:T(8,128)(2,1)S(1)} collective-permute-done((bf16[400,128]{1,0:T(8,128)(2,1)S(1)}, bf16[400,128]{1,0:T(8,128)(2,1)S(1)}, u32[]{:S(2)}, u32[]{:S(2)}) %collective-permute-start.4) | collective-permute-done | bytes 102432 | tf_op jit(solution)/shard_map/ppermute | solution.py:525
  33.5 0.8 %pad_maximum_fusion = bf16[8,240,128]{2,1,0:T(8,128)(2,1)} fusion(bf16[8,48,128]{2,1,0:T(8,128)(2,1)S(1)} %bitcast.18, bf16[8,192,128]{2,1,0:T(8,128)(2,1)S(1)} %embed_part.1), kind=kLoop, calls=%fused_computation.2 | loop fusion | flops 983040 | bytes 983040 | tf_op jit(solution)/shard_map/concatenate | solution.py:534
  34.3 6.5 %all-to-all-start.1 = ((bf16[8,240,128]{2,1,0:T(8,128)(2,1)}), bf16[8,240,128]{2,1,0:T(8,128)(2,1)S(1)}, u32[]{:S(2)}, u32[]{:S(2)}) async-start(bf16[8,240,128]{2,1,0:T(8,128)(2,1)} %pad_maximum_fusion), calls=%async_computation.1 | async-start | bytes 983040 | tf_op jit(solution)/shard_map/all_to_all | solution.py:54
  40.8 0.1 fusion.1
  40.9 0.7 %copy.25 = f32[64,32]{0,1:T(8,128)} copy(f32[64,32]{1,0:T(8,128)S(1)} %pad_maximum_fusion.1) | data formatting | bytes 16384
  41.6 8.5 %all-to-all-done.1.table_ref = bf16[8,240,128]{2,1,0:T(8,128)(2,1)S(1)} async-done(((bf16[8,240,128]{2,1,0:T(8,128)(2,1)}), bf16[8,240,128]{2,1,0:T(8,128)(2,1)S(1)}, u32[]{:S(2)}, u32[]{:S(2)}) %all-to-all-start.1) | async-done | bytes 491552 | tf_op jit(solution)/shard_map/all_to_all | solution.py:54
  50.1 0.9 %owner_part.1 = (bf16[12,16,1024]{2,1,0:T(8,128)(2,1)}, f32[32,128]{1,0:T(8,128)}, f32[32,64]{1,0:T(8,128)}) custom-call(s32[1]{0:T(128)} %bitcast.place_ref, bf16[8,240,128]{2,1,0:T(8,128)(2,1)S(1)} %all-to-all-done.1.table_ref), custom_call_target="tpu_custom_call" | custom-call | tf_op jit(solution)/shard_map/owner_part/pallas_call | solution.py:463
  (10 shorter events, 0.1 us)
Async XLA Ops:
  0.6 12.6 %copy-start.3 = (bf16[64,32]{0,1:T(8,128)(2,1)S(1)}, bf16[64,32]{0,1:T(8,128)(2,1)}, u32[]{:S(2)}) copy-start(bf16[64,32]{0,1:T(8,128)(2,1)} %param.11) | copy-start | bytes 12292
  0.6 14.7 %copy-start.2 = (bf16[32,4096]{1,0:T(8,128)(2,1)S(1)}, bf16[32,4096]{1,0:T(8,128)(2,1)}, u32[]{:S(2)}) copy-start(bf16[32,4096]{1,0:T(8,128)(2,1)} %param.9) | copy-start | bytes 786436
  3.9 17.2 %all-to-all-start = ((bf16[8,192,128]{2,1,0:T(8,128)(2,1)}), bf16[8,192,128]{2,1,0:T(8,128)(2,1)S(1)}, u32[]{:S(2)}, u32[]{:S(2)}) async-start(bf16[8,192,128]{2,1,0:T(8,128)(2,1)} %pool_bags.1), calls=%async_computation | async-start | bytes 786432 | tf_op jit(solution)/shard_map/all_to_all | solution.py:54
  13.4 3.9 %collective-permute-start = (bf16[64,32]{1,0:T(8,128)(2,1)S(1)}, bf16[64,32]{1,0:T(8,128)(2,1)S(1)}, u32[]{:S(2)}, u32[]{:S(2)}) collective-permute-start(bf16[64,32]{1,0:T(8,128)(2,1)S(1)} %copy.23.refs_0_), channel_id=1, source_target_pairs={{0,1},{1,0},{2,3},{3,2},{4,5},{5,4},{6,7},{7,6},{8,9},{9,8},{10,11... | collective-permute-start | bytes 12296 | tf_op jit(solution)/shard_map/ppermute | solution.py:502
  13.4 3.8 %collective-permute-start.1 = (bf16[64,32]{1,0:T(8,128)(2,1)S(1)}, bf16[64,32]{1,0:T(8,128)(2,1)S(1)}, u32[]{:S(2)}, u32[]{:S(2)}) collective-permute-start(bf16[64,32]{1,0:T(8,128)(2,1)S(1)} %copy.23.refs_0_), channel_id=1, source_target_pairs={{0,2},{1,3},{2,0},{3,1},{4,6},{5,7},{6,4},{7,5},{8,10},{9,11},{10,... | collective-permute-start | bytes 12296 | tf_op jit(solution)/shard_map/ppermute | solution.py:502
  15.0 3.2 %collective-permute-start.2 = (bf16[64,32]{1,0:T(8,128)(2,1)S(1)}, bf16[64,32]{1,0:T(8,128)(2,1)S(1)}, u32[]{:S(2)}, u32[]{:S(2)}) collective-permute-start(bf16[64,32]{1,0:T(8,128)(2,1)S(1)} %copy.23.refs_0_), channel_id=1, source_target_pairs={{0,3},{1,2},{2,1},{3,0},{4,7},{5,6},{6,5},{7,4},{8,11},{9,10},{10,... | collective-permute-start | bytes 12296 | tf_op jit(solution)/shard_map/ppermute | solution.py:502
  16.1 0.7 %copy-start.1 = (s32[64]{0:T(128)S(1)}, s32[64]{0:T(128)}, u32[]{:S(2)}) copy-start(s32[64]{0:T(128)} %param.8) | copy-start | bytes 772
  16.1 0.9 %copy-start = (bf16[32,2048]{1,0:T(8,128)(2,1)S(1)}, bf16[32,2048]{1,0:T(8,128)(2,1)}, u32[]{:S(2)}) copy-start(bf16[32,2048]{1,0:T(8,128)(2,1)} %filter_ref.1) | copy-start | bytes 393220
  26.3 1.7 %collective-permute-start.3 = (bf16[800,128]{1,0:T(8,128)(2,1)S(1)}, bf16[800,128]{1,0:T(8,128)(2,1)S(1)}, u32[]{:S(2)}, u32[]{:S(2)}) collective-permute-start(bf16[800,128]{1,0:T(8,128)(2,1)S(1)} %get-tuple-element.18), channel_id=1, source_target_pairs={{0,1},{1,0},{2,3},{3,2},{4,5},{5,4},{6,7},{7,6},{8,9},{9,8},{10,11... | collective-permute-start | bytes 614408 | tf_op jit(solution)/shard_map/ppermute | solution.py:525
  28.1 5.3 %collective-permute-start.4 = (bf16[400,128]{1,0:T(8,128)(2,1)S(1)}, bf16[400,128]{1,0:T(8,128)(2,1)S(1)}, u32[]{:S(2)}, u32[]{:S(2)}) collective-permute-start(bf16[400,128]{1,0:T(8,128)(2,1)S(1)} %slice.45), channel_id=1, source_target_pairs={{0,2},{1,3},{2,0},{3,1},{4,6},{5,7},{6,4},{7,5},{8,10},{9,11},{10,... | collective-permute-start | bytes 307208 | tf_op jit(solution)/shard_map/ppermute | solution.py:525
  34.3 15.8 %all-to-all-start.1 = ((bf16[8,240,128]{2,1,0:T(8,128)(2,1)}), bf16[8,240,128]{2,1,0:T(8,128)(2,1)S(1)}, u32[]{:S(2)}, u32[]{:S(2)}) async-start(bf16[8,240,128]{2,1,0:T(8,128)(2,1)} %pad_maximum_fusion), calls=%async_computation.1 | async-start | bytes 983040 | tf_op jit(solution)/shard_map/all_to_all | solution.py:54

commit v5 on v4

--- a/solution.py
+++ b/solution.py
@@ -105,7 +105,7 @@
         scratch_shapes=[
             pltpu.VMEM(bag.shape, BF16),
             pltpu.VMEM(lengths.shape, jnp.int32),
-            pltpu.VMEM((2, width * slots * items, lanes), F32),
+            pltpu.VMEM((2, width * (slots + 1) * items, lanes), F32),
             pltpu.SemaphoreType.DMA((steps + 1,)),
         ],
         compiler_params=pltpu.CompilerParams(vmem_limit_bytes=62 * 1024 * 1024),

time: 51.3 us -> 51.3 us (level)
  no operation moved by 1% of the time
where the time goes in v5:
time: 51.3 us; the launch traced here: 51 us
  starting transfers between devices  19.4 us (38%)
  Pallas kernels  13.5 us (26%)
  waiting for transfers between devices  13.3 us (26%)
  local copies, waits for them, and re-layouts  2.86 us (6%)
  other arithmetic  1.06 us (2%)
  between operations  0.81 us (2%)
    all_to_all x2, starting transfers between devices, exchange(): lax.all_to_all(value, ('tab', 'col'), split_axis=0, concat_axis=0, tiled=...  15.9 us
    all_to_all x2, waiting for transfers between devices, exchange(): lax.all_to_all(value, ('tab', 'col'), split_axis=0, concat_axis=0, tiled=...  11.4 us
    pallas_call x1, Pallas kernels, forward_part(): pl.pallas_call(functools.partial(forward_kernel, packed, orders, scales,...  5.24 us
    pallas_call x1, Pallas kernels, pool(): pl.pallas_call(functools.partial(pool_kernel, steps, orders), in_specs=[p...  3.22 us
    pallas_call x1, Pallas kernels, embed_part(): pl.pallas_call(functools.partial(embed_kernel, orders, slots), in_specs=[...  2.82 us
    ppermute x3, starting transfers between devices, per_device(): lax.ppermute(cotangent, 'col', [(c, c ^ r) for c in range(cols)])  1.93 us
    ppermute x2, starting transfers between devices, per_device(): lax.ppermute(away, 'col', [(c, c ^ bit) for c in range(cols)]).astype(F32)  1.62 us
    unnamed x10, local copies, waits for them, and re-layouts  1.6 us
  transfers between devices with their start and end apart: 7, of which 4 were waited for; matrix products, arithmetic and copies ran while one was open for 5% of the time, Pallas kernels for 8%

profile of v5, /device:TPU:0, one launch (start us, length us, event | category | flops | bytes accessed | tf_op | source)
XLA Modules:
  0.0 51.0 jit_solution(10439526226528273190)
XLA Ops:
  0.7 3.2 %pool_bags.1 = bf16[8,192,128]{2,1,0:T(8,128)(2,1)} custom-call(s32[1]{0:T(128)} %bitcast.place_ref, bf16[16,12,4,1024]{3,2,1,0:T(4,128)(2,1)} %bitcast.17, s32[16,1024]{1,0:T(8,128)} %lengths_hbm.1), custom_call_target="tpu_custom_call" | custom-call | tf_op jit(solution)/shard_map/pool_bags/pallas_call | solution.py:100
  3.9 9.4 %all-to-all-start = ((bf16[8,192,128]{2,1,0:T(8,128)(2,1)}), bf16[8,192,128]{2,1,0:T(8,128)(2,1)S(1)}, u32[]{:S(2)}, u32[]{:S(2)}) async-start(bf16[8,192,128]{2,1,0:T(8,128)(2,1)} %pool_bags.1), calls=%async_computation | async-start | bytes 786432 | tf_op jit(solution)/shard_map/all_to_all | solution.py:54
  13.3 0.1 copy.23.refs_0_
  13.4 0.1 collective-permute-start
  13.4 1.6 %collective-permute-start.1 = (bf16[64,32]{1,0:T(8,128)(2,1)S(1)}, bf16[64,32]{1,0:T(8,128)(2,1)S(1)}, u32[]{:S(2)}, u32[]{:S(2)}) collective-permute-start(bf16[64,32]{1,0:T(8,128)(2,1)S(1)} %copy.23.refs_0_), channel_id=1, source_target_pairs={{0,2},{1,3},{2,0},{3,1},{4,6},{5,7},{6,4},{7,5},{8,10},{9,11},{10,... | collective-permute-start | bytes 12296 | tf_op jit(solution)/shard_map/ppermute | solution.py:502
  15.0 0.3 collective-permute-start.2
  15.3 0.4 reshape.35
  15.7 0.3 copy.18
  16.1 0.0 copy-start.1
  16.1 0.0 copy-start
  16.1 0.2 fusion
  16.3 0.5 copy-done.1
  16.7 0.1 copy.22.slot_ref
  16.8 0.2 copy-done
  17.0 0.2 reshape.32.second_ref
  17.2 0.0 collective-permute-done.refs_1_
  17.2 0.0 collective-permute-done.1.refs_2_
  17.2 0.9 %collective-permute-done.2.refs_3_ = bf16[64,32]{1,0:T(8,128)(2,1)S(1)} collective-permute-done((bf16[64,32]{1,0:T(8,128)(2,1)S(1)}, bf16[64,32]{1,0:T(8,128)(2,1)S(1)}, u32[]{:S(2)}, u32[]{:S(2)}) %collective-permute-start.2) | collective-permute-done | bytes 4128 | tf_op jit(solution)/shard_map/ppermute | solution.py:502
  18.2 2.9 %all-to-all-done.received_ref = bf16[8,192,128]{2,1,0:T(8,128)(2,1)S(1)} async-done(((bf16[8,192,128]{2,1,0:T(8,128)(2,1)}), bf16[8,192,128]{2,1,0:T(8,128)(2,1)S(1)}, u32[]{:S(2)}, u32[]{:S(2)}) %all-to-all-start) | async-done | bytes 393248 | tf_op jit(solution)/shard_map/all_to_all | solution.py:54
  21.1 5.2 %forward_part.1 = (bf16[800,128]{1,0:T(8,128)(2,1)S(1)}, bf16[800,128]{1,0:T(8,128)(2,1)S(1)}, bf16[64,1536]{1,0:T(8,128)(2,1)S(1)}, bf16[32,1536]{1,0:T(8,128)(...) custom-call(s32[1]{0:T(128)} %bitcast.place_ref, ...), custom_call_target="tpu_custom_call" | custom-call | flops 1610612736 | bytes 786432 | tf_op jit(solution)/shard_map/forward_part/pallas_call | solution.py:300
  26.3 0.1 collective-permute-start.3
  26.4 0.3 copy.24
  26.7 1.3 %second_part.1.second_ref = f32[64,1536]{1,0:T(8,128)S(1)} custom-call(bf16[2048,32]{1,0:T(8,128)(2,1)S(1)} %bitcast.12, bf16[32,128]{1,0:T(8,128)(2,1)S(1)} %get-tuple-element.21.upper_ref, bf16[32,1536]{1,0:T(8,128)(2,1)S(1)} %get-tuple-element.22.hidden_ref), custom_call_target="tpu_custom_call" | custom-call | flops 6291456 | bytes 786432 | tf_op jit(solution)/shard_map/second_part/pallas_call | solution.py:350
  28.1 1.6 %collective-permute-start.4 = (bf16[400,128]{1,0:T(8,128)(2,1)S(1)}, bf16[400,128]{1,0:T(8,128)(2,1)S(1)}, u32[]{:S(2)}, u32[]{:S(2)}) collective-permute-start(bf16[400,128]{1,0:T(8,128)(2,1)S(1)} %slice.45), channel_id=1, source_target_pairs={{0,2},{1,3},{2,0},{3,1},{4,6},{5,7},{6,4},{7,5},{8,10},{9,11},{10,... | collective-permute-start | bytes 307208 | tf_op jit(solution)/shard_map/ppermute | solution.py:525
  29.7 2.8 %embed_part.1 = bf16[8,192,128]{2,1,0:T(8,128)(2,1)S(1)} custom-call(s32[1]{0:T(128)} %bitcast.place_ref, s32[1,64]{1,0:T(1,128)S(1)} %bitcast.16, bf16[2048,64]{1,0:T(8,128)(2,1)S(1)} %bitcast.14, bf16[64,1536]{1,0:T(8,128)(2,1)S(1)} %get-tuple-element.19.embed_ref, bf16[32,1536]{1,0:T(8,128)(2,1)S(1)} %get-tuple-element.20.lower_ref, ...), custom_call_target="tpu_custom_call" | custom-call | flops 40265318400 | bytes 786432 | tf_op jit(solution)/shard_map/embed_part/pallas_call | solution.py:419
  32.5 1.0 %collective-permute-done.4 = bf16[400,128]{1,0:T(8,128)(2,1)S(1)} collective-permute-done((bf16[400,128]{1,0:T(8,128)(2,1)S(1)}, bf16[400,128]{1,0:T(8,128)(2,1)S(1)}, u32[]{:S(2)}, u32[]{:S(2)}) %collective-permute-start.4) | collective-permute-done | bytes 102432 | tf_op jit(solution)/shard_map/ppermute | solution.py:525
  33.5 0.8 %pad_maximum_fusion = bf16[8,240,128]{2,1,0:T(8,128)(2,1)} fusion(bf16[8,48,128]{2,1,0:T(8,128)(2,1)S(1)} %bitcast.18, bf16[8,192,128]{2,1,0:T(8,128)(2,1)S(1)} %embed_part.1), kind=kLoop, calls=%fused_computation.2 | loop fusion | flops 983040 | bytes 983040 | tf_op jit(solution)/shard_map/concatenate | solution.py:534
  34.3 6.5 %all-to-all-start.1 = ((bf16[8,240,128]{2,1,0:T(8,128)(2,1)}), bf16[8,240,128]{2,1,0:T(8,128)(2,1)S(1)}, u32[]{:S(2)}, u32[]{:S(2)}) async-start(bf16[8,240,128]{2,1,0:T(8,128)(2,1)} %pad_maximum_fusion), calls=%async_computation.1 | async-start | bytes 983040 | tf_op jit(solution)/shard_map/all_to_all | solution.py:54
  40.8 0.1 fusion.1
  40.9 0.7 %copy.25 = f32[64,32]{0,1:T(8,128)} copy(f32[64,32]{1,0:T(8,128)S(1)} %pad_maximum_fusion.1) | data formatting | bytes 16384
  41.6 8.5 %all-to-all-done.1.table_ref = bf16[8,240,128]{2,1,0:T(8,128)(2,1)S(1)} async-done(((bf16[8,240,128]{2,1,0:T(8,128)(2,1)}), bf16[8,240,128]{2,1,0:T(8,128)(2,1)S(1)}, u32[]{:S(2)}, u32[]{:S(2)}) %all-to-all-start.1) | async-done | bytes 491552 | tf_op jit(solution)/shard_map/all_to_all | solution.py:54
  50.1 0.9 %owner_part.1 = (bf16[12,16,1024]{2,1,0:T(8,128)(2,1)}, f32[32,128]{1,0:T(8,128)}, f32[32,64]{1,0:T(8,128)}) custom-call(s32[1]{0:T(128)} %bitcast.place_ref, bf16[8,240,128]{2,1,0:T(8,128)(2,1)S(1)} %all-to-all-done.1.table_ref), custom_call_target="tpu_custom_call" | custom-call | tf_op jit(solution)/shard_map/owner_part/pallas_call | solution.py:463
  (10 shorter events, 0.1 us)
Async XLA Ops:
  0.6 12.6 %copy-start.3 = (bf16[64,32]{0,1:T(8,128)(2,1)S(1)}, bf16[64,32]{0,1:T(8,128)(2,1)}, u32[]{:S(2)}) copy-start(bf16[64,32]{0,1:T(8,128)(2,1)} %param.11) | copy-start | bytes 12292
  0.6 14.7 %copy-start.2 = (bf16[32,4096]{1,0:T(8,128)(2,1)S(1)}, bf16[32,4096]{1,0:T(8,128)(2,1)}, u32[]{:S(2)}) copy-start(bf16[32,4096]{1,0:T(8,128)(2,1)} %param.9) | copy-start | bytes 786436
  3.9 17.2 %all-to-all-start = ((bf16[8,192,128]{2,1,0:T(8,128)(2,1)}), bf16[8,192,128]{2,1,0:T(8,128)(2,1)S(1)}, u32[]{:S(2)}, u32[]{:S(2)}) async-start(bf16[8,192,128]{2,1,0:T(8,128)(2,1)} %pool_bags.1), calls=%async_computation | async-start | bytes 786432 | tf_op jit(solution)/shard_map/all_to_all | solution.py:54
  13.4 3.9 %collective-permute-start = (bf16[64,32]{1,0:T(8,128)(2,1)S(1)}, bf16[64,32]{1,0:T(8,128)(2,1)S(1)}, u32[]{:S(2)}, u32[]{:S(2)}) collective-permute-start(bf16[64,32]{1,0:T(8,128)(2,1)S(1)} %copy.23.refs_0_), channel_id=1, source_target_pairs={{0,1},{1,0},{2,3},{3,2},{4,5},{5,4},{6,7},{7,6},{8,9},{9,8},{10,11... | collective-permute-start | bytes 12296 | tf_op jit(solution)/shard_map/ppermute | solution.py:502
  13.4 3.8 %collective-permute-start.1 = (bf16[64,32]{1,0:T(8,128)(2,1)S(1)}, bf16[64,32]{1,0:T(8,128)(2,1)S(1)}, u32[]{:S(2)}, u32[]{:S(2)}) collective-permute-start(bf16[64,32]{1,0:T(8,128)(2,1)S(1)} %copy.23.refs_0_), channel_id=1, source_target_pairs={{0,2},{1,3},{2,0},{3,1},{4,6},{5,7},{6,4},{7,5},{8,10},{9,11},{10,... | collective-permute-start | bytes 12296 | tf_op jit(solution)/shard_map/ppermute | solution.py:502
  15.0 3.2 %collective-permute-start.2 = (bf16[64,32]{1,0:T(8,128)(2,1)S(1)}, bf16[64,32]{1,0:T(8,128)(2,1)S(1)}, u32[]{:S(2)}, u32[]{:S(2)}) collective-permute-start(bf16[64,32]{1,0:T(8,128)(2,1)S(1)} %copy.23.refs_0_), channel_id=1, source_target_pairs={{0,3},{1,2},{2,1},{3,0},{4,7},{5,6},{6,5},{7,4},{8,11},{9,10},{10,... | collective-permute-start | bytes 12296 | tf_op jit(solution)/shard_map/ppermute | solution.py:502
  16.1 0.7 %copy-start.1 = (s32[64]{0:T(128)S(1)}, s32[64]{0:T(128)}, u32[]{:S(2)}) copy-start(s32[64]{0:T(128)} %param.8) | copy-start | bytes 772
  16.1 0.9 %copy-start = (bf16[32,2048]{1,0:T(8,128)(2,1)S(1)}, bf16[32,2048]{1,0:T(8,128)(2,1)}, u32[]{:S(2)}) copy-start(bf16[32,2048]{1,0:T(8,128)(2,1)} %filter_ref.1) | copy-start | bytes 393220
  26.3 1.7 %collective-permute-start.3 = (bf16[800,128]{1,0:T(8,128)(2,1)S(1)}, bf16[800,128]{1,0:T(8,128)(2,1)S(1)}, u32[]{:S(2)}, u32[]{:S(2)}) collective-permute-start(bf16[800,128]{1,0:T(8,128)(2,1)S(1)} %get-tuple-element.18), channel_id=1, source_target_pairs={{0,1},{1,0},{2,3},{3,2},{4,5},{5,4},{6,7},{7,6},{8,9},{9,8},{10,11... | collective-permute-start | bytes 614408 | tf_op jit(solution)/shard_map/ppermute | solution.py:525
  28.1 5.3 %collective-permute-start.4 = (bf16[400,128]{1,0:T(8,128)(2,1)S(1)}, bf16[400,128]{1,0:T(8,128)(2,1)S(1)}, u32[]{:S(2)}, u32[]{:S(2)}) collective-permute-start(bf16[400,128]{1,0:T(8,128)(2,1)S(1)} %slice.45), channel_id=1, source_target_pairs={{0,2},{1,3},{2,0},{3,1},{4,6},{5,7},{6,4},{7,5},{8,10},{9,11},{10,... | collective-permute-start | bytes 307208 | tf_op jit(solution)/shard_map/ppermute | solution.py:525
  34.3 15.8 %all-to-all-start.1 = ((bf16[8,240,128]{2,1,0:T(8,128)(2,1)}), bf16[8,240,128]{2,1,0:T(8,128)(2,1)S(1)}, u32[]{:S(2)}, u32[]{:S(2)}) async-start(bf16[8,240,128]{2,1,0:T(8,128)(2,1)} %pad_maximum_fusion), calls=%async_computation.1 | async-start | bytes 983040 | tf_op jit(solution)/shard_map/all_to_all | solution.py:54

commit v6 on v5

--- a/solution.py
+++ b/solution.py
@@ -146,11 +146,14 @@
         lax.broadcasted_iota(jnp.int32, (fields, tabs * slots), 1) == slot_ref[...]
     ).astype(BF16)
     order = [position(orders, place_ref, t) if tabs > 1 else 0 for t in range(tabs)]
-    for d in range(width):
-        parts = [received_ref[order[t], d * slots : (d + 1) * slots, :] for t in range(tabs)]
-        x = dot(onehot, parts[0] if len(parts) == 1 else jnp.concatenate(parts, axis=0))
-        x_ref[:, d * lanes : (d + 1) * lanes] = x
-        embed_ref[:, d * lanes : (d + 1) * lanes] = x.astype(BF16)
+    for p in range(width // 2):
+        columns = []
+        for d in (2 * p, 2 * p + 1):
+            parts = [received_ref[order[t], d * slots : (d + 1) * slots, :] for t in range(tabs)]
+            columns.append(parts[0] if tabs == 1 else jnp.concatenate(parts, axis=0))
+        x = dot(onehot, jnp.concatenate(columns, axis=1))
+        x_ref[:, p * pair : (p + 1) * pair] = x
+        embed_ref[:, p * pair : (p + 1) * pair] = x.astype(BF16)
     sum_ref[...] = jnp.zeros_like(sum_ref)
     rows = MATMUL_ROWS
     jobs = []
@@ -399,11 +402,13 @@
         if start + rows < maps * fields:
             return
         gradient = gradient.astype(BF16)
+        table = dot(spread, gradient).astype(BF16)
         for k in range(2):
-            table = dot(spread, gradient[:, k * lanes : (k + 1) * lanes]).astype(BF16)
             at = (2 * p + k) * slots
             for t in range(tabs):
-                table_ref[order[t], at : at + slots, :] = table[t * slots : (t + 1) * slots, :]
+                table_ref[order[t], at : at + slots, :] = table[
+                    t * slots : (t + 1) * slots, k * lanes : (k + 1) * lanes
+                ]
 
     issue(0)
     for number in range(len(jobs)):

time: 51.3 us -> 51.3 us (level)
  no operation moved by 1% of the time
where the time goes in v6:
time: 51.3 us; the launch traced here: 51 us
  starting transfers between devices  19.4 us (38%)
  Pallas kernels  13.5 us (26%)
  waiting for transfers between devices  13.3 us (26%)
  local copies, waits for them, and re-layouts  2.86 us (6%)
  other arithmetic  1.06 us (2%)
  between operations  0.81 us (2%)
    all_to_all x2, starting transfers between devices, exchange(): lax.all_to_all(value, ('tab', 'col'), split_axis=0, concat_axis=0, tiled=...  15.9 us
    all_to_all x2, waiting for transfers between devices, exchange(): lax.all_to_all(value, ('tab', 'col'), split_axis=0, concat_axis=0, tiled=...  11.4 us
    pallas_call x1, Pallas kernels, forward_part(): pl.pallas_call(functools.partial(forward_kernel, packed, orders, scales,...  5.25 us
    pallas_call x1, Pallas kernels, pool(): pl.pallas_call(functools.partial(pool_kernel, steps, orders), in_specs=[p...  3.22 us
    pallas_call x1, Pallas kernels, embed_part(): pl.pallas_call(functools.partial(embed_kernel, orders, slots), in_specs=[...  2.83 us
    ppermute x3, starting transfers between devices, per_device(): lax.ppermute(cotangent, 'col', [(c, c ^ r) for c in range(cols)])  1.93 us
    ppermute x2, starting transfers between devices, per_device(): lax.ppermute(away, 'col', [(c, c ^ bit) for c in range(cols)]).astype(F32)  1.63 us
    unnamed x10, local copies, waits for them, and re-layouts  1.6 us
  transfers between devices with their start and end apart: 7, of which 4 were waited for; matrix products, arithmetic and copies ran while one was open for 5% of the time, Pallas kernels for 8%

profile of v6, /device:TPU:0, one launch (start us, length us, event | category | flops | bytes accessed | tf_op | source)
XLA Modules:
  0.0 51.0 jit_solution(497242809325438828)
XLA Ops:
  0.7 3.2 %pool_bags.1 = bf16[8,192,128]{2,1,0:T(8,128)(2,1)} custom-call(s32[1]{0:T(128)} %bitcast.place_ref, bf16[16,12,4,1024]{3,2,1,0:T(4,128)(2,1)} %bitcast.17, s32[16,1024]{1,0:T(8,128)} %lengths_hbm.1), custom_call_target="tpu_custom_call" | custom-call | tf_op jit(solution)/shard_map/pool_bags/pallas_call | solution.py:100
  3.9 9.4 %all-to-all-start = ((bf16[8,192,128]{2,1,0:T(8,128)(2,1)}), bf16[8,192,128]{2,1,0:T(8,128)(2,1)S(1)}, u32[]{:S(2)}, u32[]{:S(2)}) async-start(bf16[8,192,128]{2,1,0:T(8,128)(2,1)} %pool_bags.1), calls=%async_computation | async-start | bytes 786432 | tf_op jit(solution)/shard_map/all_to_all | solution.py:54
  13.3 0.1 copy.23.refs_0_
  13.4 0.1 collective-permute-start
  13.4 1.6 %collective-permute-start.1 = (bf16[64,32]{1,0:T(8,128)(2,1)S(1)}, bf16[64,32]{1,0:T(8,128)(2,1)S(1)}, u32[]{:S(2)}, u32[]{:S(2)}) collective-permute-start(bf16[64,32]{1,0:T(8,128)(2,1)S(1)} %copy.23.refs_0_), channel_id=1, source_target_pairs={{0,2},{1,3},{2,0},{3,1},{4,6},{5,7},{6,4},{7,5},{8,10},{9,11},{10,... | collective-permute-start | bytes 12296 | tf_op jit(solution)/shard_map/ppermute | solution.py:507
  15.0 0.3 collective-permute-start.2
  15.3 0.4 reshape.35
  15.7 0.3 copy.18
  16.1 0.0 copy-start.1
  16.1 0.0 copy-start
  16.1 0.2 fusion
  16.3 0.5 copy-done.1
  16.7 0.1 copy.22.slot_ref
  16.8 0.2 copy-done
  17.0 0.2 reshape.32.second_ref
  17.2 0.0 collective-permute-done.refs_1_
  17.2 0.0 collective-permute-done.1.refs_2_
  17.2 0.9 %collective-permute-done.2.refs_3_ = bf16[64,32]{1,0:T(8,128)(2,1)S(1)} collective-permute-done((bf16[64,32]{1,0:T(8,128)(2,1)S(1)}, bf16[64,32]{1,0:T(8,128)(2,1)S(1)}, u32[]{:S(2)}, u32[]{:S(2)}) %collective-permute-start.2) | collective-permute-done | bytes 4128 | tf_op jit(solution)/shard_map/ppermute | solution.py:507
  18.2 2.9 %all-to-all-done.received_ref = bf16[8,192,128]{2,1,0:T(8,128)(2,1)S(1)} async-done(((bf16[8,192,128]{2,1,0:T(8,128)(2,1)}), bf16[8,192,128]{2,1,0:T(8,128)(2,1)S(1)}, u32[]{:S(2)}, u32[]{:S(2)}) %all-to-all-start) | async-done | bytes 393248 | tf_op jit(solution)/shard_map/all_to_all | solution.py:54
  21.1 5.3 %forward_part.1 = (bf16[800,128]{1,0:T(8,128)(2,1)S(1)}, bf16[800,128]{1,0:T(8,128)(2,1)S(1)}, bf16[64,1536]{1,0:T(8,128)(2,1)S(1)}, bf16[32,1536]{1,0:T(8,128)(...) custom-call(s32[1]{0:T(128)} %bitcast.place_ref, ...), custom_call_target="tpu_custom_call" | custom-call | flops 1610612736 | bytes 786432 | tf_op jit(solution)/shard_map/forward_part/pallas_call | solution.py:303
  26.3 0.1 collective-permute-start.3
  26.4 0.3 copy.24
  26.7 1.3 %second_part.1.second_ref = f32[64,1536]{1,0:T(8,128)S(1)} custom-call(bf16[2048,32]{1,0:T(8,128)(2,1)S(1)} %bitcast.12, bf16[32,128]{1,0:T(8,128)(2,1)S(1)} %get-tuple-element.21.upper_ref, bf16[32,1536]{1,0:T(8,128)(2,1)S(1)} %get-tuple-element.22.hidden_ref), custom_call_target="tpu_custom_call" | custom-call | flops 6291456 | bytes 786432 | tf_op jit(solution)/shard_map/second_part/pallas_call | solution.py:353
  28.1 1.6 %collective-permute-start.4 = (bf16[400,128]{1,0:T(8,128)(2,1)S(1)}, bf16[400,128]{1,0:T(8,128)(2,1)S(1)}, u32[]{:S(2)}, u32[]{:S(2)}) collective-permute-start(bf16[400,128]{1,0:T(8,128)(2,1)S(1)} %slice.45), channel_id=1, source_target_pairs={{0,2},{1,3},{2,0},{3,1},{4,6},{5,7},{6,4},{7,5},{8,10},{9,11},{10,... | collective-permute-start | bytes 307208 | tf_op jit(solution)/shard_map/ppermute | solution.py:530
  29.7 2.8 %embed_part.1 = bf16[8,192,128]{2,1,0:T(8,128)(2,1)S(1)} custom-call(s32[1]{0:T(128)} %bitcast.place_ref, s32[1,64]{1,0:T(1,128)S(1)} %bitcast.16, bf16[2048,64]{1,0:T(8,128)(2,1)S(1)} %bitcast.14, bf16[64,1536]{1,0:T(8,128)(2,1)S(1)} %get-tuple-element.19.embed_ref, bf16[32,1536]{1,0:T(8,128)(2,1)S(1)} %get-tuple-element.20.lower_ref, ...), custom_call_target="tpu_custom_call" | custom-call | flops 40265318400 | bytes 786432 | tf_op jit(solution)/shard_map/embed_part/pallas_call | solution.py:424
  32.5 1.0 %collective-permute-done.4 = bf16[400,128]{1,0:T(8,128)(2,1)S(1)} collective-permute-done((bf16[400,128]{1,0:T(8,128)(2,1)S(1)}, bf16[400,128]{1,0:T(8,128)(2,1)S(1)}, u32[]{:S(2)}, u32[]{:S(2)}) %collective-permute-start.4) | collective-permute-done | bytes 102432 | tf_op jit(solution)/shard_map/ppermute | solution.py:530
  33.5 0.8 %pad_maximum_fusion = bf16[8,240,128]{2,1,0:T(8,128)(2,1)} fusion(bf16[8,48,128]{2,1,0:T(8,128)(2,1)S(1)} %bitcast.18, bf16[8,192,128]{2,1,0:T(8,128)(2,1)S(1)} %embed_part.1), kind=kLoop, calls=%fused_computation.2 | loop fusion | flops 983040 | bytes 983040 | tf_op jit(solution)/shard_map/concatenate | solution.py:539
  34.4 6.5 %all-to-all-start.1 = ((bf16[8,240,128]{2,1,0:T(8,128)(2,1)}), bf16[8,240,128]{2,1,0:T(8,128)(2,1)S(1)}, u32[]{:S(2)}, u32[]{:S(2)}) async-start(bf16[8,240,128]{2,1,0:T(8,128)(2,1)} %pad_maximum_fusion), calls=%async_computation.1 | async-start | bytes 983040 | tf_op jit(solution)/shard_map/all_to_all | solution.py:54
  40.9 0.1 fusion.1
  40.9 0.7 %copy.25 = f32[64,32]{0,1:T(8,128)} copy(f32[64,32]{1,0:T(8,128)S(1)} %pad_maximum_fusion.1) | data formatting | bytes 16384
  41.6 8.5 %all-to-all-done.1.table_ref = bf16[8,240,128]{2,1,0:T(8,128)(2,1)S(1)} async-done(((bf16[8,240,128]{2,1,0:T(8,128)(2,1)}), bf16[8,240,128]{2,1,0:T(8,128)(2,1)S(1)}, u32[]{:S(2)}, u32[]{:S(2)}) %all-to-all-start.1) | async-done | bytes 491552 | tf_op jit(solution)/shard_map/all_to_all | solution.py:54
  50.1 0.9 %owner_part.1 = (bf16[12,16,1024]{2,1,0:T(8,128)(2,1)}, f32[32,128]{1,0:T(8,128)}, f32[32,64]{1,0:T(8,128)}) custom-call(s32[1]{0:T(128)} %bitcast.place_ref, bf16[8,240,128]{2,1,0:T(8,128)(2,1)S(1)} %all-to-all-done.1.table_ref), custom_call_target="tpu_custom_call" | custom-call | tf_op jit(solution)/shard_map/owner_part/pallas_call | solution.py:468
  (10 shorter events, 0.1 us)
Async XLA Ops:
  0.6 12.6 %copy-start.3 = (bf16[64,32]{0,1:T(8,128)(2,1)S(1)}, bf16[64,32]{0,1:T(8,128)(2,1)}, u32[]{:S(2)}) copy-start(bf16[64,32]{0,1:T(8,128)(2,1)} %param.11) | copy-start | bytes 12292
  0.6 14.7 %copy-start.2 = (bf16[32,4096]{1,0:T(8,128)(2,1)S(1)}, bf16[32,4096]{1,0:T(8,128)(2,1)}, u32[]{:S(2)}) copy-start(bf16[32,4096]{1,0:T(8,128)(2,1)} %param.9) | copy-start | bytes 786436
  3.9 17.2 %all-to-all-start = ((bf16[8,192,128]{2,1,0:T(8,128)(2,1)}), bf16[8,192,128]{2,1,0:T(8,128)(2,1)S(1)}, u32[]{:S(2)}, u32[]{:S(2)}) async-start(bf16[8,192,128]{2,1,0:T(8,128)(2,1)} %pool_bags.1), calls=%async_computation | async-start | bytes 786432 | tf_op jit(solution)/shard_map/all_to_all | solution.py:54
  13.4 3.9 %collective-permute-start = (bf16[64,32]{1,0:T(8,128)(2,1)S(1)}, bf16[64,32]{1,0:T(8,128)(2,1)S(1)}, u32[]{:S(2)}, u32[]{:S(2)}) collective-permute-start(bf16[64,32]{1,0:T(8,128)(2,1)S(1)} %copy.23.refs_0_), channel_id=1, source_target_pairs={{0,1},{1,0},{2,3},{3,2},{4,5},{5,4},{6,7},{7,6},{8,9},{9,8},{10,11... | collective-permute-start | bytes 12296 | tf_op jit(solution)/shard_map/ppermute | solution.py:507
  13.4 3.8 %collective-permute-start.1 = (bf16[64,32]{1,0:T(8,128)(2,1)S(1)}, bf16[64,32]{1,0:T(8,128)(2,1)S(1)}, u32[]{:S(2)}, u32[]{:S(2)}) collective-permute-start(bf16[64,32]{1,0:T(8,128)(2,1)S(1)} %copy.23.refs_0_), channel_id=1, source_target_pairs={{0,2},{1,3},{2,0},{3,1},{4,6},{5,7},{6,4},{7,5},{8,10},{9,11},{10,... | collective-permute-start | bytes 12296 | tf_op jit(solution)/shard_map/ppermute | solution.py:507
  15.0 3.2 %collective-permute-start.2 = (bf16[64,32]{1,0:T(8,128)(2,1)S(1)}, bf16[64,32]{1,0:T(8,128)(2,1)S(1)}, u32[]{:S(2)}, u32[]{:S(2)}) collective-permute-start(bf16[64,32]{1,0:T(8,128)(2,1)S(1)} %copy.23.refs_0_), channel_id=1, source_target_pairs={{0,3},{1,2},{2,1},{3,0},{4,7},{5,6},{6,5},{7,4},{8,11},{9,10},{10,... | collective-permute-start | bytes 12296 | tf_op jit(solution)/shard_map/ppermute | solution.py:507
  16.1 0.7 %copy-start.1 = (s32[64]{0:T(128)S(1)}, s32[64]{0:T(128)}, u32[]{:S(2)}) copy-start(s32[64]{0:T(128)} %param.8) | copy-start | bytes 772
  16.1 0.9 %copy-start = (bf16[32,2048]{1,0:T(8,128)(2,1)S(1)}, bf16[32,2048]{1,0:T(8,128)(2,1)}, u32[]{:S(2)}) copy-start(bf16[32,2048]{1,0:T(8,128)(2,1)} %filter_ref.1) | copy-start | bytes 393220
  26.3 1.7 %collective-permute-start.3 = (bf16[800,128]{1,0:T(8,128)(2,1)S(1)}, bf16[800,128]{1,0:T(8,128)(2,1)S(1)}, u32[]{:S(2)}, u32[]{:S(2)}) collective-permute-start(bf16[800,128]{1,0:T(8,128)(2,1)S(1)} %get-tuple-element.18), channel_id=1, source_target_pairs={{0,1},{1,0},{2,3},{3,2},{4,5},{5,4},{6,7},{7,6},{8,9},{9,8},{10,11... | collective-permute-start | bytes 614408 | tf_op jit(solution)/shard_map/ppermute | solution.py:530
  28.1 5.4 %collective-permute-start.4 = (bf16[400,128]{1,0:T(8,128)(2,1)S(1)}, bf16[400,128]{1,0:T(8,128)(2,1)S(1)}, u32[]{:S(2)}, u32[]{:S(2)}) collective-permute-start(bf16[400,128]{1,0:T(8,128)(2,1)S(1)} %slice.45), channel_id=1, source_target_pairs={{0,2},{1,3},{2,0},{3,1},{4,6},{5,7},{6,4},{7,5},{8,10},{9,11},{10,... | collective-permute-start | bytes 307208 | tf_op jit(solution)/shard_map/ppermute | solution.py:530
  34.4 15.8 %all-to-all-start.1 = ((bf16[8,240,128]{2,1,0:T(8,128)(2,1)}), bf16[8,240,128]{2,1,0:T(8,128)(2,1)S(1)}, u32[]{:S(2)}, u32[]{:S(2)}) async-start(bf16[8,240,128]{2,1,0:T(8,128)(2,1)} %pad_maximum_fusion), calls=%async_computation.1 | async-start | bytes 983040 | tf_op jit(solution)/shard_map/all_to_all | solution.py:54
